TPU v7x, 256 devices: a whole 4x4x8 slice. The times are simulated.
256 devices in a mesh: depth: 32 (over y, z), dp: 8 (over x, core).
Axes of the slice: x: 4, y: 4, z: 8, core: 2. Of those that a mesh axis runs over, the one named last changes fastest.
Arguments:
- checkpoints: bfloat16 [32, 8, 8, 32, 128], P('depth', 'dp'), may hold values from -6 to 6
- conv_weight: bfloat16 [3, 3, 128, 128], replicated, may hold values from -0.1875 to 0.1875
- conv_bias: float32 [128], replicated, may hold values from -3 to 3
- point_guess: float32 [32, 8, 8, 32, 128], P('depth', 'dp'), may hold values from -6 to 6
- terminal: float32 [8, 8, 32, 128], P('dp'), may hold values from -6 to 6
Outputs:
- points: float32 [32, 8, 8, 32, 128], P('depth', 'dp')
- grad_w: float32 [3, 3, 128, 128], replicated
All inputs are finite; a program needn't handle non-finite values.
Results may differ from a plain program's by a relative error of at most 0.0022.
Values sent between devices are 32-bit elements; how exact they have to be, the bound alone decides.
No kernel may reach another device: no remote copies, remote signals or barrier semaphores. Data moves between devices by JAX's collectives and lax.ppermute only.
A program may use at most 64 MiB of HBM per device.

v0:
```python
import jax
import jax.numpy as jnp
from jax import lax
from jax.sharding import PartitionSpec as P

STEPS_DEV = 4


def passed_along(block, axis, distance):
    devices = range(lax.axis_size(axis))
    route = [(i - distance, i) for i in devices if i - distance in devices]
    return lax.ppermute(block, axis, route)


def carried_in(value, axis, join, neutral):
    count, mine = (lax.axis_size(axis), lax.axis_index(axis))
    pieces = jax.tree.map(lambda part: lax.all_gather(part, axis), value)
    pieces = jax.tree.map(lambda part: part[::-1], pieces)
    mine = count - 1 - mine
    total = jax.tree.map(
        lambda part, zero: jnp.full_like(part, 0) + jnp.asarray(zero, part.dtype), value, neutral
    )

    def turn(position, total):
        longer = join(total, jax.tree.map(lambda part: part[position], pieces))
        return jax.tree.map(lambda new, old: jnp.where(position < mine, new, old), longer, total)

    return lax.fori_loop(0, count - 1, turn, total)


def conv_apply(field, kernel):
    return lax.conv_general_dilated(
        field,
        kernel,
        (1, 1),
        "SAME",
        dimension_numbers=("NHWC", "HWIO", "NHWC"),
        preferred_element_type=jnp.float32,
    )


def forward_states(start, kernel, conv_bias, step_size, steps_here):
    current = start
    lowered = []
    slopes = []
    for section in range(steps_here):
        low_state = current.astype(jnp.bfloat16)
        tanh_out = jnp.tanh(conv_apply(low_state, kernel) + conv_bias)
        lowered.append(low_state)
        slopes.append(1.0 - tanh_out * tanh_out)
        current = current + step_size * tanh_out
    return (lowered, slopes)


def correlate(low_state, low_grad):
    rows_map = low_state.shape[1]
    cols_map = low_state.shape[2]
    channels = low_state.shape[3]
    padded = jnp.pad(low_state, ((0, 0), (1, 1), (1, 1), (0, 0)))
    flat_grad = low_grad.reshape(-1, channels)
    taps = []
    for row_tap in range(3):
        for col_tap in range(3):
            patch = padded[
                :, row_tap : row_tap + rows_map, col_tap : col_tap + cols_map, :
            ].reshape(-1, channels)
            taps.append(
                lax.dot_general(
                    patch, flat_grad, (((0,), (0,)), ((), ())), preferred_element_type=jnp.float32
                )
            )
    return jnp.stack(taps).reshape(3, 3, channels, channels)


def coarse_operator(first_slope, center, coarse_step):
    channels = center.shape[0]
    slope_mean = jnp.mean(first_slope, axis=(1, 2))
    identity = jnp.eye(channels, dtype=jnp.float32)
    return identity[None] + coarse_step * slope_mean[:, :, None] * center.T[None]


def apply_map(field, coarse_map):
    return jnp.einsum("bhwc,bcd->bhwd", field, coarse_map, precision=lax.Precision.HIGHEST)


def compose(earlier, later_map):
    first_mat, first_res = earlier
    second_mat, second_res = later_map
    joined = jnp.einsum("bcd,bde->bce", first_mat, second_mat, precision=lax.Precision.HIGHEST)
    return (joined, second_res + apply_map(first_res, second_mat))


def local(checkpoints, conv_weight, conv_bias, point_guess, terminal):
    slices = lax.axis_size("depth")
    position = lax.axis_index("depth")
    step_size = 2.0 / (STEPS_DEV * slices)
    coarse_step = STEPS_DEV * step_size
    flipped = conv_weight[::-1, ::-1].transpose(0, 1, 3, 2)
    center = conv_weight[1, 1].astype(jnp.float32)
    own_guess = point_guess[0]
    upper_guess = passed_along(point_guess, "depth", -1)[0]
    is_final = position == slices - 1
    start_up = jnp.where(is_final, terminal, upper_guess)
    start_state = checkpoints[0].astype(jnp.float32)
    lowered, slopes = forward_states(start_state, conv_weight, conv_bias, step_size, STEPS_DEV)
    adjoint = start_up
    for section in range(STEPS_DEV - 1, -1, -1):
        low_grad = (slopes[section] * adjoint).astype(jnp.bfloat16)
        adjoint = adjoint + step_size * conv_apply(low_grad, flipped)
    residue = adjoint - own_guess
    coarse_map = coarse_operator(slopes[0], center, coarse_step)
    identity = (
        jnp.broadcast_to(jnp.eye(coarse_map.shape[1], dtype=jnp.float32), coarse_map.shape),
        jnp.zeros_like(residue),
    )
    unused, upper_error = carried_in((coarse_map, residue), "depth", compose, identity)
    points = own_guess + (residue + apply_map(upper_error, coarse_map))
    start_new = jnp.where(is_final, terminal, upper_guess + upper_error)
    channels = conv_weight.shape[3]
    grad_local = jnp.zeros((3, 3, channels, channels), jnp.float32)
    adjoint = start_new
    for section in range(STEPS_DEV - 1, -1, -1):
        low_grad = (slopes[section] * adjoint).astype(jnp.bfloat16)
        grad_local = grad_local + step_size * correlate(lowered[section], low_grad)
        if section > 0:
            adjoint = adjoint + step_size * conv_apply(low_grad, flipped)
    grad_w = lax.psum(grad_local, ("depth", "dp"))
    return (points[None], grad_w)


def solution(mesh):
    placed = (
        P("depth", "dp", None, None, None),
        P(),
        P(),
        P("depth", "dp", None, None, None),
        P("dp", None, None, None),
    )
    return jax.shard_map(
        local,
        mesh=mesh,
        in_specs=placed,
        out_specs=(P("depth", "dp", None, None, None), P()),
        check_vma=False,
    )
```

profile of v0, /device:TPU:1, one launch (start us, length us, event | category | flops | bytes accessed | tf_op | source)
XLA Modules:
  0.0 483.8 jit_solution(13620022782011898540)
XLA Ops:
  8.2 1.4 select_reduce_fusion
  9.6 1.4 fusion.230
  11.1 1.3 collective-permute-start
  13.5 1.4 broadcast_multiply_fusion.1
  16.4 1.7 collective-permute-done
  21.3 65.5 %all-gather.7.cloned.1.call-done = f32[4096,128]{0,1:T(8,128)} async-done(((f32[128,128]{0,1:T(8,128)}), f32[4096,128]{0,1:T(8,128)}) %all-gather.7.cloned.1.call-update) | async-done | bytes 2097168 | tf_op jit(solution)/shard_map/all_gather | solution.py:17
  86.7 1.9 copy.128
  88.7 1.5 rev.8
  90.2 81.3 %all-gather.5.cloned.1.call-done = f32[32,8,32,128]{3,2,1,0:T(8,128)} async-done(((f32[1,8,32,128]{3,2,1,0:T(8,128)}), f32[32,8,32,128]{3,2,1,0:T(8,128)}) %all-gather.5.cloned.1.call-update) | async-done | bytes 4194320 | tf_op jit(solution)/shard_map/all_gather | solution.py:17
  171.4 4.9 %reverse_bitcast_fusion = f32[32,1,8,32,128]{4,3,2,1,0:T(8,128)} fusion(f32[32,8,32,128]{3,2,1,0:T(8,128)} %all-gather.5.cloned.1.call-done), kind=kLoop, calls=%fused_computation.12 | loop fusion | bytes 8388608
  176.3 39.2 %while.14 = (s32[]{:T(128)}, f32[1,8,32,128]{3,2,1,0:T(8,128)S(1)}, s32[]{:T(128)}, f32[32,1,8,32,128]{4,3,2,1,0:T(8,128)}, f32[32,1,128,128]{3,2,1,0:T(8,128)}, /*index=5*/s32[]{:T(128)}, s32[]{:T(128)}) while((s32[]{:T(128)}, f32[1,8,32,128]{3,2,1,0:T(8,128)S(1)}, s32[]{:T(128)}, f32[32,1,8,32,128]{4,3,2,1,0:T(8,128)}, ...), condition=%wide.region_2.3_spmd.clone, body=%wide.region_1.2_spmd.clone.sunk | while | flops 50462724 | bytes 854623 | solution.py:28
  176.3 1.2 fusion.368
  177.6 1.2 fusion.368
  178.9 1.2 fusion.368
  180.1 1.2 fusion.368
  181.4 1.2 fusion.368
  183.9 1.2 fusion.368
  185.2 1.2 fusion.368
  186.5 1.2 fusion.368
  187.7 1.2 fusion.368
  189.0 1.2 fusion.368
  190.2 1.2 fusion.368
  191.5 1.2 fusion.368
  192.8 1.2 fusion.368
  194.0 1.2 fusion.368
  195.3 1.2 fusion.368
  196.6 1.2 fusion.368
  201.6 1.2 fusion.368
  206.7 1.2 fusion.368
  211.7 1.2 fusion.368
  226.6 248.8 %all-reduce.6.cloned.1.call-done = f32[3,3,128,128]{3,2,1,0:T(8,128)} async-done(((f32[3,3,128,128]{3,2,1,0:T(8,128)}), f32[3,3,128,128]{3,2,1,0:T(8,128)}) %all-reduce.6.cloned.1.call-update) | async-done | bytes 589840 | tf_op jit(solution)/shard_map/psum | solution.py:127
  475.4 1.9 copy.320
  (198 shorter events, 32.0 us)
Async XLA Ops:
  7.2 7.9 %copy-start.7 = (pred[8,5]{0,1:T(8,128)(4,1)S(1)}, pred[8,5]{0,1:T(8,128)(4,1)}, u32[]{:S(2)}) copy-start(pred[8,5]{0,1:T(8,128)(4,1)} %constant.103) | copy-start | bytes 124
  7.2 7.8 %copy-start = (bf16[1,1,8,32,128]{4,3,2,1,0:T(8,128)(2,1)S(1)}, bf16[1,1,8,32,128]{4,3,2,1,0:T(8,128)(2,1)}, u32[]{:S(2)}) copy-start(bf16[1,1,8,32,128]{4,3,2,1,0:T(8,128)(2,1)} %param.7) | copy-start | bytes 196612
  7.2 7.9 %copy-start.4 = (bf16[3,3,128,128]{3,2,1,0:T(8,128)(2,1)S(1)}, bf16[3,3,128,128]{3,2,1,0:T(8,128)(2,1)}, u32[]{:S(2)}) copy-start(bf16[3,3,128,128]{3,2,1,0:T(8,128)(2,1)} %param.8) | copy-start | bytes 884740
  7.2 7.9 %copy-start.6 = (f32[128]{0:T(128)S(1)}, f32[128]{0:T(128)}, u32[]{:S(2)}) copy-start(f32[128]{0:T(128)} %param.9) | copy-start | bytes 1540
  7.2 79.5 %all-gather.7.cloned.1.call-start = ((), (), s32[]{:S(2)}) async-start(), calls=%async_computation.2 | async-start | bytes 2162688 | tf_op jit(solution)/shard_map/all_gather | solution.py:17
  11.1 160.4 %all-gather.5.cloned.1.call-start = ((), (), s32[]{:S(2)}) async-start(), calls=%async_computation.1 | async-start | bytes 4325376 | tf_op jit(solution)/shard_map/all_gather | solution.py:17
  11.1 6.9 %collective-permute-start = (f32[1,1,8,32,128]{4,3,2,1,0:T(8,128)}, f32[1,1,8,32,128]{4,3,2,1,0:T(8,128)S(1)}, u32[]{:S(2)}, u32[]{:S(2)}) collective-permute-start(f32[1,1,8,32,128]{4,3,2,1,0:T(8,128)} %param.10), channel_id=1, source_target_pairs={{8,0},{16,8},{24,16},{32,24},{40,32},{48,40},{56,48},{64,56},{72,6... | collective-permute-start | bytes 393224 | tf_op jit(solution)/shard_map/ppermute | solution.py:12
  13.5 4.6 copy-start.1
  18.6 1.9 copy-start.3
  21.2 454.2 %all-reduce.6.cloned.1.call-start = ((), (), s32[]{:S(2)}) async-start(), calls=%async_computation | async-start | bytes 1179648 | tf_op jit(solution)/shard_map/psum | solution.py:127
  176.3 39.5 %copy-start.5 = (bf16[3,3,128,128]{3,2,1,0:T(8,128)(2,1)S(1)}, bf16[3,3,128,128]{3,2,1,0:T(8,128)(2,1)}, u32[]{:S(2)}) copy-start(bf16[3,3,128,128]{3,2,1,0:T(8,128)(2,1)} %param.8) | copy-start | bytes 884740
  222.2 3.5 copy-start.2
Sparse Core Ops, SparseCore 0:
  11.2 75.4 all-gather.6
  89.9 81.4 all-gather.4
  225.8 249.5 all-reduce.5
where the time goes:
time: 485 us; the launch traced here: 484 us
  waiting for transfers between devices  397 us (82%)
  matrix products  51.9 us (11%)
  between operations  14.7 us (3%)
  local copies, waits for them, and re-layouts  12.8 us (3%)
    psum x1, waiting for transfers between devices, local(): grad_w = lax.psum(grad_local, ('depth', 'dp'))  249 us
    all_gather x2, waiting for transfers between devices, carried_in(): pieces = jax.tree.map(lambda part: lax.all_gather(part, axis), value)  147 us
    dot_general x32, matrix products, apply_map(): jnp.einsum('bhwc,bcd->bhwd', field, coarse_map, precision=lax.Precision.H...  38.6 us
  transfers between devices with their start and end apart: 4, of which 4 were waited for; matrix products, arithmetic and copies ran while one was open for 2% of the time, Pallas kernels for 0%

commit v1 on v0

v1 whole, which is shorter than its diff:
```python
import jax
import jax.numpy as jnp
from jax import lax
from jax.experimental import pallas as pl
from jax.experimental.pallas import tpu as pltpu
from jax.sharding import Mesh, PartitionSpec as P

STEPS_DEV = 4
ROWS = 8
COLS = 32
CH = 128
PIX = ROWS * COLS
PADDED = PIX + 2 * COLS
WIDE = 3 * CH
TAPS = 9 * CH
SIZE_Y = 4
SIZE_Z = 8
SIZE_X = 4
CHUNK = 40
HALF = SIZE_X * SIZE_Y * CHUNK
SLOT = COLS + 8


def call(kernel, outs, scratch=()):
    return pl.pallas_call(
        kernel,
        out_shape=outs,
        scratch_shapes=scratch,
        compiler_params=pltpu.CompilerParams(vmem_limit_bytes=40 << 20),
    )


def f32(*shape):
    return jax.ShapeDtypeStruct(shape, jnp.float32)


def bf16(*shape):
    return jax.ShapeDtypeStruct(shape, jnp.bfloat16)


def columns():
    return lax.broadcasted_iota(jnp.int32, (PIX, CH), 0) % COLS


def clear_edges(buffer):
    zeros = jnp.zeros((COLS, WIDE), jnp.bfloat16)
    buffer[0:COLS, :] = zeros
    buffer[COLS + PIX : PADDED, :] = zeros


def spread(buffer, low, col):
    wide = low.astype(jnp.float32)
    before = jnp.where(col > 0, pltpu.roll(wide, 1, 0), 0.0)
    after = jnp.where(col < COLS - 1, pltpu.roll(wide, PIX - 1, 0), 0.0)
    buffer[COLS : COLS + PIX, 0:CH] = before.astype(jnp.bfloat16)
    buffer[COLS : COLS + PIX, CH : 2 * CH] = low
    buffer[COLS : COLS + PIX, 2 * CH : WIDE] = after.astype(jnp.bfloat16)


def convolve(buffer, kernel):
    total = None
    for row in range(3):
        part = jnp.dot(
            buffer[row * COLS : row * COLS + PIX, :],
            kernel[row * WIDE : (row + 1) * WIDE, :],
            preferred_element_type=jnp.float32,
        )
        total = part if total is None else total + part
    return total


def split(value):
    high = value.astype(jnp.bfloat16)
    return high, (value - high.astype(jnp.float32)).astype(jnp.bfloat16)


def exact_left(value, weight_twice):
    return jnp.dot(
        jnp.concatenate(split(value), axis=1), weight_twice, preferred_element_type=jnp.float32
    )


def full_dot(left, right):
    return jnp.dot(
        left, right, preferred_element_type=jnp.float32, precision=lax.Precision.HIGHEST
    )


def forward_kernel(step, start_ref, kernel_ref, bias_ref, slope_ref, lowered_ref, flipped_ref, center_ref, mean_ref):
    col = columns()
    bias = bias_ref[...]
    current = start_ref[...].astype(jnp.float32)
    for section in range(STEPS_DEV):
        buffer = lowered_ref.at[section]
        clear_edges(buffer)
        spread(buffer, current.astype(jnp.bfloat16), col)
        tanh_out = jnp.tanh(convolve(buffer, kernel_ref) + bias)
        slope = 1.0 - tanh_out * tanh_out
        slope_ref[section] = slope
        if section == 0:
            mean = jnp.sum(slope, axis=0, keepdims=True) * (STEPS_DEV * step / PIX)
            mean_ref[...] = jnp.broadcast_to(mean, (8, CH))
        current = current + step * tanh_out
    for tap in range(9):
        block = kernel_ref[(8 - tap) * CH : (9 - tap) * CH, :].astype(jnp.float32)
        turned = block.T.astype(jnp.bfloat16)
        flipped_ref[tap * CH : (tap + 1) * CH, :] = turned
        if tap == 4:
            center_ref[0:CH, :] = turned
            center_ref[CH : 2 * CH, :] = turned


def adjoint_step(buffer, flipped, slope, value, step, col):
    low = (slope * value).astype(jnp.bfloat16)
    spread(buffer, low, col)
    return low, value + step * convolve(buffer, flipped)


def relax_kernel(step, final_ref, upper_ref, terminal_ref, own_ref, slope_ref, flipped_ref, mean_ref, packed_ref, buffer):
    col = columns()
    clear_edges(buffer)
    value = jnp.where(final_ref[0] == 1, terminal_ref[...], upper_ref[...])
    for section in range(STEPS_DEV - 1, -1, -1):
        low, value = adjoint_step(buffer, flipped_ref, slope_ref[section], value, step, col)
    residue = value - own_ref[...]
    for part in range(ROWS):
        packed_ref[part, 0:COLS, :] = residue[part * COLS : (part + 1) * COLS]
        packed_ref[part, COLS:SLOT, :] = mean_ref[...]


def group_kernel(packed_ref, center_ref, local_ref, maps_ref, total_ref):
    center = center_ref[...]
    row = lax.broadcasted_iota(jnp.int32, (CH, CH), 0)
    lane = lax.broadcasted_iota(jnp.int32, (CH, CH), 1)
    identity = jnp.where(row == lane, 1.0, 0.0)
    error = jnp.zeros((COLS, CH), jnp.float32)
    change = jnp.zeros((CH, CH), jnp.float32)
    for place in range(SIZE_Z - 1, -1, -1):
        local_ref[place] = error
        maps_ref[place] = change
        mean = packed_ref[place, COLS : COLS + 1, :]
        both = jnp.concatenate([error, change + identity], axis=0) * mean
        moved = exact_left(both, center)
        error = packed_ref[place, 0:COLS, :] + error + moved[0:COLS]
        change = change + moved[COLS:]
    total_ref[0:COLS, :] = error
    total_ref[COLS:, :] = change


def carry_kernel(first_ref, second_ref, third_ref, local_ref, maps_ref, upper_ref):
    third = third_ref[...]
    carry = second_ref[0:COLS, :] + third + full_dot(third, second_ref[COLS:, :])
    carry = first_ref[0:COLS, :] + carry + full_dot(carry, first_ref[COLS:, :])
    for place in range(SIZE_Z):
        upper_ref[place] = local_ref[place] + carry + full_dot(carry, maps_ref[place])


def second_kernel(
    step, final_ref, core_ref, upper_ref, terminal_ref, own_ref, packed_ref, error_ref, slope_ref, lowered_ref,
    flipped_ref, center_ref, mean_ref, points_ref, kept_ref, sent_ref, buffer, total,
):
    col = columns()
    clear_edges(buffer)
    error = error_ref[...]
    moved = exact_left(error * mean_ref[0:1, :], center_ref[...])
    for part in range(ROWS):
        span = slice(part * COLS, (part + 1) * COLS)
        points_ref[span, :] = own_ref[span, :] + (packed_ref[part, 0:COLS, :] + error[span] + moved[span])
    value = jnp.where(final_ref[0] == 1, terminal_ref[...], upper_ref[...] + error)
    for section in range(STEPS_DEV - 1, -1, -1):
        if section > 0:
            low, value = adjoint_step(buffer, flipped_ref, slope_ref[section], value, step, col)
        else:
            low = (slope_ref[section] * value).astype(jnp.bfloat16)
        for row in range(3):
            term = lax.dot_general(
                lowered_ref[section, row * COLS : row * COLS + PIX, :],
                low,
                (((0,), (0,)), ((), ())),
                preferred_element_type=jnp.float32,
            )
            span = slice(row * WIDE, (row + 1) * WIDE)
            if section == STEPS_DEV - 1:
                total[span, :] = step * term
            else:
                total[span, :] += step * term
    total[TAPS : 2 * HALF, :] = jnp.zeros((2 * HALF - TAPS, CH), jnp.float32)
    core = core_ref[0]
    kept_ref[...] = total[pl.ds(pl.multiple_of(core * HALF, 8), HALF), :]
    sent_ref[...] = total[pl.ds(pl.multiple_of((1 - core) * HALF, 8), HALF), :]


def add_kernel(left_ref, right_ref, out_ref):
    out_ref[...] = left_ref[...] + right_ref[...]


def sum_kernel(parts_ref, out_ref):
    total = parts_ref[0]
    for part in range(1, parts_ref.shape[0]):
        total = total + parts_ref[part]
    for copy in range(out_ref.shape[0]):
        out_ref[copy] = total


def passed_down(value, axes, count, distance):
    return lax.ppermute(value, axes, [(i + distance, i) for i in range(count - distance)])


def local(checkpoints, conv_weight, conv_bias, point_guess, terminal):
    slices = SIZE_Y * SIZE_Z
    step = 2.0 / (STEPS_DEV * slices)
    own = point_guess.reshape(PIX, CH)
    terminal = terminal.reshape(PIX, CH)
    kernel = conv_weight.reshape(TAPS, CH)
    final = (lax.axis_index(("y", "z")) == slices - 1).astype(jnp.int32).reshape(1)
    core = lax.axis_index("core").astype(jnp.int32).reshape(1)
    upper = passed_down(own, ("y", "z"), slices, 1)

    def bound(function):
        def kernel_of(*refs):
            function(step, *refs)

        return kernel_of

    slopes, lowered, flipped, center, mean = call(
        bound(forward_kernel),
        [f32(STEPS_DEV, PIX, CH), bf16(STEPS_DEV, PADDED, WIDE), bf16(TAPS, CH), bf16(2 * CH, CH), f32(8, CH)],
    )(checkpoints.reshape(PIX, CH), kernel, conv_bias.reshape(1, CH))

    smem = pl.BlockSpec(memory_space=pltpu.SMEM)
    vmem = pl.BlockSpec(memory_space=pltpu.VMEM)
    packed = pl.pallas_call(
        bound(relax_kernel),
        out_shape=f32(ROWS, SLOT, CH),
        in_specs=[smem] + [vmem] * 6,
        out_specs=vmem,
        scratch_shapes=[pltpu.VMEM((PADDED, WIDE), jnp.bfloat16)],
        compiler_params=pltpu.CompilerParams(vmem_limit_bytes=40 << 20),
    )(final, upper, terminal, own, slopes, flipped, mean)

    gathered = lax.all_to_all(packed, "z", 0, 0)
    in_group, maps, total = call(
        group_kernel, [f32(SIZE_Z, COLS, CH), f32(SIZE_Z, CH, CH), f32(COLS + CH, CH)]
    )(gathered, center)
    first = passed_down(total, "y", SIZE_Y, 1)
    second = passed_down(total, "y", SIZE_Y, 2)
    third = passed_down(total[0:COLS], "y", SIZE_Y, 3)
    upper_error = call(carry_kernel, f32(SIZE_Z, COLS, CH))(first, second, third, in_group, maps)
    upper_error = lax.all_to_all(upper_error, "z", 0, 0).reshape(PIX, CH)

    points, kept, sent = pl.pallas_call(
        bound(second_kernel),
        out_shape=[f32(PIX, CH), f32(HALF, CH), f32(HALF, CH)],
        in_specs=[smem] * 2 + [vmem] * 10,
        out_specs=[vmem] * 3,
        scratch_shapes=[pltpu.VMEM((PADDED, WIDE), jnp.bfloat16), pltpu.VMEM((2 * HALF, CH), jnp.float32)],
        compiler_params=pltpu.CompilerParams(vmem_limit_bytes=40 << 20),
    )(final, core, upper, terminal, own, packed, upper_error, slopes, lowered, flipped, center, mean)

    plane = SIZE_X * SIZE_Y
    received = lax.ppermute(sent, "core", [(0, 1), (1, 0)])
    half = call(add_kernel, f32(HALF, CH))(kept, received)
    parts = lax.all_to_all(half.reshape(plane, CHUNK, CH), ("y", "x"), 0, 0)
    copies = call(sum_kernel, f32(SIZE_Z, CHUNK, CH))(parts)
    parts = lax.all_to_all(copies, "z", 0, 0)
    copies = call(sum_kernel, f32(plane, CHUNK, CH))(parts)
    half = lax.all_to_all(copies, ("y", "x"), 0, 0).reshape(HALF, CH)
    grad_w = lax.all_gather(half, "core").reshape(2 * HALF, CH)[0:TAPS]
    return points.reshape(1, 1, ROWS, COLS, CH), grad_w.reshape(3, 3, CH, CH)


def solution(mesh):
    fine = Mesh(mesh.devices.reshape(SIZE_Y, SIZE_Z, SIZE_X, 2), ("y", "z", "x", "core"))
    state = P(("y", "z"), ("x", "core"), None, None, None)
    return jax.shard_map(
        local,
        mesh=fine,
        in_specs=(state, P(), P(), state, P(("x", "core"), None, None, None)),
        out_specs=(state, P()),
        check_vma=False,
    )
```

time: 485 us -> 100 us (0.21)
  waiting for transfers between devices: 397 us -> 17.2 us
  blocking collectives: 0 us -> 57.6 us
  matrix products: 51.9 us -> 0 us
  between operations: 14.7 us -> 0.75 us
  starting transfers between devices: 1.41 us -> 13.2 us
  local copies, waits for them, and re-layouts: 12.8 us -> 3.31 us
  Pallas kernels: 0 us -> 7.44 us
    psum x1 -> x0, waiting for transfers between devices: 249 us -> none  [local(): grad_w = lax.psum(grad_local, ('depth', 'dp'))]
    all_gather x2 -> x0, waiting for transfers between devices: 147 us -> none  [carried_in(): pieces = jax.tree.map(lambda part: lax.all_gather(part, axis), value)]
    all_to_all x0 -> x4, blocking collectives: none -> 51.8 us  [the longest x1 17.4 us: local(): gathered = lax.all_to_all(packed, 'z', 0, 0)]
    dot_general x68 -> x0, matrix products: 45.8 us -> none  [the longest x32 38.6 us: apply_map(): jnp.einsum('bhwc,bcd->bhwd', field, coarse_map, precision=lax.Precision.H...]
    ppermute x1 -> x5, starting transfers between devices: 1.29 us -> 9.79 us  [the longest x4 5.17 us: passed_down(): lax.ppermute(value, axes, [(i + distance, i) for i in range(count - dista...]
    all_to_all x0 -> x1, waiting for transfers between devices: none -> 7.84 us  [local(): upper_error = lax.all_to_all(upper_error, 'z', 0, 0).reshape(PIX, CH)]
    ppermute x1 -> x5, waiting for transfers between devices: 1.69 us -> 9.39 us  [the longest x4 8.14 us: passed_down(): lax.ppermute(value, axes, [(i + distance, i) for i in range(count - dista...]
    pallas_call x0 -> x8, Pallas kernels: none -> 7.44 us  [the longest x1 1.8 us: local(): pl.pallas_call(bound(second_kernel), out_shape=[f32(PIX, CH), f32(HALF, C...]
  transfers between devices with their start and end apart: 4 -> 6, of which waited for: 4 -> 4; matrix products, arithmetic and copies ran while one was open for 2% -> 0% of each run, Pallas kernels for 0% -> 1%
where the time goes in v1:
time: 100 us; the launch traced here: 99.5 us
  blocking collectives  57.6 us (58%)
  waiting for transfers between devices  17.2 us (17%)
  starting transfers between devices  13.2 us (13%)
  Pallas kernels  7.44 us (7%)
  local copies, waits for them, and re-layouts  3.31 us (3%)
    all_to_all x1, blocking collectives, local(): gathered = lax.all_to_all(packed, 'z', 0, 0)  17.4 us
    all_to_all x1, blocking collectives, local(): parts = lax.all_to_all(half.reshape(plane, CHUNK, CH), ('y', 'x'), 0, 0)  13 us
    all_to_all x1, blocking collectives, local(): parts = lax.all_to_all(copies, 'z', 0, 0)  10.8 us
    all_to_all x1, blocking collectives, local(): half = lax.all_to_all(copies, ('y', 'x'), 0, 0).reshape(HALF, CH)  10.6 us
    ppermute x4, waiting for transfers between devices, passed_down(): lax.ppermute(value, axes, [(i + distance, i) for i in range(count - dista...  8.14 us
    all_to_all x1, waiting for transfers between devices, local(): upper_error = lax.all_to_all(upper_error, 'z', 0, 0).reshape(PIX, CH)  7.84 us
    all_gather x1, blocking collectives, local(): grad_w = lax.all_gather(half, 'core').reshape(2 * HALF, CH)[0:TAPS]  5.79 us
    ppermute x4, starting transfers between devices, passed_down(): lax.ppermute(value, axes, [(i + distance, i) for i in range(count - dista...  5.17 us
  transfers between devices with their start and end apart: 6, of which 4 were waited for; matrix products, arithmetic and copies ran while one was open for 0% of the time, Pallas kernels for 1%

profile of v1, /device:TPU:1, one launch (start us, length us, event | category | flops | bytes accessed | tf_op | source)
XLA Modules:
  0.0 99.5 jit_solution(10231605659786152601)
XLA Ops:
  0.6 1.3 %collective-permute-start = (f32[256,128]{1,0:T(8,128)}, f32[256,128]{1,0:T(8,128)S(1)}, u32[]{:S(2)}, u32[]{:S(2)}) collective-permute-start(f32[256,128]{1,0:T(8,128)} %bitcast.14), channel_id=1, source_target_pairs={{8,0},{16,8},{24,16},{32,24},{40,32},{48,40},{56,48},{64,56},{72,6... | collective-permute-start | bytes 393224 | tf_op jit(solution)/shard_map/ppermute | solution.py:206
  1.9 0.0 copy-start.4
  1.9 0.6 copy-done.4
  2.6 0.0 copy-start.2
  2.6 1.0 copy-done.2
  3.6 0.0 copy-start.3
  3.6 0.8 copy-done.3
  4.4 0.0 copy-start
  4.4 1.5 %shard_map.68 = (f32[4,256,128]{2,1,0:T(8,128)S(1)}, bf16[4,320,384]{2,1,0:T(8,128)(2,1)S(1)}, bf16[1152,128]{1,0:T(8,128)(2,1)S(1)}, bf16[256,128]{1,0:T(8,128)(2,1)S(1)}, f32[8,128]{1,0:T(8,128)S(1)}) custom-call(bf16[256,128]{1,0:T(8,128)(2,1)S(1)} %bitcast.21, bf16[1152,128]{1,0:T(8,128)(2,1)S(1)} %bitcast.20, f32[1,128]{1,0:T(1,128)S(1)} %bitcast.22), custom_call_target="tpu_custom_call" | custom-call | tf_op jit(solution)/shard_map/pallas_call | solution.py:225
  5.9 1.7 %collective-permute-done.refs_1_.refs_2_ = f32[256,128]{1,0:T(8,128)S(1)} collective-permute-done((f32[256,128]{1,0:T(8,128)}, f32[256,128]{1,0:T(8,128)S(1)}, u32[]{:S(2)}, u32[]{:S(2)}) %collective-permute-start) | collective-permute-done | bytes 131104 | tf_op jit(solution)/shard_map/ppermute | solution.py:206
  7.6 0.0 copy-done
  7.6 0.0 copy-done.1
  7.6 1.4 %shard_map.69.refs_5_ = f32[8,40,128]{2,1,0:T(8,128)S(1)} custom-call(s32[1]{0:T(128)} %bitcast.refs_0_, f32[256,128]{1,0:T(8,128)S(1)} %collective-permute-done.refs_1_.refs_2_, f32[256,128]{1,0:T(8,128)S(1)} %bitcast.17, f32[256,128]{1,0:T(8,128)S(1)} %bitcast.15, f32[4,256,128]{2,1,0:T(8,128)S(1)} %get-tuple-element.13.refs_4_.refs_7_, ...), custom_call_target="tpu_custom_call" | custom-call | tf_op jit(solution)/shard_map/pallas_call | solution.py:232
  9.0 17.4 %all_to_all.25.packed_ref = f32[8,40,128]{2,1,0:T(8,128)S(1)} all-to-all(f32[8,40,128]{2,1,0:T(8,128)S(1)} %shard_map.69.refs_5_), channel_id=1, replica_groups=mesh['y'=4,'z'=8,'x'=4,'core'=2] {'z'}, dimensions={0} | all-to-all | bytes 327680 | tf_op jit(solution)/shard_map/all_to_all | solution.py:241
  26.5 1.0 %shard_map.70 = (f32[8,32,128]{2,1,0:T(8,128)S(1)}, f32[8,128,128]{2,1,0:T(8,128)S(1)}, f32[160,128]{1,0:T(8,128)S(1)}) custom-call(f32[8,40,128]{2,1,0:T(8,128)S(1)} %all_to_all.25.packed_ref, bf16[256,128]{1,0:T(8,128)(2,1)S(1)} %get-tuple-element.16.center_ref.refs_10_), custom_call_target="tpu_custom_call" | custom-call | tf_op jit(solution)/shard_map/pallas_call | solution.py:242
  27.5 1.3 %collective-permute-start.2 = (f32[160,128]{1,0:T(8,128)S(1)}, f32[160,128]{1,0:T(8,128)S(1)}, u32[]{:S(2)}, u32[]{:S(2)}) collective-permute-start(f32[160,128]{1,0:T(8,128)S(1)} %get-tuple-element.17), channel_id=1, source_target_pairs={{128,0},{192,64},{129,1},{193,65},{130,2},{194,66},{131,3},{195,67... | collective-permute-start | bytes 245768 | tf_op jit(solution)/shard_map/ppermute | solution.py:206
  28.8 1.3 %collective-permute-start.1 = (f32[160,128]{1,0:T(8,128)S(1)}, f32[160,128]{1,0:T(8,128)S(1)}, u32[]{:S(2)}, u32[]{:S(2)}) collective-permute-start(f32[160,128]{1,0:T(8,128)S(1)} %get-tuple-element.17), channel_id=1, source_target_pairs={{64,0},{128,64},{192,128},{65,1},{129,65},{193,129},{66,2},{130,66... | collective-permute-start | bytes 245768 | tf_op jit(solution)/shard_map/ppermute | solution.py:206
  30.1 1.3 %collective-permute-start.3 = (f32[32,128]{1,0:T(8,128)S(1)}, f32[32,128]{1,0:T(8,128)S(1)}, u32[]{:S(2)}, u32[]{:S(2)}) collective-permute-start(f32[32,128]{1,0:T(8,128)S(1)} %slice.6), channel_id=1, source_target_pairs={{192,0},{193,1},{194,2},{195,3},{196,4},{197,5},{198,6},{199,7},{2... | collective-permute-start | bytes 49160 | tf_op jit(solution)/shard_map/ppermute | solution.py:206
  31.4 6.5 %collective-permute-done.3.third_ref = f32[32,128]{1,0:T(8,128)S(1)} collective-permute-done((f32[32,128]{1,0:T(8,128)S(1)}, f32[32,128]{1,0:T(8,128)S(1)}, u32[]{:S(2)}, u32[]{:S(2)}) %collective-permute-start.3) | collective-permute-done | bytes 16416 | tf_op jit(solution)/shard_map/ppermute | solution.py:206
  37.9 0.0 collective-permute-done.2.second_ref
  37.9 0.0 collective-permute-done.1.first_ref
  37.9 1.6 %shard_map.71 = f32[8,32,128]{2,1,0:T(8,128)} custom-call(f32[160,128]{1,0:T(8,128)S(1)} %collective-permute-done.1.first_ref, f32[160,128]{1,0:T(8,128)S(1)} %collective-permute-done.2.second_ref, f32[32,128]{1,0:T(8,128)S(1)} %collective-permute-done.3.third_ref, f32[8,32,128]{2,1,0:T(8,128)S(1)} %get-tuple-element.18.local_ref, ...), custom_call_target="tpu_custom_call" | custom-call | tf_op jit(solution)/shard_map/pallas_call | solution.py:248
  39.5 3.4 %all-to-all-start.1 = ((f32[8,32,128]{2,1,0:T(8,128)}), f32[8,32,128]{2,1,0:T(8,128)S(1)}, u32[]{:S(2)}, u32[]{:S(2)}) async-start(f32[8,32,128]{2,1,0:T(8,128)} %shard_map.71), calls=%async_computation.1 | async-start | bytes 262144 | tf_op jit(solution)/shard_map/all_to_all | solution.py:249
  42.9 7.8 %all-to-all-done.1 = f32[8,32,128]{2,1,0:T(8,128)S(1)} async-done(((f32[8,32,128]{2,1,0:T(8,128)}), f32[8,32,128]{2,1,0:T(8,128)S(1)}, u32[]{:S(2)}, u32[]{:S(2)}) %all-to-all-start.1) | async-done | bytes 131104 | tf_op jit(solution)/shard_map/all_to_all | solution.py:249
  50.7 1.8 %shard_map.72 = (f32[256,128]{1,0:T(8,128)}, f32[640,128]{1,0:T(8,128)S(1)}, f32[640,128]{1,0:T(8,128)S(1)}) custom-call(s32[1]{0:T(128)} %bitcast.refs_0_, s32[1]{0:T(128)} %bitcast.1.refs_1_, f32[256,128]{1,0:T(8,128)S(1)} %collective-permute-done.refs_1_.refs_2_, f32[256,128]{1,0:T(8,128)S(1)} %bitcast.18, f32[256,128]{1,0:T(8,128)S(1)} %bitcast.16, ...), custom_call_target="tpu_custom_call" | custom-call | tf_op jit(solution)/shard_map/pallas_call | solution.py:251
  52.5 4.6 %collective-permute-start.4 = (f32[640,128]{1,0:T(8,128)S(1)}, f32[640,128]{1,0:T(8,128)S(1)}, u32[]{:S(2)}, u32[]{:S(2)}) collective-permute-start(f32[640,128]{1,0:T(8,128)S(1)} %get-tuple-element.23), channel_id=1, source_target_pairs={{0,1},{1,0},{2,3},{3,2},{4,5},{5,4},{6,7},{7,6},{8,9},{9,8},{10,11... | collective-permute-start | bytes 983048 | tf_op jit(solution)/shard_map/ppermute | solution.py:261
  57.1 1.3 %collective-permute-done.4.right_ref = f32[640,128]{1,0:T(8,128)S(1)} collective-permute-done((f32[640,128]{1,0:T(8,128)S(1)}, f32[640,128]{1,0:T(8,128)S(1)}, u32[]{:S(2)}, u32[]{:S(2)}) %collective-permute-start.4) | collective-permute-done | bytes 327712 | tf_op jit(solution)/shard_map/ppermute | solution.py:261
  58.4 13.0 %all_to_all.26.parts_ref = f32[16,40,128]{2,1,0:T(8,128)S(1)} all-to-all(f32[16,40,128]{2,1,0:T(8,128)S(1)} %bitcast.13), channel_id=1, replica_groups=mesh['y'=4,'z'=8,'x'=4,'core'=2] {'y','x'}, dimensions={0} | all-to-all | bytes 655360 | tf_op jit(solution)/shard_map/all_to_all | solution.py:263
  71.5 10.8 %all_to_all.27.parts_ref = f32[8,40,128]{2,1,0:T(8,128)S(1)} all-to-all(f32[8,40,128]{2,1,0:T(8,128)S(1)} %shard_map.74), channel_id=1, replica_groups=mesh['y'=4,'z'=8,'x'=4,'core'=2] {'z'}, dimensions={0} | all-to-all | bytes 327680 | tf_op jit(solution)/shard_map/all_to_all | solution.py:265
  82.3 10.6 %all_to_all.28 = f32[16,40,128]{2,1,0:T(8,128)S(1)} all-to-all(f32[16,40,128]{2,1,0:T(8,128)S(1)} %shard_map.75), channel_id=1, replica_groups=mesh['y'=4,'z'=8,'x'=4,'core'=2] {'y','x'}, dimensions={0} | all-to-all | bytes 655360 | tf_op jit(solution)/shard_map/all_to_all | solution.py:267
  92.9 5.8 %all_gather.3 = f32[2,640,128]{2,1,0:T(8,128)S(1)} all-gather(f32[1,640,128]{2,1,0:T(8,128)S(1)} %bitcast.24), channel_id=1, replica_groups=mesh['y'=4,'z'=8,'x'=4,'core'=2] {'core'}, dimensions={0}, use_global_device_ids=true | all-gather | bytes 983040 | tf_op jit(solution)/shard_map/all_gather | solution.py:268
  98.7 0.9 slice.8
  (5 shorter events, 0.1 us)
Async XLA Ops:
  0.6 6.9 %collective-permute-start = (f32[256,128]{1,0:T(8,128)}, f32[256,128]{1,0:T(8,128)S(1)}, u32[]{:S(2)}, u32[]{:S(2)}) collective-permute-start(f32[256,128]{1,0:T(8,128)} %bitcast.14), channel_id=1, source_target_pairs={{8,0},{16,8},{24,16},{32,24},{40,32},{48,40},{56,48},{64,56},{72,6... | collective-permute-start | bytes 393224 | tf_op jit(solution)/shard_map/ppermute | solution.py:206
  1.9 0.7 copy-start.4
  2.6 1.0 copy-start.2
  3.6 0.8 copy-start.3
  4.4 3.2 %copy-start = (f32[1,1,8,32,128]{4,3,2,1,0:T(8,128)S(1)}, f32[1,1,8,32,128]{4,3,2,1,0:T(8,128)}, u32[]{:S(2)}) copy-start(f32[1,1,8,32,128]{4,3,2,1,0:T(8,128)} %param.8) | copy-start | bytes 393220
  4.4 3.2 %copy-start.1 = (f32[1,8,32,128]{3,2,1,0:T(8,128)S(1)}, f32[1,8,32,128]{3,2,1,0:T(8,128)}, u32[]{:S(2)}) copy-start(f32[1,8,32,128]{3,2,1,0:T(8,128)} %param.9) | copy-start | bytes 393220
  27.5 10.4 %collective-permute-start.2 = (f32[160,128]{1,0:T(8,128)S(1)}, f32[160,128]{1,0:T(8,128)S(1)}, u32[]{:S(2)}, u32[]{:S(2)}) collective-permute-start(f32[160,128]{1,0:T(8,128)S(1)} %get-tuple-element.17), channel_id=1, source_target_pairs={{128,0},{192,64},{129,1},{193,65},{130,2},{194,66},{131,3},{195,67... | collective-permute-start | bytes 245768 | tf_op jit(solution)/shard_map/ppermute | solution.py:206
  28.8 9.1 %collective-permute-start.1 = (f32[160,128]{1,0:T(8,128)S(1)}, f32[160,128]{1,0:T(8,128)S(1)}, u32[]{:S(2)}, u32[]{:S(2)}) collective-permute-start(f32[160,128]{1,0:T(8,128)S(1)} %get-tuple-element.17), channel_id=1, source_target_pairs={{64,0},{128,64},{192,128},{65,1},{129,65},{193,129},{66,2},{130,66... | collective-permute-start | bytes 245768 | tf_op jit(solution)/shard_map/ppermute | solution.py:206
  30.1 7.8 %collective-permute-start.3 = (f32[32,128]{1,0:T(8,128)S(1)}, f32[32,128]{1,0:T(8,128)S(1)}, u32[]{:S(2)}, u32[]{:S(2)}) collective-permute-start(f32[32,128]{1,0:T(8,128)S(1)} %slice.6), channel_id=1, source_target_pairs={{192,0},{193,1},{194,2},{195,3},{196,4},{197,5},{198,6},{199,7},{2... | collective-permute-start | bytes 49160 | tf_op jit(solution)/shard_map/ppermute | solution.py:206
  39.5 11.2 %all-to-all-start.1 = ((f32[8,32,128]{2,1,0:T(8,128)}), f32[8,32,128]{2,1,0:T(8,128)S(1)}, u32[]{:S(2)}, u32[]{:S(2)}) async-start(f32[8,32,128]{2,1,0:T(8,128)} %shard_map.71), calls=%async_computation.1 | async-start | bytes 262144 | tf_op jit(solution)/shard_map/all_to_all | solution.py:249
  52.5 5.9 %collective-permute-start.4 = (f32[640,128]{1,0:T(8,128)S(1)}, f32[640,128]{1,0:T(8,128)S(1)}, u32[]{:S(2)}, u32[]{:S(2)}) collective-permute-start(f32[640,128]{1,0:T(8,128)S(1)} %get-tuple-element.23), channel_id=1, source_target_pairs={{0,1},{1,0},{2,3},{3,2},{4,5},{5,4},{6,7},{7,6},{8,9},{9,8},{10,11... | collective-permute-start | bytes 983048 | tf_op jit(solution)/shard_map/ppermute | solution.py:261

commit v2 on v1

v2 whole, which is shorter than its diff:
```python
import jax
import jax.numpy as jnp
from jax import lax
from jax.experimental import pallas as pl
from jax.experimental.pallas import tpu as pltpu
from jax.sharding import Mesh, PartitionSpec as P

STEPS_DEV = 4
ROWS = 8
COLS = 32
CH = 128
PIX = ROWS * COLS
PADDED = PIX + 2 * COLS
WIDE = 3 * CH
TAPS = 9 * CH
SIZE_Y = 4
SIZE_Z = 8
SIZE_X = 4
PLANE = SIZE_X * SIZE_Y
PART = 36
CHUNK = 40
HALF = PLANE * PART
SLOT = COLS + 8
LIMIT = 12 << 20


def call(kernel, outs, scratch=()):
    return pl.pallas_call(
        kernel,
        out_shape=outs,
        scratch_shapes=scratch,
        compiler_params=pltpu.CompilerParams(vmem_limit_bytes=LIMIT),
    )


def f32(*shape):
    return jax.ShapeDtypeStruct(shape, jnp.float32)


def bf16(*shape):
    return jax.ShapeDtypeStruct(shape, jnp.bfloat16)


def columns():
    return lax.broadcasted_iota(jnp.int32, (PIX, CH), 0) % COLS


def clear_edges(buffer):
    zeros = jnp.zeros((COLS, WIDE), jnp.bfloat16)
    buffer[0:COLS, :] = zeros
    buffer[COLS + PIX : PADDED, :] = zeros


def spread(buffer, low, col):
    wide = low.astype(jnp.float32)
    before = jnp.where(col > 0, pltpu.roll(wide, 1, 0), 0.0)
    after = jnp.where(col < COLS - 1, pltpu.roll(wide, PIX - 1, 0), 0.0)
    buffer[COLS : COLS + PIX, 0:CH] = before.astype(jnp.bfloat16)
    buffer[COLS : COLS + PIX, CH : 2 * CH] = low
    buffer[COLS : COLS + PIX, 2 * CH : WIDE] = after.astype(jnp.bfloat16)


def convolve(buffer, kernel):
    total = None
    for row in range(3):
        part = jnp.dot(
            buffer[row * COLS : row * COLS + PIX, :],
            kernel[row * WIDE : (row + 1) * WIDE, :],
            preferred_element_type=jnp.float32,
        )
        total = part if total is None else total + part
    return total


def split(value):
    high = value.astype(jnp.bfloat16)
    return high, (value - high.astype(jnp.float32)).astype(jnp.bfloat16)


def exact_left(value, weight_twice):
    return jnp.dot(
        jnp.concatenate(split(value), axis=1), weight_twice, preferred_element_type=jnp.float32
    )


def forward_kernel(
    step, core_ref, start_ref, kernel_ref, bias_ref, slope_ref, lowered_ref, flipped_ref, center_ref, mean_ref
):
    col = columns()
    bias = bias_ref[...]
    current = start_ref[...].astype(jnp.float32)
    for section in range(STEPS_DEV):
        buffer = lowered_ref.at[section]
        clear_edges(buffer)
        spread(buffer, current.astype(jnp.bfloat16), col)
        tanh_out = jnp.tanh(convolve(buffer, kernel_ref) + bias)
        slope = 1.0 - tanh_out * tanh_out
        slope_ref[section] = slope
        if section == 0:
            mean = jnp.sum(slope, axis=0, keepdims=True) * (STEPS_DEV * step / PIX)
            mean_ref[...] = jnp.broadcast_to(mean, (8, CH))
        current = current + step * tanh_out
    for tap in range(9):
        block = kernel_ref[(8 - tap) * CH : (9 - tap) * CH, :].astype(jnp.float32)
        turned = block.T.astype(jnp.bfloat16)
        flipped_ref[tap * CH : (tap + 1) * CH, :] = turned
        if tap == 4:
            center_ref[0:CH, :] = turned
            center_ref[CH : 2 * CH, :] = turned


def adjoint_step(buffer, flipped, slope, value, step, col):
    low = (slope * value).astype(jnp.bfloat16)
    spread(buffer, low, col)
    return low, value + step * convolve(buffer, flipped)


def load_kernel(own_ref, terminal_ref, after_ref, own_out, terminal_out):
    own_out[...] = own_ref[...]
    terminal_out[...] = terminal_ref[...]


def relax_kernel(
    step, final_ref, upper_ref, terminal_ref, own_ref, slope_ref, flipped_ref, mean_ref, packed_ref, chosen_ref, buffer
):
    col = columns()
    clear_edges(buffer)
    value = jnp.where(final_ref[0] == 1, terminal_ref[...], upper_ref[...])
    chosen_ref[...] = value
    for section in range(STEPS_DEV - 1, -1, -1):
        low, value = adjoint_step(buffer, flipped_ref, slope_ref[section], value, step, col)
    residue = value - own_ref[...]
    for part in range(ROWS):
        packed_ref[part, 0:COLS, :] = residue[part * COLS : (part + 1) * COLS]
        packed_ref[part, COLS:SLOT, :] = mean_ref[...]


def moved_by(value, mean, center):
    return exact_left(value * mean, center)


def group_kernel(packed_ref, center_ref, local_ref, total_ref):
    center = center_ref[...]
    error = jnp.zeros((COLS, CH), jnp.float32)
    for place in range(SIZE_Z - 1, -1, -1):
        local_ref[place] = error
        mean = packed_ref[place, COLS : COLS + 1, :]
        error = packed_ref[place, 0:COLS, :] + error + moved_by(error, mean, center)
        total_ref[COLS + place : COLS + place + 1, :] = mean
    total_ref[0:COLS, :] = error


def maps_kernel(packed_ref, center_ref, after_ref, maps_ref):
    center = center_ref[...]
    row = lax.broadcasted_iota(jnp.int32, (CH, CH), 0)
    lane = lax.broadcasted_iota(jnp.int32, (CH, CH), 1)
    identity = jnp.where(row == lane, 1.0, 0.0)
    change = jnp.zeros((CH, CH), jnp.float32)
    for place in range(SIZE_Z - 1, -1, -1):
        high, low = split(change)
        lanes = slice(place * CH, (place + 1) * CH)
        maps_ref[0:CH, lanes] = high
        maps_ref[CH : 2 * CH, lanes] = high
        maps_ref[2 * CH : 3 * CH, lanes] = low
        if place > 0:
            change = change + moved_by(change + identity, packed_ref[place, COLS : COLS + 1, :], center)


def carry_kernel(first_ref, second_ref, third_ref, local_ref, maps_ref, center_ref, after_ref, upper_ref):
    center = center_ref[...]
    carry = third_ref[...]
    for group_ref in (second_ref, first_ref):
        for place in range(SIZE_Z - 1, -1, -1):
            carry = carry + moved_by(carry, group_ref[COLS + place : COLS + place + 1, :], center)
        carry = carry + group_ref[0:COLS, :]
    high, low = split(carry)
    moved = jnp.dot(
        jnp.concatenate([high, low, high], axis=1), maps_ref[...], preferred_element_type=jnp.float32
    )
    for place in range(SIZE_Z):
        upper_ref[place] = local_ref[place] + carry + moved[:, place * CH : (place + 1) * CH]


def turn_kernel(lowered_ref, after_ref, turned_ref):
    for section in range(STEPS_DEV):
        for row in range(3):
            block = lowered_ref[section, row * COLS : row * COLS + PIX, :].astype(jnp.float32)
            turned_ref[row * WIDE : (row + 1) * WIDE, section * PIX : (section + 1) * PIX] = block.T.astype(jnp.bfloat16)


def points_kernel(own_ref, packed_ref, error_ref, mean_ref, center_ref, points_ref):
    error = error_ref[...]
    moved = moved_by(error, mean_ref[0:1, :], center_ref[...])
    for part in range(ROWS):
        span = slice(part * COLS, (part + 1) * COLS)
        points_ref[span, :] = own_ref[span, :] + (packed_ref[part, 0:COLS, :] + error[span] + moved[span])


def second_kernel(
    step, core_ref, chosen_ref, error_ref, slope_ref, turned_ref, flipped_ref,
    kept_ref, sent_ref, buffer, total,
):
    col = columns()
    clear_edges(buffer)
    value = chosen_ref[...] + error_ref[...]
    for section in range(STEPS_DEV - 1, -1, -1):
        if section > 0:
            low, value = adjoint_step(buffer, flipped_ref, slope_ref[section], value, step, col)
        else:
            low = (slope_ref[section] * value).astype(jnp.bfloat16)
        term = jnp.dot(
            turned_ref[:, section * PIX : (section + 1) * PIX], low, preferred_element_type=jnp.float32
        )
        if section == STEPS_DEV - 1:
            total[...] = term
        else:
            total[...] += term
    first_core = core_ref[0] == 0
    blank = jnp.zeros((CHUNK - PART, CH), jnp.float32)
    for part in range(PLANE):
        lower = step * total[part * PART : (part + 1) * PART, :]
        upper = step * total[HALF + part * PART : HALF + (part + 1) * PART, :]
        kept_ref[part, 0:PART, :] = jnp.where(first_core, lower, upper)
        sent_ref[part, 0:PART, :] = jnp.where(first_core, upper, lower)
        kept_ref[part, PART:CHUNK, :] = blank
        sent_ref[part, PART:CHUNK, :] = blank


def compact_kernel(parts_ref, out_ref):
    for part in range(PLANE):
        out_ref[part * PART : (part + 1) * PART, :] = parts_ref[part, 0:PART, :]


def add_kernel(left_ref, right_ref, out_ref):
    out_ref[...] = left_ref[...] + right_ref[...]


def sum_kernel(parts_ref, out_ref):
    total = parts_ref[0]
    for part in range(1, parts_ref.shape[0]):
        total = total + parts_ref[part]
    for copy in range(out_ref.shape[0]):
        out_ref[copy] = total


def join_kernel(core_ref, own_ref, other_ref, out_ref, sems):
    core = core_ref[0]
    copies = [
        pltpu.make_async_copy(part, out_ref.at[pl.ds(pl.multiple_of(place * HALF, 8), HALF), :], sems.at[k])
        for k, (part, place) in enumerate(((own_ref, core), (other_ref, 1 - core)))
    ]
    for copy in copies:
        copy.start()
    for copy in copies:
        copy.wait()


def passed_down(value, axes, count, distance):
    return lax.ppermute(value, axes, [(i + distance, i) for i in range(count - distance)])


def local(checkpoints, conv_weight, conv_bias, point_guess, terminal):
    slices = SIZE_Y * SIZE_Z
    step = 2.0 / (STEPS_DEV * slices)
    own = point_guess.reshape(PIX, CH)
    terminal = terminal.reshape(PIX, CH)
    kernel = conv_weight.reshape(TAPS, CH)
    final = (lax.axis_index(("y", "z")) == slices - 1).astype(jnp.int32).reshape(1)
    core = lax.axis_index("core").astype(jnp.int32).reshape(1)
    upper = passed_down(own, ("y", "z"), slices, 1)

    def bound(function):
        def kernel_of(*refs):
            function(step, *refs)

        return kernel_of

    smem = pl.BlockSpec(memory_space=pltpu.SMEM)
    vmem = pl.BlockSpec(memory_space=pltpu.VMEM)
    slopes, lowered, flipped, center, mean = pl.pallas_call(
        bound(forward_kernel),
        out_shape=[f32(STEPS_DEV, PIX, CH), bf16(STEPS_DEV, PADDED, WIDE), bf16(TAPS, CH), bf16(2 * CH, CH), f32(8, CH)],
        in_specs=[smem] + [vmem] * 3,
        out_specs=[vmem] * 5,
        compiler_params=pltpu.CompilerParams(vmem_limit_bytes=LIMIT),
    )(core, checkpoints.reshape(PIX, CH), kernel, conv_bias.reshape(1, CH))
    own_here, terminal_here = call(load_kernel, [f32(PIX, CH)] * 2)(own, terminal, mean)

    packed, chosen = pl.pallas_call(
        bound(relax_kernel),
        out_shape=[f32(ROWS, SLOT, CH), f32(PIX, CH)],
        in_specs=[smem] + [vmem] * 6,
        out_specs=[vmem] * 2,
        scratch_shapes=[pltpu.VMEM((PADDED, WIDE), jnp.bfloat16)],
        compiler_params=pltpu.CompilerParams(vmem_limit_bytes=LIMIT),
    )(final, upper, terminal_here, own_here, slopes, flipped, mean)

    gathered = lax.all_to_all(packed, "z", 0, 0)
    in_group, total = call(group_kernel, [f32(SIZE_Z, COLS, CH), f32(SLOT, CH)])(gathered, center)
    first = passed_down(total, "y", SIZE_Y, 1)
    second = passed_down(total, "y", SIZE_Y, 2)
    third = passed_down(total[0:COLS], "y", SIZE_Y, 3)
    maps = call(maps_kernel, bf16(3 * CH, SIZE_Z * CH))(gathered, center, total)
    turned = call(turn_kernel, bf16(TAPS, STEPS_DEV * PIX))(lowered, total)
    upper_error = pl.pallas_call(
        carry_kernel,
        out_shape=f32(SIZE_Z, COLS, CH),
        in_specs=[vmem] * 6 + [pl.BlockSpec(memory_space=pl.ANY)],
        out_specs=vmem,
        compiler_params=pltpu.CompilerParams(vmem_limit_bytes=LIMIT),
    )(first, second, third, in_group, maps, center, turned)
    upper_error = lax.all_to_all(upper_error, "z", 0, 0).reshape(PIX, CH)

    kept, sent = pl.pallas_call(
        bound(second_kernel),
        out_shape=[f32(PLANE, CHUNK, CH)] * 2,
        in_specs=[smem] + [vmem] * 5,
        out_specs=[vmem] * 2,
        scratch_shapes=[pltpu.VMEM((PADDED, WIDE), jnp.bfloat16), pltpu.VMEM((TAPS, CH), jnp.float32)],
        compiler_params=pltpu.CompilerParams(vmem_limit_bytes=LIMIT),
    )(core, chosen, upper_error, slopes, turned, flipped)

    received = lax.ppermute(sent, "core", [(0, 1), (1, 0)])
    points = call(points_kernel, f32(PIX, CH))(own_here, packed, upper_error, mean, center)
    half = call(add_kernel, f32(PLANE, CHUNK, CH))(kept, received)
    parts = lax.all_to_all(half, ("y", "x"), 0, 0)
    copies = call(sum_kernel, f32(SIZE_Z, CHUNK, CH))(parts)
    parts = lax.all_to_all(copies, "z", 0, 0)
    copies = call(sum_kernel, f32(PLANE, CHUNK, CH))(parts)
    parts = lax.all_to_all(copies, ("y", "x"), 0, 0)
    half = call(compact_kernel, f32(HALF, CH))(parts)
    other = lax.ppermute(half, "core", [(0, 1), (1, 0)])
    grad_w = pl.pallas_call(
        join_kernel,
        out_shape=f32(TAPS, CH),
        in_specs=[smem, vmem, vmem],
        out_specs=pl.BlockSpec(memory_space=pl.ANY),
        scratch_shapes=[pltpu.SemaphoreType.DMA((2,))],
        compiler_params=pltpu.CompilerParams(vmem_limit_bytes=LIMIT),
    )(core, half, other)
    return points.reshape(1, 1, ROWS, COLS, CH), grad_w.reshape(3, 3, CH, CH)


def solution(mesh):
    fine = Mesh(mesh.devices.reshape(SIZE_Y, SIZE_Z, SIZE_X, 2), ("y", "z", "x", "core"))
    state = P(("y", "z"), ("x", "core"), None, None, None)
    return jax.shard_map(
        local,
        mesh=fine,
        in_specs=(state, P(), P(), state, P(("x", "core"), None, None, None)),
        out_specs=(state, P()),
        check_vma=False,
    )
```

time: 100 us -> 99.6 us (level)
  waiting for transfers between devices: 17.2 us -> 6.21 us
  blocking collectives: 57.6 us -> 62.2 us
  Pallas kernels: 7.44 us -> 11.2 us
  starting transfers between devices: 13.2 us -> 14.5 us
    all_to_all x2 -> x3, blocking collectives: 23.6 us -> 33.6 us  [the longest x1 12.7 us: local(): parts = lax.all_to_all(half, ('y', 'x'), 0, 0)]
    all_to_all x1 -> x0, waiting for transfers between devices: 7.84 us -> none  [local(): upper_error = lax.all_to_all(upper_error, 'z', 0, 0).reshape(PIX, CH)]
    all_gather x1 -> x0, blocking collectives: 5.79 us -> none  [local(): grad_w = lax.all_gather(half, 'core').reshape(2 * HALF, CH)[0:TAPS]]
    ppermute x0 -> x1, starting transfers between devices: none -> 3.99 us  [local(): other = lax.ppermute(half, 'core', [(0, 1), (1, 0)])]
    pallas_call x7 -> x13, Pallas kernels: 7.42 us -> 11.2 us  [the longest x1 2.18 us: local(): pl.pallas_call(carry_kernel, out_shape=f32(SIZE_Z, COLS, CH), in_specs=[v...]
    ppermute x4, waiting for transfers between devices: 8.14 us -> 4.58 us  [passed_down(): lax.ppermute(value, axes, [(i + distance, i) for i in range(count - dista...]
    all_to_all x1 -> x0, starting transfers between devices: 3.37 us -> none  [local(): upper_error = lax.all_to_all(upper_error, 'z', 0, 0).reshape(PIX, CH)]
    unnamed x10, local copies, waits for them, and re-layouts: 2.46 us -> 4.25 us
  transfers between devices with their start and end apart: 6 -> 6, of which waited for: 4 -> 3; matrix products, arithmetic and copies ran while one was open for 0% -> 0% of each run, Pallas kernels for 1% -> 4%
where the time goes in v2:
time: 99.6 us; the launch traced here: 99.1 us
  blocking collectives  62.2 us (62%)
  starting transfers between devices  14.5 us (15%)
  Pallas kernels  11.2 us (11%)
  waiting for transfers between devices  6.21 us (6%)
  local copies, waits for them, and re-layouts  4.25 us (4%)
    all_to_all x1, blocking collectives, local(): gathered = lax.all_to_all(packed, 'z', 0, 0)  17.8 us
    all_to_all x1, blocking collectives, local(): parts = lax.all_to_all(half, ('y', 'x'), 0, 0)  12.7 us
    all_to_all x1, blocking collectives, local(): parts = lax.all_to_all(copies, 'z', 0, 0)  10.8 us
    all_to_all x1, blocking collectives, local(): parts = lax.all_to_all(copies, ('y', 'x'), 0, 0)  10.6 us
    all_to_all x1, blocking collectives, local(): upper_error = lax.all_to_all(upper_error, 'z', 0, 0).reshape(PIX, CH)  10.3 us
    ppermute x1, starting transfers between devices, local(): received = lax.ppermute(sent, 'core', [(0, 1), (1, 0)])  5.33 us
    ppermute x4, starting transfers between devices, passed_down(): lax.ppermute(value, axes, [(i + distance, i) for i in range(count - dista...  5.17 us
    ppermute x4, waiting for transfers between devices, passed_down(): lax.ppermute(value, axes, [(i + distance, i) for i in range(count - dista...  4.58 us
  transfers between devices with their start and end apart: 6, of which 3 were waited for; matrix products, arithmetic and copies ran while one was open for 0% of the time, Pallas kernels for 4%

profile of v2, /device:TPU:1, one launch (start us, length us, event | category | flops | bytes accessed | tf_op | source)
XLA Modules:
  0.0 99.1 jit_solution(11856164437583931827)
XLA Ops:
  0.6 1.3 %collective-permute-start = (f32[256,128]{1,0:T(8,128)}, f32[256,128]{1,0:T(8,128)S(1)}, u32[]{:S(2)}, u32[]{:S(2)}) collective-permute-start(f32[256,128]{1,0:T(8,128)} %bitcast.14), channel_id=1, source_target_pairs={{8,0},{16,8},{24,16},{32,24},{40,32},{48,40},{56,48},{64,56},{72,6... | collective-permute-start | bytes 393224 | tf_op jit(solution)/shard_map/ppermute | solution.py:259
  1.9 1.0 copy-done
  2.9 0.8 copy-done.3
  3.7 0.7 copy-done.4
  4.4 1.5 %shard_map.68 = (f32[4,256,128]{2,1,0:T(8,128)S(1)}, bf16[4,320,384]{2,1,0:T(8,128)(2,1)S(1)}, bf16[1152,128]{1,0:T(8,128)(2,1)S(1)}, bf16[256,128]{1,0:T(8,128)(2,1)S(1)}, f32[8,128]{1,0:T(8,128)S(1)}) custom-call(s32[1]{0:T(128)} %bitcast.2.refs_0_.core_ref, bf16[256,128]{1,0:T(8,128)(2,1)S(1)} %bitcast.16, bf16[1152,128]{1,0:T(8,128)(2,1)S(1)} %bitcast.12, ...), custom_call_target="tpu_custom_call" | custom-call | tf_op jit(solution)/shard_map/pallas_call | solution.py:280
  5.9 0.0 copy-start.1
  5.9 0.9 copy-done.1
  6.8 0.9 copy-done.2
  7.7 0.0 collective-permute-done.refs_1_
  7.7 1.4 %shard_map.70 = (f32[8,40,128]{2,1,0:T(8,128)S(1)}, f32[256,128]{1,0:T(8,128)S(1)}) custom-call(s32[1]{0:T(128)} %bitcast.6.refs_0_, f32[256,128]{1,0:T(8,128)S(1)} %collective-permute-done.refs_1_, f32[256,128]{1,0:T(8,128)S(1)} %get-tuple-element.17.refs_2_, f32[256,128]{1,0:T(8,128)S(1)} %get-tuple-element.16.refs_3_.own_ref, ...), custom_call_target="tpu_custom_call" | custom-call | tf_op jit(solution)/shard_map/pallas_call | solution.py:289
  9.2 17.8 %all_to_all.25.packed_ref = f32[8,40,128]{2,1,0:T(8,128)S(1)} all-to-all(f32[8,40,128]{2,1,0:T(8,128)S(1)} %get-tuple-element.20.packed_ref), channel_id=1, replica_groups=mesh['y'=4,'z'=8,'x'=4,'core'=2] {'z'}, dimensions={0} | all-to-all | bytes 327680 | tf_op jit(solution)/shard_map/all_to_all | solution.py:298
  27.0 1.0 shard_map.71
  28.0 1.3 %collective-permute-start.1 = (f32[40,128]{1,0:T(8,128)S(1)}, f32[40,128]{1,0:T(8,128)S(1)}, u32[]{:S(2)}, u32[]{:S(2)}) collective-permute-start(f32[40,128]{1,0:T(8,128)S(1)} %get-tuple-element.22.after_ref), channel_id=1, source_target_pairs={{64,0},{128,64},{192,128},{65,1},{129,65},{193,129},{66,2},{130,66... | collective-permute-start | bytes 61448 | tf_op jit(solution)/shard_map/ppermute | solution.py:259
  29.3 1.3 %collective-permute-start.2 = (f32[40,128]{1,0:T(8,128)S(1)}, f32[40,128]{1,0:T(8,128)S(1)}, u32[]{:S(2)}, u32[]{:S(2)}) collective-permute-start(f32[40,128]{1,0:T(8,128)S(1)} %get-tuple-element.22.after_ref), channel_id=1, source_target_pairs={{128,0},{192,64},{129,1},{193,65},{130,2},{194,66},{131,3},{195,67... | collective-permute-start | bytes 61448 | tf_op jit(solution)/shard_map/ppermute | solution.py:259
  30.6 1.3 %collective-permute-start.3 = (f32[32,128]{1,0:T(8,128)S(1)}, f32[32,128]{1,0:T(8,128)S(1)}, u32[]{:S(2)}, u32[]{:S(2)}) collective-permute-start(f32[32,128]{1,0:T(8,128)S(1)} %slice.3), channel_id=1, source_target_pairs={{192,0},{193,1},{194,2},{195,3},{196,4},{197,5},{198,6},{199,7},{2... | collective-permute-start | bytes 49160 | tf_op jit(solution)/shard_map/ppermute | solution.py:259
  31.9 0.7 shard_map.73.after_ref.refs_4_
  32.6 0.9 shard_map.72.maps_ref
  33.5 4.6 %collective-permute-done.3.third_ref = f32[32,128]{1,0:T(8,128)S(1)} collective-permute-done((f32[32,128]{1,0:T(8,128)S(1)}, f32[32,128]{1,0:T(8,128)S(1)}, u32[]{:S(2)}, u32[]{:S(2)}) %collective-permute-start.3) | collective-permute-done | bytes 16416 | tf_op jit(solution)/shard_map/ppermute | solution.py:259
  38.1 0.0 collective-permute-done.1.first_ref
  38.1 0.0 collective-permute-done.2.second_ref
  38.1 2.2 %shard_map.74 = f32[8,32,128]{2,1,0:T(8,128)S(1)} custom-call(f32[40,128]{1,0:T(8,128)S(1)} %collective-permute-done.1.first_ref, f32[40,128]{1,0:T(8,128)S(1)} %collective-permute-done.2.second_ref, f32[32,128]{1,0:T(8,128)S(1)} %collective-permute-done.3.third_ref, f32[8,32,128]{2,1,0:T(8,128)S(1)} %get-tuple-element.23.local_ref, ...), custom_call_target="tpu_custom_call" | custom-call | tf_op jit(solution)/shard_map/pallas_call | solution.py:305
  40.3 10.3 %all_to_all.26 = f32[8,32,128]{2,1,0:T(8,128)S(1)} all-to-all(f32[8,32,128]{2,1,0:T(8,128)S(1)} %shard_map.74), channel_id=1, replica_groups=mesh['y'=4,'z'=8,'x'=4,'core'=2] {'z'}, dimensions={0} | all-to-all | bytes 262144 | tf_op jit(solution)/shard_map/all_to_all | solution.py:312
  50.6 1.7 %shard_map.76 = (f32[16,40,128]{2,1,0:T(8,128)S(1)}, f32[16,40,128]{2,1,0:T(8,128)S(1)}) custom-call(s32[1]{0:T(128)} %bitcast.2.refs_0_.core_ref, f32[256,128]{1,0:T(8,128)S(1)} %get-tuple-element.25.refs_1_, f32[256,128]{1,0:T(8,128)S(1)} %bitcast.10, f32[4,256,128]{2,1,0:T(8,128)S(1)} %get-tuple-element.18.refs_4_.refs_3_, ...), custom_call_target="tpu_custom_call" | custom-call | tf_op jit(solution)/shard_map/pallas_call | solution.py:314
  52.3 5.3 %collective-permute-start.4 = (f32[16,40,128]{2,1,0:T(8,128)S(1)}, f32[16,40,128]{2,1,0:T(8,128)S(1)}, u32[]{:S(2)}, u32[]{:S(2)}) collective-permute-start(f32[16,40,128]{2,1,0:T(8,128)S(1)} %get-tuple-element.27), channel_id=1, source_target_pairs={{0,1},{1,0},{2,3},{3,2},{4,5},{5,4},{6,7},{7,6},{8,9},{9,8},{10,11... | collective-permute-start | bytes 983048 | tf_op jit(solution)/shard_map/ppermute | solution.py:323
  57.6 1.3 %collective-permute-done.4.right_ref = f32[16,40,128]{2,1,0:T(8,128)S(1)} collective-permute-done((f32[16,40,128]{2,1,0:T(8,128)S(1)}, f32[16,40,128]{2,1,0:T(8,128)S(1)}, u32[]{:S(2)}, u32[]{:S(2)}) %collective-permute-start.4) | collective-permute-done | bytes 327712 | tf_op jit(solution)/shard_map/ppermute | solution.py:323
  58.9 12.7 %all_to_all.27.parts_ref = f32[16,40,128]{2,1,0:T(8,128)S(1)} all-to-all(f32[16,40,128]{2,1,0:T(8,128)S(1)} %shard_map.77), channel_id=1, replica_groups=mesh['y'=4,'z'=8,'x'=4,'core'=2] {'y','x'}, dimensions={0} | all-to-all | bytes 655360 | tf_op jit(solution)/shard_map/all_to_all | solution.py:326
  71.7 10.8 %all_to_all.28.parts_ref = f32[8,40,128]{2,1,0:T(8,128)S(1)} all-to-all(f32[8,40,128]{2,1,0:T(8,128)S(1)} %shard_map.78), channel_id=1, replica_groups=mesh['y'=4,'z'=8,'x'=4,'core'=2] {'z'}, dimensions={0} | all-to-all | bytes 327680 | tf_op jit(solution)/shard_map/all_to_all | solution.py:328
  82.5 10.6 %all_to_all.29.parts_ref = f32[16,40,128]{2,1,0:T(8,128)S(1)} all-to-all(f32[16,40,128]{2,1,0:T(8,128)S(1)} %shard_map.79), channel_id=1, replica_groups=mesh['y'=4,'z'=8,'x'=4,'core'=2] {'y','x'}, dimensions={0} | all-to-all | bytes 655360 | tf_op jit(solution)/shard_map/all_to_all | solution.py:330
  93.1 4.0 %collective-permute-start.5 = (f32[576,128]{1,0:T(8,128)S(1)}, f32[576,128]{1,0:T(8,128)S(1)}, u32[]{:S(2)}, u32[]{:S(2)}) collective-permute-start(f32[576,128]{1,0:T(8,128)S(1)} %shard_map.80.own_ref), channel_id=1, source_target_pairs={{0,1},{1,0},{2,3},{3,2},{4,5},{5,4},{6,7},{7,6},{8,9},{9,8},{10,11... | collective-permute-start | bytes 884744 | tf_op jit(solution)/shard_map/ppermute | solution.py:332
  97.1 0.8 shard_map.75
  97.9 0.4 collective-permute-done.5.other_ref
  98.3 0.8 shard_map.81
  (10 shorter events, 0.2 us)
Async XLA Ops:
  0.6 7.1 %collective-permute-start = (f32[256,128]{1,0:T(8,128)}, f32[256,128]{1,0:T(8,128)S(1)}, u32[]{:S(2)}, u32[]{:S(2)}) collective-permute-start(f32[256,128]{1,0:T(8,128)} %bitcast.14), channel_id=1, source_target_pairs={{8,0},{16,8},{24,16},{32,24},{40,32},{48,40},{56,48},{64,56},{72,6... | collective-permute-start | bytes 393224 | tf_op jit(solution)/shard_map/ppermute | solution.py:259
  1.9 1.0 copy-start
  2.9 0.8 copy-start.3
  3.7 0.7 copy-start.4
  5.9 0.9 copy-start.1
  6.8 0.9 copy-start.2
  28.0 10.1 %collective-permute-start.1 = (f32[40,128]{1,0:T(8,128)S(1)}, f32[40,128]{1,0:T(8,128)S(1)}, u32[]{:S(2)}, u32[]{:S(2)}) collective-permute-start(f32[40,128]{1,0:T(8,128)S(1)} %get-tuple-element.22.after_ref), channel_id=1, source_target_pairs={{64,0},{128,64},{192,128},{65,1},{129,65},{193,129},{66,2},{130,66... | collective-permute-start | bytes 61448 | tf_op jit(solution)/shard_map/ppermute | solution.py:259
  29.3 8.8 %collective-permute-start.2 = (f32[40,128]{1,0:T(8,128)S(1)}, f32[40,128]{1,0:T(8,128)S(1)}, u32[]{:S(2)}, u32[]{:S(2)}) collective-permute-start(f32[40,128]{1,0:T(8,128)S(1)} %get-tuple-element.22.after_ref), channel_id=1, source_target_pairs={{128,0},{192,64},{129,1},{193,65},{130,2},{194,66},{131,3},{195,67... | collective-permute-start | bytes 61448 | tf_op jit(solution)/shard_map/ppermute | solution.py:259
  30.6 7.5 %collective-permute-start.3 = (f32[32,128]{1,0:T(8,128)S(1)}, f32[32,128]{1,0:T(8,128)S(1)}, u32[]{:S(2)}, u32[]{:S(2)}) collective-permute-start(f32[32,128]{1,0:T(8,128)S(1)} %slice.3), channel_id=1, source_target_pairs={{192,0},{193,1},{194,2},{195,3},{196,4},{197,5},{198,6},{199,7},{2... | collective-permute-start | bytes 49160 | tf_op jit(solution)/shard_map/ppermute | solution.py:259
  52.3 6.6 %collective-permute-start.4 = (f32[16,40,128]{2,1,0:T(8,128)S(1)}, f32[16,40,128]{2,1,0:T(8,128)S(1)}, u32[]{:S(2)}, u32[]{:S(2)}) collective-permute-start(f32[16,40,128]{2,1,0:T(8,128)S(1)} %get-tuple-element.27), channel_id=1, source_target_pairs={{0,1},{1,0},{2,3},{3,2},{4,5},{5,4},{6,7},{7,6},{8,9},{9,8},{10,11... | collective-permute-start | bytes 983048 | tf_op jit(solution)/shard_map/ppermute | solution.py:323
  93.1 5.2 %collective-permute-start.5 = (f32[576,128]{1,0:T(8,128)S(1)}, f32[576,128]{1,0:T(8,128)S(1)}, u32[]{:S(2)}, u32[]{:S(2)}) collective-permute-start(f32[576,128]{1,0:T(8,128)S(1)} %shard_map.80.own_ref), channel_id=1, source_target_pairs={{0,1},{1,0},{2,3},{3,2},{4,5},{5,4},{6,7},{7,6},{8,9},{9,8},{10,11... | collective-permute-start | bytes 884744 | tf_op jit(solution)/shard_map/ppermute | solution.py:332

commit v3 on v2

--- a/solution.py
+++ b/solution.py
@@ -24,13 +24,25 @@
 LIMIT = 12 << 20
 
 
-def call(kernel, outs, scratch=()):
-    return pl.pallas_call(
-        kernel,
-        out_shape=outs,
-        scratch_shapes=scratch,
-        compiler_params=pltpu.CompilerParams(vmem_limit_bytes=LIMIT),
-    )
+def call(kernel, outs, micros, specs=None, scratch=()):
+    space = pl.BlockSpec(memory_space=pltpu.VMEM)
+    places = {"s": pl.BlockSpec(memory_space=pltpu.SMEM), "v": space, "a": pl.BlockSpec(memory_space=pl.ANY)}
+
+    def run(*operands):
+        kinds = specs or "v" * len(operands)
+        return pl.pallas_call(
+            kernel,
+            out_shape=outs,
+            in_specs=[places[kind] for kind in kinds],
+            out_specs=[space] * len(outs) if isinstance(outs, list) else space,
+            scratch_shapes=scratch,
+            cost_estimate=pl.CostEstimate(
+                flops=int(micros * 1e9), bytes_accessed=int(micros * 3.6e6), transcendentals=0
+            ),
+            compiler_params=pltpu.CompilerParams(vmem_limit_bytes=LIMIT),
+        )(*operands)
+
+    return run
 
 
 def f32(*shape):
@@ -84,7 +96,7 @@
 
 
 def forward_kernel(
-    step, core_ref, start_ref, kernel_ref, bias_ref, slope_ref, lowered_ref, flipped_ref, center_ref, mean_ref
+    step, core_ref, place_ref, final_ref, start_ref, kernel_ref, bias_ref, slope_ref, lowered_ref, flipped_ref, center_ref, mean_ref,
 ):
     col = columns()
     bias = bias_ref[...]
@@ -115,11 +127,6 @@
     return low, value + step * convolve(buffer, flipped)
 
 
-def load_kernel(own_ref, terminal_ref, after_ref, own_out, terminal_out):
-    own_out[...] = own_ref[...]
-    terminal_out[...] = terminal_ref[...]
-
-
 def relax_kernel(
     step, final_ref, upper_ref, terminal_ref, own_ref, slope_ref, flipped_ref, mean_ref, packed_ref, chosen_ref, buffer
 ):
@@ -139,44 +146,44 @@
     return exact_left(value * mean, center)
 
 
-def group_kernel(packed_ref, center_ref, local_ref, total_ref):
-    center = center_ref[...]
-    error = jnp.zeros((COLS, CH), jnp.float32)
-    for place in range(SIZE_Z - 1, -1, -1):
-        local_ref[place] = error
-        mean = packed_ref[place, COLS : COLS + 1, :]
-        error = packed_ref[place, 0:COLS, :] + error + moved_by(error, mean, center)
-        total_ref[COLS + place : COLS + place + 1, :] = mean
-    total_ref[0:COLS, :] = error
-
-
-def maps_kernel(packed_ref, center_ref, after_ref, maps_ref):
+def group_kernel(packed_ref, center_ref, local_ref, maps_ref, total_ref):
     center = center_ref[...]
     row = lax.broadcasted_iota(jnp.int32, (CH, CH), 0)
     lane = lax.broadcasted_iota(jnp.int32, (CH, CH), 1)
     identity = jnp.where(row == lane, 1.0, 0.0)
+    error = jnp.zeros((COLS, CH), jnp.float32)
     change = jnp.zeros((CH, CH), jnp.float32)
     for place in range(SIZE_Z - 1, -1, -1):
-        high, low = split(change)
-        lanes = slice(place * CH, (place + 1) * CH)
-        maps_ref[0:CH, lanes] = high
-        maps_ref[CH : 2 * CH, lanes] = high
-        maps_ref[2 * CH : 3 * CH, lanes] = low
-        if place > 0:
-            change = change + moved_by(change + identity, packed_ref[place, COLS : COLS + 1, :], center)
-
-
-def carry_kernel(first_ref, second_ref, third_ref, local_ref, maps_ref, center_ref, after_ref, upper_ref):
-    center = center_ref[...]
-    carry = third_ref[...]
-    for group_ref in (second_ref, first_ref):
-        for place in range(SIZE_Z - 1, -1, -1):
-            carry = carry + moved_by(carry, group_ref[COLS + place : COLS + place + 1, :], center)
-        carry = carry + group_ref[0:COLS, :]
-    high, low = split(carry)
-    moved = jnp.dot(
-        jnp.concatenate([high, low, high], axis=1), maps_ref[...], preferred_element_type=jnp.float32
-    )
+        local_ref[place] = error
+        stack_parts(maps_ref, change, slice(place * CH, (place + 1) * CH))
+        mean = packed_ref[place, COLS : COLS + 1, :]
+        moved = moved_by(jnp.concatenate([error, change + identity], axis=0), mean, center)
+        error = packed_ref[place, 0:COLS, :] + error + moved[0:COLS]
+        change = change + moved[COLS:]
+    total_ref[0:COLS, :] = error
+    total_ref[COLS:, :] = change
+
+
+def stack_parts(parts_ref, value, lanes):
+    high, low = split(value)
+    parts_ref[0:CH, lanes] = high
+    parts_ref[CH : 2 * CH, lanes] = high
+    parts_ref[2 * CH : 3 * CH, lanes] = low
+
+
+def times(value, parts):
+    high, low = split(value)
+    return jnp.dot(jnp.concatenate([high, low, high], axis=1), parts, preferred_element_type=jnp.float32)
+
+
+def carry_kernel(place_ref, first_ref, second_ref, third_ref, local_ref, maps_ref, after_ref, upper_ref, parts):
+    place_y = place_ref[0]
+    carry = jnp.where(place_y < SIZE_Y - 3, third_ref[...], 0.0)
+    for distance, group_ref in ((2, second_ref), (1, first_ref)):
+        stack_parts(parts.at[distance - 1], group_ref[COLS:, :], slice(0, CH))
+        carry = carry + times(carry, parts[distance - 1])
+        carry = carry + jnp.where(place_y < SIZE_Y - distance, group_ref[0:COLS, :], 0.0)
+    moved = times(carry, maps_ref[...])
     for place in range(SIZE_Z):
         upper_ref[place] = local_ref[place] + carry + moved[:, place * CH : (place + 1) * CH]
 
@@ -255,8 +262,8 @@
         copy.wait()
 
 
-def passed_down(value, axes, count, distance):
-    return lax.ppermute(value, axes, [(i + distance, i) for i in range(count - distance)])
+def ring_down(value, axis, count, distance):
+    return lax.ppermute(value, axis, [((i + distance) % count, i) for i in range(count)])
 
 
 def local(checkpoints, conv_weight, conv_bias, point_guess, terminal):
@@ -265,9 +272,10 @@
     own = point_guess.reshape(PIX, CH)
     terminal = terminal.reshape(PIX, CH)
     kernel = conv_weight.reshape(TAPS, CH)
+    place_y = lax.axis_index("y").astype(jnp.int32).reshape(1)
     final = (lax.axis_index(("y", "z")) == slices - 1).astype(jnp.int32).reshape(1)
     core = lax.axis_index("core").astype(jnp.int32).reshape(1)
-    upper = passed_down(own, ("y", "z"), slices, 1)
+    upper = lax.ppermute(own, ("y", "z"), [(i + 1, i) for i in range(slices - 1)])
 
     def bound(function):
         def kernel_of(*refs):
@@ -275,65 +283,53 @@
 
         return kernel_of
 
-    smem = pl.BlockSpec(memory_space=pltpu.SMEM)
-    vmem = pl.BlockSpec(memory_space=pltpu.VMEM)
-    slopes, lowered, flipped, center, mean = pl.pallas_call(
+    slopes, lowered, flipped, center, mean = call(
         bound(forward_kernel),
-        out_shape=[f32(STEPS_DEV, PIX, CH), bf16(STEPS_DEV, PADDED, WIDE), bf16(TAPS, CH), bf16(2 * CH, CH), f32(8, CH)],
-        in_specs=[smem] + [vmem] * 3,
-        out_specs=[vmem] * 5,
-        compiler_params=pltpu.CompilerParams(vmem_limit_bytes=LIMIT),
-    )(core, checkpoints.reshape(PIX, CH), kernel, conv_bias.reshape(1, CH))
-    own_here, terminal_here = call(load_kernel, [f32(PIX, CH)] * 2)(own, terminal, mean)
-
-    packed, chosen = pl.pallas_call(
-        bound(relax_kernel),
-        out_shape=[f32(ROWS, SLOT, CH), f32(PIX, CH)],
-        in_specs=[smem] + [vmem] * 6,
-        out_specs=[vmem] * 2,
-        scratch_shapes=[pltpu.VMEM((PADDED, WIDE), jnp.bfloat16)],
-        compiler_params=pltpu.CompilerParams(vmem_limit_bytes=LIMIT),
-    )(final, upper, terminal_here, own_here, slopes, flipped, mean)
+        [f32(STEPS_DEV, PIX, CH), bf16(STEPS_DEV, PADDED, WIDE), bf16(TAPS, CH), bf16(2 * CH, CH), f32(8, CH)],
+        1.5,
+        "sssvvv",
+    )(core, place_y, final, checkpoints.reshape(PIX, CH), kernel, conv_bias.reshape(1, CH))
+
+    wide = pltpu.VMEM((PADDED, WIDE), jnp.bfloat16)
+    packed, chosen = call(
+        bound(relax_kernel), [f32(ROWS, SLOT, CH), f32(PIX, CH)], 1.4, "svvvvvv", [wide]
+    )(final, upper, terminal, own, slopes, flipped, mean)
 
     gathered = lax.all_to_all(packed, "z", 0, 0)
-    in_group, total = call(group_kernel, [f32(SIZE_Z, COLS, CH), f32(SLOT, CH)])(gathered, center)
-    first = passed_down(total, "y", SIZE_Y, 1)
-    second = passed_down(total, "y", SIZE_Y, 2)
-    third = passed_down(total[0:COLS], "y", SIZE_Y, 3)
-    maps = call(maps_kernel, bf16(3 * CH, SIZE_Z * CH))(gathered, center, total)
-    turned = call(turn_kernel, bf16(TAPS, STEPS_DEV * PIX))(lowered, total)
-    upper_error = pl.pallas_call(
-        carry_kernel,
-        out_shape=f32(SIZE_Z, COLS, CH),
-        in_specs=[vmem] * 6 + [pl.BlockSpec(memory_space=pl.ANY)],
-        out_specs=vmem,
-        compiler_params=pltpu.CompilerParams(vmem_limit_bytes=LIMIT),
-    )(first, second, third, in_group, maps, center, turned)
+    in_group, maps, total = call(
+        group_kernel, [f32(SIZE_Z, COLS, CH), bf16(3 * CH, SIZE_Z * CH), f32(COLS + CH, CH)], 1.0
+    )(gathered, center)
+    first = ring_down(total, "y", SIZE_Y, 1)
+    third = ring_down(total[0:COLS], "y", SIZE_Y, 3)
+    second = ring_down(total, "y", SIZE_Y, 2)
+    turned = call(turn_kernel, bf16(TAPS, STEPS_DEV * PIX), 0.7)(lowered, total)
+    upper_error = call(
+        carry_kernel, f32(SIZE_Z, COLS, CH), 1.0, "svvvvva", [pltpu.VMEM((2, 3 * CH, CH), jnp.bfloat16)]
+    )(place_y, first, second, third, in_group, maps, turned)
     upper_error = lax.all_to_all(upper_error, "z", 0, 0).reshape(PIX, CH)
 
-    kept, sent = pl.pallas_call(
+    kept, sent = call(
         bound(second_kernel),
-        out_shape=[f32(PLANE, CHUNK, CH)] * 2,
-        in_specs=[smem] + [vmem] * 5,
-        out_specs=[vmem] * 2,
-        scratch_shapes=[pltpu.VMEM((PADDED, WIDE), jnp.bfloat16), pltpu.VMEM((TAPS, CH), jnp.float32)],
-        compiler_params=pltpu.CompilerParams(vmem_limit_bytes=LIMIT),
+        [f32(PLANE, CHUNK, CH)] * 2,
+        1.7,
+        "svvvvv",
+        [wide, pltpu.VMEM((TAPS, CH), jnp.float32)],
     )(core, chosen, upper_error, slopes, turned, flipped)
 
     received = lax.ppermute(sent, "core", [(0, 1), (1, 0)])
-    points = call(points_kernel, f32(PIX, CH))(own_here, packed, upper_error, mean, center)
-    half = call(add_kernel, f32(PLANE, CHUNK, CH))(kept, received)
+    points = call(points_kernel, f32(PIX, CH), 0.8)(own, packed, upper_error, mean, center)
+    half = call(add_kernel, f32(PLANE, CHUNK, CH), 0.1)(kept, received)
     parts = lax.all_to_all(half, ("y", "x"), 0, 0)
-    copies = call(sum_kernel, f32(SIZE_Z, CHUNK, CH))(parts)
+    copies = call(sum_kernel, f32(SIZE_Z, CHUNK, CH), 0.1)(parts)
     parts = lax.all_to_all(copies, "z", 0, 0)
-    copies = call(sum_kernel, f32(PLANE, CHUNK, CH))(parts)
+    copies = call(sum_kernel, f32(PLANE, CHUNK, CH), 0.1)(parts)
     parts = lax.all_to_all(copies, ("y", "x"), 0, 0)
-    half = call(compact_kernel, f32(HALF, CH))(parts)
+    half = call(compact_kernel, f32(HALF, CH), 0.1)(parts)
     other = lax.ppermute(half, "core", [(0, 1), (1, 0)])
     grad_w = pl.pallas_call(
         join_kernel,
         out_shape=f32(TAPS, CH),
-        in_specs=[smem, vmem, vmem],
+        in_specs=[pl.BlockSpec(memory_space=pltpu.SMEM)] + [pl.BlockSpec(memory_space=pltpu.VMEM)] * 2,
         out_specs=pl.BlockSpec(memory_space=pl.ANY),
         scratch_shapes=[pltpu.SemaphoreType.DMA((2,))],
         compiler_params=pltpu.CompilerParams(vmem_limit_bytes=LIMIT),

time: 99.6 us -> 95.4 us (0.958)
  Pallas kernels: 11.2 us -> 8.65 us
  local copies, waits for them, and re-layouts: 4.25 us -> 2.46 us
    pallas_call x14 -> x12, Pallas kernels: 11.2 us -> 8.65 us  [the longest x11 7.83 us: run(): pl.pallas_call(kernel, out_shape=outs, in_specs=[places[kind] for kind in...]
    unnamed x10, local copies, waits for them, and re-layouts: 4.25 us -> 2.46 us
  transfers between devices with their start and end apart: 6 -> 6, of which waited for: 3 -> 4; matrix products, arithmetic and copies ran while one was open for 0% -> 0% of each run, Pallas kernels for 4% -> 3%
where the time goes in v3:
time: 95.4 us; the launch traced here: 95 us
  blocking collectives  62.4 us (65%)
  starting transfers between devices  15 us (16%)
  Pallas kernels  8.65 us (9%)
  waiting for transfers between devices  5.76 us (6%)
  local copies, waits for them, and re-layouts  2.46 us (3%)
    all_to_all x1, blocking collectives, local(): gathered = lax.all_to_all(packed, 'z', 0, 0)  17.4 us
    all_to_all x1, blocking collectives, local(): parts = lax.all_to_all(half, ('y', 'x'), 0, 0)  13.3 us
    all_to_all x1, blocking collectives, local(): parts = lax.all_to_all(copies, 'z', 0, 0)  10.8 us
    all_to_all x1, blocking collectives, local(): parts = lax.all_to_all(copies, ('y', 'x'), 0, 0)  10.6 us
    all_to_all x1, blocking collectives, local(): upper_error = lax.all_to_all(upper_error, 'z', 0, 0).reshape(PIX, CH)  10.3 us
    pallas_call x11, Pallas kernels, run(): pl.pallas_call(kernel, out_shape=outs, in_specs=[places[kind] for kind in...  7.83 us
    ppermute x1, starting transfers between devices, local(): received = lax.ppermute(sent, 'core', [(0, 1), (1, 0)])  5.86 us
    ppermute x1, starting transfers between devices, local(): other = lax.ppermute(half, 'core', [(0, 1), (1, 0)])  3.99 us
  transfers between devices with their start and end apart: 6, of which 4 were waited for; matrix products, arithmetic and copies ran while one was open for 0% of the time, Pallas kernels for 3%

profile of v3, /device:TPU:1, one launch (start us, length us, event | category | flops | bytes accessed | tf_op | source)
XLA Modules:
  0.0 95.0 jit_solution(13556091598133185400)
XLA Ops:
  0.6 1.3 %collective-permute-start = (f32[256,128]{1,0:T(8,128)}, f32[256,128]{1,0:T(8,128)S(1)}, u32[]{:S(2)}, u32[]{:S(2)}) collective-permute-start(f32[256,128]{1,0:T(8,128)} %bitcast.15), channel_id=1, source_target_pairs={{8,0},{16,8},{24,16},{32,24},{40,32},{48,40},{56,48},{64,56},{72,6... | collective-permute-start | bytes 393224 | tf_op jit(solution)/shard_map/ppermute | solution.py:278
  1.9 0.0 copy-start
  2.0 1.0 %copy-done = bf16[3,3,128,128]{3,2,1,0:T(8,128)(2,1)S(1)} copy-done((bf16[3,3,128,128]{3,2,1,0:T(8,128)(2,1)S(1)}, bf16[3,3,128,128]{3,2,1,0:T(8,128)(2,1)}, u32[]{:S(2)}) %copy-start) | copy-done | bytes 294936
  2.9 0.0 copy-start.3
  2.9 0.8 copy-done.3
  3.7 0.7 copy-done.4
  4.4 1.5 %shard_map.68 = (f32[4,256,128]{2,1,0:T(8,128)S(1)}, bf16[4,320,384]{2,1,0:T(8,128)(2,1)S(1)}, bf16[1152,128]{1,0:T(8,128)(2,1)S(1)}, bf16[256,128]{1,0:T(8,128)(2,1)S(1)}, f32[8,128]{1,0:T(8,128)S(1)}) custom-call(s32[1]{0:T(128)} %bitcast.3.refs_0_.core_ref, s32[1]{0:T(128)} %bitcast.4.refs_1_.place_ref, s32[1]{0:T(128)} %bitcast.1.refs_2_.refs_0_, ...), custom_call_target="tpu_custom_call" | custom-call | flops 1500000000 | bytes 5400000 | tf_op jit(solution)/shard_map/pallas_call | solution.py:33
  5.9 1.7 %collective-permute-done.refs_1_ = f32[256,128]{1,0:T(8,128)S(1)} collective-permute-done((f32[256,128]{1,0:T(8,128)}, f32[256,128]{1,0:T(8,128)S(1)}, u32[]{:S(2)}, u32[]{:S(2)}) %collective-permute-start) | collective-permute-done | bytes 131104 | tf_op jit(solution)/shard_map/ppermute | solution.py:278
  7.6 0.0 copy-done.1
  7.6 0.0 copy-done.2
  7.6 1.4 %shard_map.69 = (f32[8,40,128]{2,1,0:T(8,128)S(1)}, f32[256,128]{1,0:T(8,128)S(1)}) custom-call(s32[1]{0:T(128)} %bitcast.1.refs_2_.refs_0_, f32[256,128]{1,0:T(8,128)S(1)} %collective-permute-done.refs_1_, f32[256,128]{1,0:T(8,128)S(1)} %bitcast.14, f32[256,128]{1,0:T(8,128)S(1)} %bitcast.16, f32[4,256,128]{2,1,0:T(8,128)S(1)} %get-tuple-element.14.refs_4_.refs_3_, ...), custom_call_target="tpu_custom_call" | custom-call | flops 1400000000 | bytes 5040000 | tf_op jit(solution)/shard_map/pallas_call | solution.py:33
  9.0 17.4 %all_to_all.25.packed_ref = f32[8,40,128]{2,1,0:T(8,128)S(1)} all-to-all(f32[8,40,128]{2,1,0:T(8,128)S(1)} %get-tuple-element.17.packed_ref), channel_id=1, replica_groups=mesh['y'=4,'z'=8,'x'=4,'core'=2] {'z'}, dimensions={0} | all-to-all | bytes 327680 | tf_op jit(solution)/shard_map/all_to_all | solution.py:298
  26.5 1.1 %shard_map.70 = (f32[8,32,128]{2,1,0:T(8,128)S(1)}, bf16[384,1024]{1,0:T(8,128)(2,1)S(1)}, f32[160,128]{1,0:T(8,128)S(1)}) custom-call(f32[8,40,128]{2,1,0:T(8,128)S(1)} %all_to_all.25.packed_ref, bf16[256,128]{1,0:T(8,128)(2,1)S(1)} %get-tuple-element.18.center_ref), custom_call_target="tpu_custom_call" | custom-call | flops 1000000000 | bytes 3600000 | tf_op jit(solution)/shard_map/pallas_call | solution.py:33
  27.5 2.0 %collective-permute-start.1 = (f32[160,128]{1,0:T(8,128)S(1)}, f32[160,128]{1,0:T(8,128)S(1)}, u32[]{:S(2)}, u32[]{:S(2)}) collective-permute-start(f32[160,128]{1,0:T(8,128)S(1)} %get-tuple-element.19.after_ref), channel_id=1, source_target_pairs={{64,0},{128,64},{192,128},{0,192},{65,1},{129,65},{193,129},{1,193... | collective-permute-start | bytes 245768 | tf_op jit(solution)/shard_map/ppermute | solution.py:266
  29.6 1.1 %collective-permute-start.2 = (f32[160,128]{1,0:T(8,128)S(1)}, f32[160,128]{1,0:T(8,128)S(1)}, u32[]{:S(2)}, u32[]{:S(2)}) collective-permute-start(f32[160,128]{1,0:T(8,128)S(1)} %get-tuple-element.19.after_ref), channel_id=1, source_target_pairs={{128,0},{192,64},{0,128},{64,192},{129,1},{193,65},{1,129},{65,193... | collective-permute-start | bytes 245768 | tf_op jit(solution)/shard_map/ppermute | solution.py:266
  30.7 0.7 collective-permute-start.3
  31.4 0.7 shard_map.71.after_ref.refs_4_
  32.1 2.5 %collective-permute-done.3.third_ref = f32[32,128]{1,0:T(8,128)S(1)} collective-permute-done((f32[32,128]{1,0:T(8,128)S(1)}, f32[32,128]{1,0:T(8,128)S(1)}, u32[]{:S(2)}, u32[]{:S(2)}) %collective-permute-start.3) | collective-permute-done | bytes 16416 | tf_op jit(solution)/shard_map/ppermute | solution.py:266
  34.5 0.0 collective-permute-done.1.first_ref
  34.5 0.0 collective-permute-done.2.second_ref
  34.5 0.5 shard_map.72
  35.0 10.3 %all_to_all.26 = f32[8,32,128]{2,1,0:T(8,128)S(1)} all-to-all(f32[8,32,128]{2,1,0:T(8,128)S(1)} %shard_map.72), channel_id=1, replica_groups=mesh['y'=4,'z'=8,'x'=4,'core'=2] {'z'}, dimensions={0} | all-to-all | bytes 262144 | tf_op jit(solution)/shard_map/all_to_all | solution.py:309
  45.3 1.7 %shard_map.74 = (f32[16,40,128]{2,1,0:T(8,128)S(1)}, f32[16,40,128]{2,1,0:T(8,128)S(1)}) custom-call(s32[1]{0:T(128)} %bitcast.3.refs_0_.core_ref, f32[256,128]{1,0:T(8,128)S(1)} %get-tuple-element.23.refs_1_, f32[256,128]{1,0:T(8,128)S(1)} %bitcast.11, f32[4,256,128]{2,1,0:T(8,128)S(1)} %get-tuple-element.14.refs_4_.refs_3_, ...), custom_call_target="tpu_custom_call" | custom-call | flops 1700000000 | bytes 6120000 | tf_op jit(solution)/shard_map/pallas_call | solution.py:33
  47.1 5.9 %collective-permute-start.4 = (f32[16,40,128]{2,1,0:T(8,128)S(1)}, f32[16,40,128]{2,1,0:T(8,128)S(1)}, u32[]{:S(2)}, u32[]{:S(2)}) collective-permute-start(f32[16,40,128]{2,1,0:T(8,128)S(1)} %get-tuple-element.25), channel_id=1, source_target_pairs={{0,1},{1,0},{2,3},{3,2},{4,5},{5,4},{6,7},{7,6},{8,9},{9,8},{10,11... | collective-permute-start | bytes 983048 | tf_op jit(solution)/shard_map/ppermute | solution.py:319
  52.9 1.3 %collective-permute-done.4.right_ref = f32[16,40,128]{2,1,0:T(8,128)S(1)} collective-permute-done((f32[16,40,128]{2,1,0:T(8,128)S(1)}, f32[16,40,128]{2,1,0:T(8,128)S(1)}, u32[]{:S(2)}, u32[]{:S(2)}) %collective-permute-start.4) | collective-permute-done | bytes 327712 | tf_op jit(solution)/shard_map/ppermute | solution.py:319
  54.2 13.3 %all_to_all.27.parts_ref = f32[16,40,128]{2,1,0:T(8,128)S(1)} all-to-all(f32[16,40,128]{2,1,0:T(8,128)S(1)} %shard_map.75), channel_id=1, replica_groups=mesh['y'=4,'z'=8,'x'=4,'core'=2] {'y','x'}, dimensions={0} | all-to-all | bytes 655360 | tf_op jit(solution)/shard_map/all_to_all | solution.py:322
  67.6 10.8 %all_to_all.28.parts_ref = f32[8,40,128]{2,1,0:T(8,128)S(1)} all-to-all(f32[8,40,128]{2,1,0:T(8,128)S(1)} %shard_map.76), channel_id=1, replica_groups=mesh['y'=4,'z'=8,'x'=4,'core'=2] {'z'}, dimensions={0} | all-to-all | bytes 327680 | tf_op jit(solution)/shard_map/all_to_all | solution.py:324
  78.4 10.6 %all_to_all.29.parts_ref = f32[16,40,128]{2,1,0:T(8,128)S(1)} all-to-all(f32[16,40,128]{2,1,0:T(8,128)S(1)} %shard_map.77), channel_id=1, replica_groups=mesh['y'=4,'z'=8,'x'=4,'core'=2] {'y','x'}, dimensions={0} | all-to-all | bytes 655360 | tf_op jit(solution)/shard_map/all_to_all | solution.py:326
  89.0 4.0 %collective-permute-start.5 = (f32[576,128]{1,0:T(8,128)S(1)}, f32[576,128]{1,0:T(8,128)S(1)}, u32[]{:S(2)}, u32[]{:S(2)}) collective-permute-start(f32[576,128]{1,0:T(8,128)S(1)} %shard_map.78.own_ref), channel_id=1, source_target_pairs={{0,1},{1,0},{2,3},{3,2},{4,5},{5,4},{6,7},{7,6},{8,9},{9,8},{10,11... | collective-permute-start | bytes 884744 | tf_op jit(solution)/shard_map/ppermute | solution.py:328
  93.0 0.8 shard_map.73
  93.8 0.4 collective-permute-done.5.other_ref
  94.2 0.8 shard_map.79
  (8 shorter events, 0.1 us)
Async XLA Ops:
  0.6 6.9 %collective-permute-start = (f32[256,128]{1,0:T(8,128)}, f32[256,128]{1,0:T(8,128)S(1)}, u32[]{:S(2)}, u32[]{:S(2)}) collective-permute-start(f32[256,128]{1,0:T(8,128)} %bitcast.15), channel_id=1, source_target_pairs={{8,0},{16,8},{24,16},{32,24},{40,32},{48,40},{56,48},{64,56},{72,6... | collective-permute-start | bytes 393224 | tf_op jit(solution)/shard_map/ppermute | solution.py:278
  1.9 1.0 %copy-start = (bf16[3,3,128,128]{3,2,1,0:T(8,128)(2,1)S(1)}, bf16[3,3,128,128]{3,2,1,0:T(8,128)(2,1)}, u32[]{:S(2)}) copy-start(bf16[3,3,128,128]{3,2,1,0:T(8,128)(2,1)} %param.6) | copy-start | bytes 884740
  2.9 0.8 copy-start.3
  3.7 0.7 copy-start.4
  4.4 3.2 %copy-start.1 = (f32[1,8,32,128]{3,2,1,0:T(8,128)S(1)}, f32[1,8,32,128]{3,2,1,0:T(8,128)}, u32[]{:S(2)}) copy-start(f32[1,8,32,128]{3,2,1,0:T(8,128)} %param.9) | copy-start | bytes 393220
  4.4 3.2 %copy-start.2 = (f32[1,1,8,32,128]{4,3,2,1,0:T(8,128)S(1)}, f32[1,1,8,32,128]{4,3,2,1,0:T(8,128)}, u32[]{:S(2)}) copy-start(f32[1,1,8,32,128]{4,3,2,1,0:T(8,128)} %param.8) | copy-start | bytes 393220
  27.5 7.0 %collective-permute-start.1 = (f32[160,128]{1,0:T(8,128)S(1)}, f32[160,128]{1,0:T(8,128)S(1)}, u32[]{:S(2)}, u32[]{:S(2)}) collective-permute-start(f32[160,128]{1,0:T(8,128)S(1)} %get-tuple-element.19.after_ref), channel_id=1, source_target_pairs={{64,0},{128,64},{192,128},{0,192},{65,1},{129,65},{193,129},{1,193... | collective-permute-start | bytes 245768 | tf_op jit(solution)/shard_map/ppermute | solution.py:266
  29.6 5.0 %collective-permute-start.2 = (f32[160,128]{1,0:T(8,128)S(1)}, f32[160,128]{1,0:T(8,128)S(1)}, u32[]{:S(2)}, u32[]{:S(2)}) collective-permute-start(f32[160,128]{1,0:T(8,128)S(1)} %get-tuple-element.19.after_ref), channel_id=1, source_target_pairs={{128,0},{192,64},{0,128},{64,192},{129,1},{193,65},{1,129},{65,193... | collective-permute-start | bytes 245768 | tf_op jit(solution)/shard_map/ppermute | solution.py:266
  30.7 3.8 %collective-permute-start.3 = (f32[32,128]{1,0:T(8,128)S(1)}, f32[32,128]{1,0:T(8,128)S(1)}, u32[]{:S(2)}, u32[]{:S(2)}) collective-permute-start(f32[32,128]{1,0:T(8,128)S(1)} %slice.3), channel_id=1, source_target_pairs={{192,0},{0,64},{64,128},{128,192},{193,1},{1,65},{65,129},{129,193... | collective-permute-start | bytes 49160 | tf_op jit(solution)/shard_map/ppermute | solution.py:266
  47.1 7.1 %collective-permute-start.4 = (f32[16,40,128]{2,1,0:T(8,128)S(1)}, f32[16,40,128]{2,1,0:T(8,128)S(1)}, u32[]{:S(2)}, u32[]{:S(2)}) collective-permute-start(f32[16,40,128]{2,1,0:T(8,128)S(1)} %get-tuple-element.25), channel_id=1, source_target_pairs={{0,1},{1,0},{2,3},{3,2},{4,5},{5,4},{6,7},{7,6},{8,9},{9,8},{10,11... | collective-permute-start | bytes 983048 | tf_op jit(solution)/shard_map/ppermute | solution.py:319
  89.0 5.2 %collective-permute-start.5 = (f32[576,128]{1,0:T(8,128)S(1)}, f32[576,128]{1,0:T(8,128)S(1)}, u32[]{:S(2)}, u32[]{:S(2)}) collective-permute-start(f32[576,128]{1,0:T(8,128)S(1)} %shard_map.78.own_ref), channel_id=1, source_target_pairs={{0,1},{1,0},{2,3},{3,2},{4,5},{5,4},{6,7},{7,6},{8,9},{9,8},{10,11... | collective-permute-start | bytes 884744 | tf_op jit(solution)/shard_map/ppermute | solution.py:328

commit v4 on v3

--- a/solution.py
+++ b/solution.py
@@ -10,7 +10,6 @@
 COLS = 32
 CH = 128
 PIX = ROWS * COLS
-PADDED = PIX + 2 * COLS
 WIDE = 3 * CH
 TAPS = 9 * CH
 SIZE_Y = 4
@@ -58,30 +57,29 @@
 
 
 def clear_edges(buffer):
-    zeros = jnp.zeros((COLS, WIDE), jnp.bfloat16)
-    buffer[0:COLS, :] = zeros
-    buffer[COLS + PIX : PADDED, :] = zeros
-
-
-def spread(buffer, low, col):
-    wide = low.astype(jnp.float32)
-    before = jnp.where(col > 0, pltpu.roll(wide, 1, 0), 0.0)
-    after = jnp.where(col < COLS - 1, pltpu.roll(wide, PIX - 1, 0), 0.0)
-    buffer[COLS : COLS + PIX, 0:CH] = before.astype(jnp.bfloat16)
-    buffer[COLS : COLS + PIX, CH : 2 * CH] = low
-    buffer[COLS : COLS + PIX, 2 * CH : WIDE] = after.astype(jnp.bfloat16)
-
-
-def convolve(buffer, kernel):
-    total = None
-    for row in range(3):
-        part = jnp.dot(
-            buffer[row * COLS : row * COLS + PIX, :],
-            kernel[row * WIDE : (row + 1) * WIDE, :],
-            preferred_element_type=jnp.float32,
-        )
-        total = part if total is None else total + part
-    return total
+    zeros = jnp.zeros((COLS, CH), jnp.bfloat16)
+    buffer[0:COLS, 0:CH] = zeros
+    buffer[PIX - COLS : PIX, 2 * CH : WIDE] = zeros
+
+
+def spread(buffer, low):
+    buffer[COLS:PIX, 0:CH] = low[0 : PIX - COLS]
+    buffer[:, CH : 2 * CH] = low
+    buffer[0 : PIX - COLS, 2 * CH : WIDE] = low[COLS:PIX]
+
+
+def from_left(value, col):
+    return jnp.where(col > 0, pltpu.roll(value, 1, 0), 0.0)
+
+
+def from_right(value, col):
+    return jnp.where(col < COLS - 1, pltpu.roll(value, PIX - 1, 0), 0.0)
+
+
+def convolve(buffer, kernel, col):
+    taps = jnp.dot(buffer[...], kernel[...], preferred_element_type=jnp.float32)
+    sides = from_left(taps[:, 0:CH], col) + from_right(taps[:, 2 * CH : WIDE], col)
+    return taps[:, CH : 2 * CH] + sides
 
 
 def split(value):
@@ -96,35 +94,40 @@
 
 
 def forward_kernel(
-    step, core_ref, place_ref, final_ref, start_ref, kernel_ref, bias_ref, slope_ref, lowered_ref, flipped_ref, center_ref, mean_ref,
+    step, core_ref, place_ref, final_ref, start_ref, kernel_ref, bias_ref, slope_ref, lowered_ref, flipped_ref,
+    center_ref, mean_ref, weights,
 ):
     col = columns()
     bias = bias_ref[...]
+    for row in range(3):
+        for tap in range(3):
+            begin = (3 * row + tap) * CH
+            weights[row * CH : (row + 1) * CH, tap * CH : (tap + 1) * CH] = kernel_ref[begin : begin + CH, :]
     current = start_ref[...].astype(jnp.float32)
     for section in range(STEPS_DEV):
         buffer = lowered_ref.at[section]
         clear_edges(buffer)
-        spread(buffer, current.astype(jnp.bfloat16), col)
-        tanh_out = jnp.tanh(convolve(buffer, kernel_ref) + bias)
+        spread(buffer, current.astype(jnp.bfloat16))
+        tanh_out = jnp.tanh(convolve(buffer, weights, col) + bias)
         slope = 1.0 - tanh_out * tanh_out
         slope_ref[section] = slope
         if section == 0:
             mean = jnp.sum(slope, axis=0, keepdims=True) * (STEPS_DEV * step / PIX)
             mean_ref[...] = jnp.broadcast_to(mean, (8, CH))
         current = current + step * tanh_out
-    for tap in range(9):
-        block = kernel_ref[(8 - tap) * CH : (9 - tap) * CH, :].astype(jnp.float32)
-        turned = block.T.astype(jnp.bfloat16)
-        flipped_ref[tap * CH : (tap + 1) * CH, :] = turned
-        if tap == 4:
-            center_ref[0:CH, :] = turned
-            center_ref[CH : 2 * CH, :] = turned
-
-
-def adjoint_step(buffer, flipped, slope, value, step, col):
-    low = (slope * value).astype(jnp.bfloat16)
-    spread(buffer, low, col)
-    return low, value + step * convolve(buffer, flipped)
+    for row in range(3):
+        for tap in range(3):
+            begin = (8 - 3 * row - tap) * CH
+            turned = kernel_ref[begin : begin + CH, :].astype(jnp.float32).T.astype(jnp.bfloat16)
+            flipped_ref[row * CH : (row + 1) * CH, tap * CH : (tap + 1) * CH] = turned
+            if row == 1 and tap == 1:
+                center_ref[0:CH, :] = turned
+                center_ref[CH : 2 * CH, :] = turned
+
+
+def adjoint_step(buffer, flipped, low, value, step, col):
+    spread(buffer, low)
+    return value + step * convolve(buffer, flipped, col)
 
 
 def relax_kernel(
@@ -135,7 +138,8 @@
     value = jnp.where(final_ref[0] == 1, terminal_ref[...], upper_ref[...])
     chosen_ref[...] = value
     for section in range(STEPS_DEV - 1, -1, -1):
-        low, value = adjoint_step(buffer, flipped_ref, slope_ref[section], value, step, col)
+        low = (slope_ref[section] * value).astype(jnp.bfloat16)
+        value = adjoint_step(buffer, flipped_ref, low, value, step, col)
     residue = value - own_ref[...]
     for part in range(ROWS):
         packed_ref[part, 0:COLS, :] = residue[part * COLS : (part + 1) * COLS]
@@ -190,12 +194,12 @@
 
 def turn_kernel(lowered_ref, after_ref, turned_ref):
     for section in range(STEPS_DEV):
-        for row in range(3):
-            block = lowered_ref[section, row * COLS : row * COLS + PIX, :].astype(jnp.float32)
-            turned_ref[row * WIDE : (row + 1) * WIDE, section * PIX : (section + 1) * PIX] = block.T.astype(jnp.bfloat16)
-
-
-def points_kernel(own_ref, packed_ref, error_ref, mean_ref, center_ref, points_ref):
+        block = lowered_ref[section].astype(jnp.float32)
+        turned_ref[:, section * PIX : (section + 1) * PIX] = block.T.astype(jnp.bfloat16)
+
+
+def points_kernel(own_ref, packed_ref, error_ref, mean_ref, center_ref, points_ref, mark_ref):
+    mark_ref[...] = mean_ref[...]
     error = error_ref[...]
     moved = moved_by(error, mean_ref[0:1, :], center_ref[...])
     for part in range(ROWS):
@@ -204,29 +208,38 @@
 
 
 def second_kernel(
-    step, core_ref, chosen_ref, error_ref, slope_ref, turned_ref, flipped_ref,
-    kept_ref, sent_ref, buffer, total,
+    step, core_ref, chosen_ref, error_ref, slope_ref, turned_ref, flipped_ref, kept_ref, sent_ref,
+    buffer, grads, total, ordered,
 ):
     col = columns()
     clear_edges(buffer)
     value = chosen_ref[...] + error_ref[...]
     for section in range(STEPS_DEV - 1, -1, -1):
+        low = (slope_ref[section] * value).astype(jnp.bfloat16)
         if section > 0:
-            low, value = adjoint_step(buffer, flipped_ref, slope_ref[section], value, step, col)
-        else:
-            low = (slope_ref[section] * value).astype(jnp.bfloat16)
+            value = adjoint_step(buffer, flipped_ref, low, value, step, col)
+        grad = low.astype(jnp.float32)
+        grads[section, :, 0:CH] = from_right(grad, col).astype(jnp.bfloat16)
+        grads[section, :, CH : 2 * CH] = low
+        grads[section, :, 2 * CH : WIDE] = from_left(grad, col).astype(jnp.bfloat16)
         term = jnp.dot(
-            turned_ref[:, section * PIX : (section + 1) * PIX], low, preferred_element_type=jnp.float32
+            turned_ref[:, section * PIX : (section + 1) * PIX], grads[section], preferred_element_type=jnp.float32
         )
         if section == STEPS_DEV - 1:
             total[...] = term
+        elif section > 0:
+            total[...] += term
         else:
-            total[...] += term
+            for row in range(3):
+                for tap in range(3):
+                    rows, lanes = slice(row * CH, (row + 1) * CH), slice(tap * CH, (tap + 1) * CH)
+                    begin = (3 * row + tap) * CH
+                    ordered[begin : begin + CH, :] = step * (total[rows, lanes] + term[rows, lanes])
     first_core = core_ref[0] == 0
     blank = jnp.zeros((CHUNK - PART, CH), jnp.float32)
     for part in range(PLANE):
-        lower = step * total[part * PART : (part + 1) * PART, :]
-        upper = step * total[HALF + part * PART : HALF + (part + 1) * PART, :]
+        lower = ordered[part * PART : (part + 1) * PART, :]
+        upper = ordered[HALF + part * PART : HALF + (part + 1) * PART, :]
         kept_ref[part, 0:PART, :] = jnp.where(first_core, lower, upper)
         sent_ref[part, 0:PART, :] = jnp.where(first_core, upper, lower)
         kept_ref[part, PART:CHUNK, :] = blank
@@ -238,7 +251,7 @@
         out_ref[part * PART : (part + 1) * PART, :] = parts_ref[part, 0:PART, :]
 
 
-def add_kernel(left_ref, right_ref, out_ref):
+def add_kernel(left_ref, right_ref, after_ref, out_ref):
     out_ref[...] = left_ref[...] + right_ref[...]
 
 
@@ -285,12 +298,13 @@
 
     slopes, lowered, flipped, center, mean = call(
         bound(forward_kernel),
-        [f32(STEPS_DEV, PIX, CH), bf16(STEPS_DEV, PADDED, WIDE), bf16(TAPS, CH), bf16(2 * CH, CH), f32(8, CH)],
+        [f32(STEPS_DEV, PIX, CH), bf16(STEPS_DEV, PIX, WIDE), bf16(WIDE, WIDE), bf16(2 * CH, CH), f32(8, CH)],
         1.5,
         "sssvvv",
+        [pltpu.VMEM((WIDE, WIDE), jnp.bfloat16)],
     )(core, place_y, final, checkpoints.reshape(PIX, CH), kernel, conv_bias.reshape(1, CH))
 
-    wide = pltpu.VMEM((PADDED, WIDE), jnp.bfloat16)
+    wide = pltpu.VMEM((PIX, WIDE), jnp.bfloat16)
     packed, chosen = call(
         bound(relax_kernel), [f32(ROWS, SLOT, CH), f32(PIX, CH)], 1.4, "svvvvvv", [wide]
     )(final, upper, terminal, own, slopes, flipped, mean)
@@ -302,7 +316,7 @@
     first = ring_down(total, "y", SIZE_Y, 1)
     third = ring_down(total[0:COLS], "y", SIZE_Y, 3)
     second = ring_down(total, "y", SIZE_Y, 2)
-    turned = call(turn_kernel, bf16(TAPS, STEPS_DEV * PIX), 0.7)(lowered, total)
+    turned = call(turn_kernel, bf16(WIDE, STEPS_DEV * PIX), 0.4)(lowered, total)
     upper_error = call(
         carry_kernel, f32(SIZE_Z, COLS, CH), 1.0, "svvvvva", [pltpu.VMEM((2, 3 * CH, CH), jnp.bfloat16)]
     )(place_y, first, second, third, in_group, maps, turned)
@@ -313,12 +327,17 @@
         [f32(PLANE, CHUNK, CH)] * 2,
         1.7,
         "svvvvv",
-        [wide, pltpu.VMEM((TAPS, CH), jnp.float32)],
+        [
+            wide,
+            pltpu.VMEM((STEPS_DEV, PIX, WIDE), jnp.bfloat16),
+            pltpu.VMEM((WIDE, WIDE), jnp.float32),
+            pltpu.VMEM((TAPS, CH), jnp.float32),
+        ],
     )(core, chosen, upper_error, slopes, turned, flipped)
 
     received = lax.ppermute(sent, "core", [(0, 1), (1, 0)])
-    points = call(points_kernel, f32(PIX, CH), 0.8)(own, packed, upper_error, mean, center)
-    half = call(add_kernel, f32(PLANE, CHUNK, CH), 0.1)(kept, received)
+    points, mark = call(points_kernel, [f32(PIX, CH), f32(8, CH)], 0.8)(own, packed, upper_error, mean, center)
+    half = call(add_kernel, f32(PLANE, CHUNK, CH), 0.1, "vva")(kept, received, mark)
     parts = lax.all_to_all(half, ("y", "x"), 0, 0)
     copies = call(sum_kernel, f32(SIZE_Z, CHUNK, CH), 0.1)(parts)
     parts = lax.all_to_all(copies, "z", 0, 0)

time: 95.4 us -> 94.7 us (level)
  waiting for transfers between devices: 5.76 us -> 7.4 us
  Pallas kernels: 8.65 us -> 7.17 us
    pallas_call x11, Pallas kernels: 7.83 us -> 6.35 us  [run(): pl.pallas_call(kernel, out_shape=outs, in_specs=[places[kind] for kind in...]
    ppermute x3, waiting for transfers between devices: 2.47 us -> 3.83 us  [ring_down(): lax.ppermute(value, axis, [((i + distance) % count, i) for i in range(cou...]
    ppermute x1, starting transfers between devices: 5.86 us -> 4.9 us  [local(): received = lax.ppermute(sent, 'core', [(0, 1), (1, 0)])]
  transfers between devices with their start and end apart: 6 -> 6, of which waited for: 4 -> 4; matrix products, arithmetic and copies ran while one was open for 0% -> 0% of each run, Pallas kernels for 3% -> 2%
where the time goes in v4:
time: 94.7 us; the launch traced here: 94.4 us
  blocking collectives  62 us (65%)
  starting transfers between devices  14.6 us (15%)
  waiting for transfers between devices  7.4 us (8%)
  Pallas kernels  7.17 us (8%)
  local copies, waits for them, and re-layouts  2.46 us (3%)
    all_to_all x1, blocking collectives, local(): gathered = lax.all_to_all(packed, 'z', 0, 0)  17.4 us
    all_to_all x1, blocking collectives, local(): parts = lax.all_to_all(half, ('y', 'x'), 0, 0)  12.9 us
    all_to_all x1, blocking collectives, local(): parts = lax.all_to_all(copies, 'z', 0, 0)  10.8 us
    all_to_all x1, blocking collectives, local(): parts = lax.all_to_all(copies, ('y', 'x'), 0, 0)  10.6 us
    all_to_all x1, blocking collectives, local(): upper_error = lax.all_to_all(upper_error, 'z', 0, 0).reshape(PIX, CH)  10.3 us
    pallas_call x11, Pallas kernels, run(): pl.pallas_call(kernel, out_shape=outs, in_specs=[places[kind] for kind in...  6.35 us
    ppermute x1, starting transfers between devices, local(): received = lax.ppermute(sent, 'core', [(0, 1), (1, 0)])  4.9 us
    ppermute x3, starting transfers between devices, ring_down(): lax.ppermute(value, axis, [((i + distance) % count, i) for i in range(cou...  4.47 us
  transfers between devices with their start and end apart: 6, of which 4 were waited for; matrix products, arithmetic and copies ran while one was open for 0% of the time, Pallas kernels for 2%

profile of v4, /device:TPU:1, one launch (start us, length us, event | category | flops | bytes accessed | tf_op | source)
XLA Modules:
  0.0 94.4 jit_solution(12960970534420664908)
XLA Ops:
  0.6 1.3 %collective-permute-start = (f32[256,128]{1,0:T(8,128)}, f32[256,128]{1,0:T(8,128)S(1)}, u32[]{:S(2)}, u32[]{:S(2)}) collective-permute-start(f32[256,128]{1,0:T(8,128)} %bitcast.15), channel_id=1, source_target_pairs={{8,0},{16,8},{24,16},{32,24},{40,32},{48,40},{56,48},{64,56},{72,6... | collective-permute-start | bytes 393224 | tf_op jit(solution)/shard_map/ppermute | solution.py:291
  1.9 0.0 copy-start.4
  2.0 0.6 copy-done.4
  2.6 0.0 copy-start
  2.6 1.0 %copy-done = bf16[3,3,128,128]{3,2,1,0:T(8,128)(2,1)S(1)} copy-done((bf16[3,3,128,128]{3,2,1,0:T(8,128)(2,1)S(1)}, bf16[3,3,128,128]{3,2,1,0:T(8,128)(2,1)}, u32[]{:S(2)}) %copy-start) | copy-done | bytes 294936
  3.6 0.8 copy-done.3
  4.4 1.2 %shard_map.68 = (f32[4,256,128]{2,1,0:T(8,128)S(1)}, bf16[4,256,384]{2,1,0:T(8,128)(2,1)S(1)}, bf16[384,384]{1,0:T(8,128)(2,1)S(1)}, bf16[256,128]{1,0:T(8,128)(2,1)S(1)}, f32[8,128]{1,0:T(8,128)S(1)}) custom-call(s32[1]{0:T(128)} %bitcast.3.refs_0_.core_ref, s32[1]{0:T(128)} %bitcast.4.refs_1_.place_ref, s32[1]{0:T(128)} %bitcast.1.refs_2_.refs_0_, ...), custom_call_target="tpu_custom_call" | custom-call | flops 1500000000 | bytes 5400000 | tf_op jit(solution)/shard_map/pallas_call | solution.py:32
  5.6 1.9 %collective-permute-done.refs_1_ = f32[256,128]{1,0:T(8,128)S(1)} collective-permute-done((f32[256,128]{1,0:T(8,128)}, f32[256,128]{1,0:T(8,128)S(1)}, u32[]{:S(2)}, u32[]{:S(2)}) %collective-permute-start) | collective-permute-done | bytes 131104 | tf_op jit(solution)/shard_map/ppermute | solution.py:291
  7.6 0.0 copy-done.1
  7.6 0.0 copy-done.2
  7.6 1.1 %shard_map.69 = (f32[8,40,128]{2,1,0:T(8,128)S(1)}, f32[256,128]{1,0:T(8,128)S(1)}) custom-call(s32[1]{0:T(128)} %bitcast.1.refs_2_.refs_0_, f32[256,128]{1,0:T(8,128)S(1)} %collective-permute-done.refs_1_, f32[256,128]{1,0:T(8,128)S(1)} %bitcast.14, f32[256,128]{1,0:T(8,128)S(1)} %bitcast.16, f32[4,256,128]{2,1,0:T(8,128)S(1)} %get-tuple-element.16.refs_4_.refs_3_, ...), custom_call_target="tpu_custom_call" | custom-call | flops 1400000000 | bytes 5040000 | tf_op jit(solution)/shard_map/pallas_call | solution.py:32
  8.7 17.4 %all_to_all.25.packed_ref = f32[8,40,128]{2,1,0:T(8,128)S(1)} all-to-all(f32[8,40,128]{2,1,0:T(8,128)S(1)} %get-tuple-element.19.packed_ref), channel_id=1, replica_groups=mesh['y'=4,'z'=8,'x'=4,'core'=2] {'z'}, dimensions={0} | all-to-all | bytes 327680 | tf_op jit(solution)/shard_map/all_to_all | solution.py:312
  26.2 1.1 %shard_map.70 = (f32[8,32,128]{2,1,0:T(8,128)S(1)}, bf16[384,1024]{1,0:T(8,128)(2,1)S(1)}, f32[160,128]{1,0:T(8,128)S(1)}) custom-call(f32[8,40,128]{2,1,0:T(8,128)S(1)} %all_to_all.25.packed_ref, bf16[256,128]{1,0:T(8,128)(2,1)S(1)} %get-tuple-element.20.center_ref), custom_call_target="tpu_custom_call" | custom-call | flops 1000000000 | bytes 3600000 | tf_op jit(solution)/shard_map/pallas_call | solution.py:32
  27.2 3.0 %collective-permute-start.2 = (f32[160,128]{1,0:T(8,128)S(1)}, f32[160,128]{1,0:T(8,128)S(1)}, u32[]{:S(2)}, u32[]{:S(2)}) collective-permute-start(f32[160,128]{1,0:T(8,128)S(1)} %get-tuple-element.21.after_ref), channel_id=1, source_target_pairs={{128,0},{192,64},{0,128},{64,192},{129,1},{193,65},{1,129},{65,193... | collective-permute-start | bytes 245768 | tf_op jit(solution)/shard_map/ppermute | solution.py:279
  30.2 0.8 collective-permute-start.1
  31.0 0.7 collective-permute-start.3
  31.7 0.3 shard_map.71.after_ref.refs_4_
  32.0 3.8 %collective-permute-done.3.third_ref = f32[32,128]{1,0:T(8,128)S(1)} collective-permute-done((f32[32,128]{1,0:T(8,128)S(1)}, f32[32,128]{1,0:T(8,128)S(1)}, u32[]{:S(2)}, u32[]{:S(2)}) %collective-permute-start.3) | collective-permute-done | bytes 16416 | tf_op jit(solution)/shard_map/ppermute | solution.py:279
  35.8 0.0 collective-permute-done.2.second_ref
  35.8 0.0 collective-permute-done.1.first_ref
  35.8 0.5 shard_map.72
  36.3 10.3 %all_to_all.26 = f32[8,32,128]{2,1,0:T(8,128)S(1)} all-to-all(f32[8,32,128]{2,1,0:T(8,128)S(1)} %shard_map.72), channel_id=1, replica_groups=mesh['y'=4,'z'=8,'x'=4,'core'=2] {'z'}, dimensions={0} | all-to-all | bytes 262144 | tf_op jit(solution)/shard_map/all_to_all | solution.py:323
  46.6 1.2 %shard_map.74 = (f32[16,40,128]{2,1,0:T(8,128)S(1)}, f32[16,40,128]{2,1,0:T(8,128)S(1)}) custom-call(s32[1]{0:T(128)} %bitcast.3.refs_0_.core_ref, f32[256,128]{1,0:T(8,128)S(1)} %get-tuple-element.26.refs_1_, f32[256,128]{1,0:T(8,128)S(1)} %bitcast.11, f32[4,256,128]{2,1,0:T(8,128)S(1)} %get-tuple-element.16.refs_4_.refs_3_, ...), custom_call_target="tpu_custom_call" | custom-call | flops 1700000000 | bytes 6120000 | tf_op jit(solution)/shard_map/pallas_call | solution.py:32
  47.9 4.9 %collective-permute-start.4 = (f32[16,40,128]{2,1,0:T(8,128)S(1)}, f32[16,40,128]{2,1,0:T(8,128)S(1)}, u32[]{:S(2)}, u32[]{:S(2)}) collective-permute-start(f32[16,40,128]{2,1,0:T(8,128)S(1)} %get-tuple-element.28), channel_id=1, source_target_pairs={{0,1},{1,0},{2,3},{3,2},{4,5},{5,4},{6,7},{7,6},{8,9},{9,8},{10,11... | collective-permute-start | bytes 983048 | tf_op jit(solution)/shard_map/ppermute | solution.py:338
  52.7 0.8 shard_map.73
  53.6 0.4 collective-permute-done.4.right_ref
  54.0 12.9 %all_to_all.27.parts_ref = f32[16,40,128]{2,1,0:T(8,128)S(1)} all-to-all(f32[16,40,128]{2,1,0:T(8,128)S(1)} %shard_map.75), channel_id=1, replica_groups=mesh['y'=4,'z'=8,'x'=4,'core'=2] {'y','x'}, dimensions={0} | all-to-all | bytes 655360 | tf_op jit(solution)/shard_map/all_to_all | solution.py:341
  66.9 10.8 %all_to_all.28.parts_ref = f32[8,40,128]{2,1,0:T(8,128)S(1)} all-to-all(f32[8,40,128]{2,1,0:T(8,128)S(1)} %shard_map.76), channel_id=1, replica_groups=mesh['y'=4,'z'=8,'x'=4,'core'=2] {'z'}, dimensions={0} | all-to-all | bytes 327680 | tf_op jit(solution)/shard_map/all_to_all | solution.py:343
  77.7 10.6 %all_to_all.29.parts_ref = f32[16,40,128]{2,1,0:T(8,128)S(1)} all-to-all(f32[16,40,128]{2,1,0:T(8,128)S(1)} %shard_map.77), channel_id=1, replica_groups=mesh['y'=4,'z'=8,'x'=4,'core'=2] {'y','x'}, dimensions={0} | all-to-all | bytes 655360 | tf_op jit(solution)/shard_map/all_to_all | solution.py:345
  88.3 4.0 %collective-permute-start.5 = (f32[576,128]{1,0:T(8,128)S(1)}, f32[576,128]{1,0:T(8,128)S(1)}, u32[]{:S(2)}, u32[]{:S(2)}) collective-permute-start(f32[576,128]{1,0:T(8,128)S(1)} %shard_map.78.own_ref), channel_id=1, source_target_pairs={{0,1},{1,0},{2,3},{3,2},{4,5},{5,4},{6,7},{7,6},{8,9},{9,8},{10,11... | collective-permute-start | bytes 884744 | tf_op jit(solution)/shard_map/ppermute | solution.py:347
  92.3 1.2 %collective-permute-done.5.other_ref = f32[576,128]{1,0:T(8,128)S(1)} collective-permute-done((f32[576,128]{1,0:T(8,128)S(1)}, f32[576,128]{1,0:T(8,128)S(1)}, u32[]{:S(2)}, u32[]{:S(2)}) %collective-permute-start.5) | collective-permute-done | bytes 294944 | tf_op jit(solution)/shard_map/ppermute | solution.py:347
  93.5 0.8 shard_map.79
  (8 shorter events, 0.1 us)
Async XLA Ops:
  0.6 6.9 %collective-permute-start = (f32[256,128]{1,0:T(8,128)}, f32[256,128]{1,0:T(8,128)S(1)}, u32[]{:S(2)}, u32[]{:S(2)}) collective-permute-start(f32[256,128]{1,0:T(8,128)} %bitcast.15), channel_id=1, source_target_pairs={{8,0},{16,8},{24,16},{32,24},{40,32},{48,40},{56,48},{64,56},{72,6... | collective-permute-start | bytes 393224 | tf_op jit(solution)/shard_map/ppermute | solution.py:291
  1.9 0.7 copy-start.4
  2.6 1.0 %copy-start = (bf16[3,3,128,128]{3,2,1,0:T(8,128)(2,1)S(1)}, bf16[3,3,128,128]{3,2,1,0:T(8,128)(2,1)}, u32[]{:S(2)}) copy-start(bf16[3,3,128,128]{3,2,1,0:T(8,128)(2,1)} %param.6) | copy-start | bytes 884740
  3.6 0.8 copy-start.3
  4.4 3.2 %copy-start.1 = (f32[1,8,32,128]{3,2,1,0:T(8,128)S(1)}, f32[1,8,32,128]{3,2,1,0:T(8,128)}, u32[]{:S(2)}) copy-start(f32[1,8,32,128]{3,2,1,0:T(8,128)} %param.9) | copy-start | bytes 393220
  4.4 3.2 %copy-start.2 = (f32[1,1,8,32,128]{4,3,2,1,0:T(8,128)S(1)}, f32[1,1,8,32,128]{4,3,2,1,0:T(8,128)}, u32[]{:S(2)}) copy-start(f32[1,1,8,32,128]{4,3,2,1,0:T(8,128)} %param.8) | copy-start | bytes 393220
  27.2 8.6 %collective-permute-start.2 = (f32[160,128]{1,0:T(8,128)S(1)}, f32[160,128]{1,0:T(8,128)S(1)}, u32[]{:S(2)}, u32[]{:S(2)}) collective-permute-start(f32[160,128]{1,0:T(8,128)S(1)} %get-tuple-element.21.after_ref), channel_id=1, source_target_pairs={{128,0},{192,64},{0,128},{64,192},{129,1},{193,65},{1,129},{65,193... | collective-permute-start | bytes 245768 | tf_op jit(solution)/shard_map/ppermute | solution.py:279
  30.2 5.6 %collective-permute-start.1 = (f32[160,128]{1,0:T(8,128)S(1)}, f32[160,128]{1,0:T(8,128)S(1)}, u32[]{:S(2)}, u32[]{:S(2)}) collective-permute-start(f32[160,128]{1,0:T(8,128)S(1)} %get-tuple-element.21.after_ref), channel_id=1, source_target_pairs={{64,0},{128,64},{192,128},{0,192},{65,1},{129,65},{193,129},{1,193... | collective-permute-start | bytes 245768 | tf_op jit(solution)/shard_map/ppermute | solution.py:279
  31.0 4.8 %collective-permute-start.3 = (f32[32,128]{1,0:T(8,128)S(1)}, f32[32,128]{1,0:T(8,128)S(1)}, u32[]{:S(2)}, u32[]{:S(2)}) collective-permute-start(f32[32,128]{1,0:T(8,128)S(1)} %slice.3), channel_id=1, source_target_pairs={{192,0},{0,64},{64,128},{128,192},{193,1},{1,65},{65,129},{129,193... | collective-permute-start | bytes 49160 | tf_op jit(solution)/shard_map/ppermute | solution.py:279
  47.9 6.2 %collective-permute-start.4 = (f32[16,40,128]{2,1,0:T(8,128)S(1)}, f32[16,40,128]{2,1,0:T(8,128)S(1)}, u32[]{:S(2)}, u32[]{:S(2)}) collective-permute-start(f32[16,40,128]{2,1,0:T(8,128)S(1)} %get-tuple-element.28), channel_id=1, source_target_pairs={{0,1},{1,0},{2,3},{3,2},{4,5},{5,4},{6,7},{7,6},{8,9},{9,8},{10,11... | collective-permute-start | bytes 983048 | tf_op jit(solution)/shard_map/ppermute | solution.py:338
  88.3 5.2 %collective-permute-start.5 = (f32[576,128]{1,0:T(8,128)S(1)}, f32[576,128]{1,0:T(8,128)S(1)}, u32[]{:S(2)}, u32[]{:S(2)}) collective-permute-start(f32[576,128]{1,0:T(8,128)S(1)} %shard_map.78.own_ref), channel_id=1, source_target_pairs={{0,1},{1,0},{2,3},{3,2},{4,5},{5,4},{6,7},{7,6},{8,9},{9,8},{10,11... | collective-permute-start | bytes 884744 | tf_op jit(solution)/shard_map/ppermute | solution.py:347

commit v5 on v4

--- a/solution.py
+++ b/solution.py
@@ -17,7 +17,6 @@
 SIZE_X = 4
 PLANE = SIZE_X * SIZE_Y
 PART = 36
-CHUNK = 40
 HALF = PLANE * PART
 SLOT = COLS + 8
 LIMIT = 12 << 20
@@ -236,19 +235,9 @@
                     begin = (3 * row + tap) * CH
                     ordered[begin : begin + CH, :] = step * (total[rows, lanes] + term[rows, lanes])
     first_core = core_ref[0] == 0
-    blank = jnp.zeros((CHUNK - PART, CH), jnp.float32)
-    for part in range(PLANE):
-        lower = ordered[part * PART : (part + 1) * PART, :]
-        upper = ordered[HALF + part * PART : HALF + (part + 1) * PART, :]
-        kept_ref[part, 0:PART, :] = jnp.where(first_core, lower, upper)
-        sent_ref[part, 0:PART, :] = jnp.where(first_core, upper, lower)
-        kept_ref[part, PART:CHUNK, :] = blank
-        sent_ref[part, PART:CHUNK, :] = blank
-
-
-def compact_kernel(parts_ref, out_ref):
-    for part in range(PLANE):
-        out_ref[part * PART : (part + 1) * PART, :] = parts_ref[part, 0:PART, :]
+    lower, upper = ordered[0:HALF, :], ordered[HALF:TAPS, :]
+    kept_ref[...] = jnp.where(first_core, lower, upper)
+    sent_ref[...] = jnp.where(first_core, upper, lower)
 
 
 def add_kernel(left_ref, right_ref, after_ref, out_ref):
@@ -256,11 +245,11 @@
 
 
 def sum_kernel(parts_ref, out_ref):
-    total = parts_ref[0]
-    for part in range(1, parts_ref.shape[0]):
-        total = total + parts_ref[part]
-    for copy in range(out_ref.shape[0]):
-        out_ref[copy] = total
+    total = parts_ref[0:PART, :]
+    for part in range(1, parts_ref.shape[0] // PART):
+        total = total + parts_ref[part * PART : (part + 1) * PART, :]
+    for copy in range(out_ref.shape[0] // PART):
+        out_ref[copy * PART : (copy + 1) * PART, :] = total
 
 
 def join_kernel(core_ref, own_ref, other_ref, out_ref, sems):
@@ -279,6 +268,11 @@
     return lax.ppermute(value, axis, [((i + distance) % count, i) for i in range(count)])
 
 
+def swapped(rows, axes, count):
+    parts = rows.reshape(count, 1, rows.shape[0] // count * CH)
+    return lax.all_to_all(parts, axes, 0, 0).reshape(rows.shape)
+
+
 def local(checkpoints, conv_weight, conv_bias, point_guess, terminal):
     slices = SIZE_Y * SIZE_Z
     step = 2.0 / (STEPS_DEV * slices)
@@ -288,7 +282,7 @@
     place_y = lax.axis_index("y").astype(jnp.int32).reshape(1)
     final = (lax.axis_index(("y", "z")) == slices - 1).astype(jnp.int32).reshape(1)
     core = lax.axis_index("core").astype(jnp.int32).reshape(1)
-    upper = lax.ppermute(own, ("y", "z"), [(i + 1, i) for i in range(slices - 1)])
+    upper = ring_down(own, ("y", "z"), slices, 1)
 
     def bound(function):
         def kernel_of(*refs):
@@ -324,7 +318,7 @@
 
     kept, sent = call(
         bound(second_kernel),
-        [f32(PLANE, CHUNK, CH)] * 2,
+        [f32(HALF, CH)] * 2,
         1.7,
         "svvvvv",
         [
@@ -337,13 +331,12 @@
 
     received = lax.ppermute(sent, "core", [(0, 1), (1, 0)])
     points, mark = call(points_kernel, [f32(PIX, CH), f32(8, CH)], 0.8)(own, packed, upper_error, mean, center)
-    half = call(add_kernel, f32(PLANE, CHUNK, CH), 0.1, "vva")(kept, received, mark)
-    parts = lax.all_to_all(half, ("y", "x"), 0, 0)
-    copies = call(sum_kernel, f32(SIZE_Z, CHUNK, CH), 0.1)(parts)
-    parts = lax.all_to_all(copies, "z", 0, 0)
-    copies = call(sum_kernel, f32(PLANE, CHUNK, CH), 0.1)(parts)
-    parts = lax.all_to_all(copies, ("y", "x"), 0, 0)
-    half = call(compact_kernel, f32(HALF, CH), 0.1)(parts)
+    half = call(add_kernel, f32(HALF, CH), 0.1, "vva")(kept, received, mark)
+    parts = swapped(half, ("y", "x"), PLANE)
+    copies = call(sum_kernel, f32(SIZE_Z * PART, CH), 0.1)(parts)
+    parts = swapped(copies, "z", SIZE_Z)
+    copies = call(sum_kernel, f32(HALF, CH), 0.1)(parts)
+    half = swapped(copies, ("y", "x"), PLANE)
     other = lax.ppermute(half, "core", [(0, 1), (1, 0)])
     grad_w = pl.pallas_call(
         join_kernel,

time: 94.7 us -> 93 us (0.982)
  starting transfers between devices: 14.6 us -> 21.4 us
  blocking collectives: 62 us -> 55.4 us
  waiting for transfers between devices: 7.4 us -> 5.54 us
    ppermute x3 -> x4, starting transfers between devices: 4.47 us -> 13 us  [ring_down(): lax.ppermute(value, axis, [((i + distance) % count, i) for i in range(cou...]
    all_to_all x1, blocking collectives: 17.4 us -> 10.5 us  [local(): gathered = lax.all_to_all(packed, 'z', 0, 0)]
    ppermute x1 -> x0, waiting for transfers between devices: 1.94 us -> none  [local(): lax.ppermute(own, ('y', 'z'), [(i + 1, i) for i in range(slices - 1)])]
    ppermute x1 -> x0, starting transfers between devices: 1.29 us -> none  [local(): lax.ppermute(own, ('y', 'z'), [(i + 1, i) for i in range(slices - 1)])]
    ppermute x3 -> x4, waiting for transfers between devices: 3.83 us -> 3.95 us  [ring_down(): lax.ppermute(value, axis, [((i + distance) % count, i) for i in range(cou...]
    pallas_call x11 -> x10, Pallas kernels: 6.35 us -> 6.31 us  [run(): pl.pallas_call(kernel, out_shape=outs, in_specs=[places[kind] for kind in...]
  transfers between devices with their start and end apart: 6 -> 6, of which waited for: 4 -> 3; matrix products, arithmetic and copies ran while one was open for 0% -> 0% of each run, Pallas kernels for 2% -> 2%
where the time goes in v5:
time: 93 us; the launch traced here: 92.7 us
  blocking collectives  55.4 us (60%)
  starting transfers between devices  21.4 us (23%)
  Pallas kernels  7.13 us (8%)
  waiting for transfers between devices  5.54 us (6%)
  local copies, waits for them, and re-layouts  2.46 us (3%)
    all_to_all x3, blocking collectives, swapped(): return lax.all_to_all(parts, axes, 0, 0).reshape(rows.shape)  34.5 us
    ppermute x4, starting transfers between devices, ring_down(): lax.ppermute(value, axis, [((i + distance) % count, i) for i in range(cou...  13 us
    all_to_all x1, blocking collectives, local(): gathered = lax.all_to_all(packed, 'z', 0, 0)  10.5 us
    all_to_all x1, blocking collectives, local(): upper_error = lax.all_to_all(upper_error, 'z', 0, 0).reshape(PIX, CH)  10.4 us
    pallas_call x10, Pallas kernels, run(): pl.pallas_call(kernel, out_shape=outs, in_specs=[places[kind] for kind in...  6.31 us
    ppermute x1, starting transfers between devices, local(): received = lax.ppermute(sent, 'core', [(0, 1), (1, 0)])  4.6 us
    ppermute x4, waiting for transfers between devices, ring_down(): lax.ppermute(value, axis, [((i + distance) % count, i) for i in range(cou...  3.95 us
    ppermute x1, starting transfers between devices, local(): other = lax.ppermute(half, 'core', [(0, 1), (1, 0)])  3.79 us
  transfers between devices with their start and end apart: 6, of which 3 were waited for; matrix products, arithmetic and copies ran while one was open for 0% of the time, Pallas kernels for 2%

profile of v5, /device:TPU:1, one launch (start us, length us, event | category | flops | bytes accessed | tf_op | source)
XLA Modules:
  0.0 92.7 jit_solution(17522378000726407551)
XLA Ops:
  0.6 8.9 %collective-permute-start = (f32[256,128]{1,0:T(8,128)}, f32[256,128]{1,0:T(8,128)S(1)}, u32[]{:S(2)}, u32[]{:S(2)}) collective-permute-start(f32[256,128]{1,0:T(8,128)} %bitcast.28), channel_id=1, source_target_pairs={{8,0},{16,8},{24,16},{32,24},{40,32},{48,40},{56,48},{64,56},{72,6... | collective-permute-start | bytes 393224 | tf_op jit(solution)/shard_map/ppermute | solution.py:268
  9.6 0.0 copy-start.4
  9.6 0.7 copy-done.4
  10.2 0.0 copy-start
  10.2 1.0 %copy-done = bf16[3,3,128,128]{3,2,1,0:T(8,128)(2,1)S(1)} copy-done((bf16[3,3,128,128]{3,2,1,0:T(8,128)(2,1)S(1)}, bf16[3,3,128,128]{3,2,1,0:T(8,128)(2,1)}, u32[]{:S(2)}) %copy-start) | copy-done | bytes 294936
  11.2 0.8 copy-done.3
  12.0 1.2 %shard_map.68 = (f32[4,256,128]{2,1,0:T(8,128)S(1)}, bf16[4,256,384]{2,1,0:T(8,128)(2,1)S(1)}, bf16[384,384]{1,0:T(8,128)(2,1)S(1)}, bf16[256,128]{1,0:T(8,128)(2,1)S(1)}, f32[8,128]{1,0:T(8,128)S(1)}) custom-call(s32[1]{0:T(128)} %bitcast.3.refs_0_.core_ref, s32[1]{0:T(128)} %bitcast.4.refs_1_.place_ref, s32[1]{0:T(128)} %bitcast.1.refs_2_.refs_0_, ...), custom_call_target="tpu_custom_call" | custom-call | flops 1500000000 | bytes 5400000 | tf_op jit(solution)/shard_map/pallas_call | solution.py:31
  13.2 0.0 collective-permute-done.refs_1_
  13.3 0.0 copy-done.1
  13.3 0.0 copy-done.2
  13.3 1.2 %shard_map.69 = (f32[8,40,128]{2,1,0:T(8,128)S(1)}, f32[256,128]{1,0:T(8,128)S(1)}) custom-call(s32[1]{0:T(128)} %bitcast.1.refs_2_.refs_0_, f32[256,128]{1,0:T(8,128)S(1)} %collective-permute-done.refs_1_, f32[256,128]{1,0:T(8,128)S(1)} %bitcast.27, f32[256,128]{1,0:T(8,128)S(1)} %bitcast.29, f32[4,256,128]{2,1,0:T(8,128)S(1)} %get-tuple-element.16.refs_4_.refs_3_, ...), custom_call_target="tpu_custom_call" | custom-call | flops 1400000000 | bytes 5040000 | tf_op jit(solution)/shard_map/pallas_call | solution.py:31
  14.4 10.5 %all_to_all.25.packed_ref = f32[8,40,128]{2,1,0:T(8,128)S(1)} all-to-all(f32[8,40,128]{2,1,0:T(8,128)S(1)} %get-tuple-element.19.packed_ref), channel_id=1, replica_groups=mesh['y'=4,'z'=8,'x'=4,'core'=2] {'z'}, dimensions={0} | all-to-all | bytes 327680 | tf_op jit(solution)/shard_map/all_to_all | solution.py:306
  24.9 1.1 %shard_map.70 = (f32[8,32,128]{2,1,0:T(8,128)S(1)}, bf16[384,1024]{1,0:T(8,128)(2,1)S(1)}, f32[160,128]{1,0:T(8,128)S(1)}) custom-call(f32[8,40,128]{2,1,0:T(8,128)S(1)} %all_to_all.25.packed_ref, bf16[256,128]{1,0:T(8,128)(2,1)S(1)} %get-tuple-element.20.center_ref), custom_call_target="tpu_custom_call" | custom-call | flops 1000000000 | bytes 3600000 | tf_op jit(solution)/shard_map/pallas_call | solution.py:31
  26.0 2.4 %collective-permute-start.2 = (f32[160,128]{1,0:T(8,128)S(1)}, f32[160,128]{1,0:T(8,128)S(1)}, u32[]{:S(2)}, u32[]{:S(2)}) collective-permute-start(f32[160,128]{1,0:T(8,128)S(1)} %get-tuple-element.21.after_ref), channel_id=1, source_target_pairs={{128,0},{192,64},{0,128},{64,192},{129,1},{193,65},{1,129},{65,193... | collective-permute-start | bytes 245768 | tf_op jit(solution)/shard_map/ppermute | solution.py:268
  28.4 1.1 %collective-permute-start.1 = (f32[160,128]{1,0:T(8,128)S(1)}, f32[160,128]{1,0:T(8,128)S(1)}, u32[]{:S(2)}, u32[]{:S(2)}) collective-permute-start(f32[160,128]{1,0:T(8,128)S(1)} %get-tuple-element.21.after_ref), channel_id=1, source_target_pairs={{64,0},{128,64},{192,128},{0,192},{65,1},{129,65},{193,129},{1,193... | collective-permute-start | bytes 245768 | tf_op jit(solution)/shard_map/ppermute | solution.py:268
  29.5 0.5 collective-permute-start.3
  30.0 0.3 shard_map.71.after_ref.refs_4_
  30.3 3.9 %collective-permute-done.3.third_ref = f32[32,128]{1,0:T(8,128)S(1)} collective-permute-done((f32[32,128]{1,0:T(8,128)S(1)}, f32[32,128]{1,0:T(8,128)S(1)}, u32[]{:S(2)}, u32[]{:S(2)}) %collective-permute-start.3) | collective-permute-done | bytes 16416 | tf_op jit(solution)/shard_map/ppermute | solution.py:268
  34.2 0.0 collective-permute-done.2.second_ref
  34.2 0.0 collective-permute-done.1.first_ref
  34.3 0.5 shard_map.72
  34.7 10.4 %all_to_all.26 = f32[8,32,128]{2,1,0:T(8,128)S(1)} all-to-all(f32[8,32,128]{2,1,0:T(8,128)S(1)} %shard_map.72), channel_id=1, replica_groups=mesh['y'=4,'z'=8,'x'=4,'core'=2] {'z'}, dimensions={0} | all-to-all | bytes 262144 | tf_op jit(solution)/shard_map/all_to_all | solution.py:317
  45.2 1.2 %shard_map.74 = (f32[576,128]{1,0:T(8,128)S(1)}, f32[576,128]{1,0:T(8,128)S(1)}) custom-call(s32[1]{0:T(128)} %bitcast.3.refs_0_.core_ref, f32[256,128]{1,0:T(8,128)S(1)} %get-tuple-element.26.refs_1_, f32[256,128]{1,0:T(8,128)S(1)} %bitcast.24, f32[4,256,128]{2,1,0:T(8,128)S(1)} %get-tuple-element.16.refs_4_.refs_3_, ...), custom_call_target="tpu_custom_call" | custom-call | flops 1700000000 | bytes 6120000 | tf_op jit(solution)/shard_map/pallas_call | solution.py:31
  46.4 4.6 %collective-permute-start.4 = (f32[576,128]{1,0:T(8,128)S(1)}, f32[576,128]{1,0:T(8,128)S(1)}, u32[]{:S(2)}, u32[]{:S(2)}) collective-permute-start(f32[576,128]{1,0:T(8,128)S(1)} %get-tuple-element.28), channel_id=1, source_target_pairs={{0,1},{1,0},{2,3},{3,2},{4,5},{5,4},{6,7},{7,6},{8,9},{9,8},{10,11... | collective-permute-start | bytes 884744 | tf_op jit(solution)/shard_map/ppermute | solution.py:332
  51.0 0.8 shard_map.73
  51.8 0.4 collective-permute-done.4.right_ref
  52.2 13.4 %all_to_all.27 = f32[16,1,4608]{2,1,0:T(1,128)S(1)} all-to-all(f32[16,1,4608]{2,1,0:T(1,128)S(1)} %bitcast.17), channel_id=1, replica_groups=mesh['y'=4,'z'=8,'x'=4,'core'=2] {'y','x'}, dimensions={0} | all-to-all | bytes 589824 | tf_op jit(solution)/shard_map/all_to_all | solution.py:273
  65.7 10.6 %all_to_all.28 = f32[8,1,4608]{2,1,0:T(1,128)S(1)} all-to-all(f32[8,1,4608]{2,1,0:T(1,128)S(1)} %bitcast.22), channel_id=1, replica_groups=mesh['y'=4,'z'=8,'x'=4,'core'=2] {'z'}, dimensions={0} | all-to-all | bytes 294912 | tf_op jit(solution)/shard_map/all_to_all | solution.py:273
  76.3 10.5 %all_to_all.29 = f32[16,1,4608]{2,1,0:T(1,128)S(1)} all-to-all(f32[16,1,4608]{2,1,0:T(1,128)S(1)} %bitcast.19), channel_id=1, replica_groups=mesh['y'=4,'z'=8,'x'=4,'core'=2] {'y','x'}, dimensions={0} | all-to-all | bytes 589824 | tf_op jit(solution)/shard_map/all_to_all | solution.py:273
  86.8 3.8 %collective-permute-start.5 = (f32[576,128]{1,0:T(8,128)S(1)}, f32[576,128]{1,0:T(8,128)S(1)}, u32[]{:S(2)}, u32[]{:S(2)}) collective-permute-start(f32[576,128]{1,0:T(8,128)S(1)} %bitcast.20), channel_id=1, source_target_pairs={{0,1},{1,0},{2,3},{3,2},{4,5},{5,4},{6,7},{7,6},{8,9},{9,8},{10,11... | collective-permute-start | bytes 884744 | tf_op jit(solution)/shard_map/ppermute | solution.py:340
  90.6 1.2 %collective-permute-done.5.other_ref = f32[576,128]{1,0:T(8,128)S(1)} collective-permute-done((f32[576,128]{1,0:T(8,128)S(1)}, f32[576,128]{1,0:T(8,128)S(1)}, u32[]{:S(2)}, u32[]{:S(2)}) %collective-permute-start.5) | collective-permute-done | bytes 294944 | tf_op jit(solution)/shard_map/ppermute | solution.py:340
  91.8 0.8 shard_map.78
  (7 shorter events, 0.1 us)
Async XLA Ops:
  0.6 12.6 %collective-permute-start = (f32[256,128]{1,0:T(8,128)}, f32[256,128]{1,0:T(8,128)S(1)}, u32[]{:S(2)}, u32[]{:S(2)}) collective-permute-start(f32[256,128]{1,0:T(8,128)} %bitcast.28), channel_id=1, source_target_pairs={{8,0},{16,8},{24,16},{32,24},{40,32},{48,40},{56,48},{64,56},{72,6... | collective-permute-start | bytes 393224 | tf_op jit(solution)/shard_map/ppermute | solution.py:268
  9.6 0.7 copy-start.4
  10.2 1.0 %copy-start = (bf16[3,3,128,128]{3,2,1,0:T(8,128)(2,1)S(1)}, bf16[3,3,128,128]{3,2,1,0:T(8,128)(2,1)}, u32[]{:S(2)}) copy-start(bf16[3,3,128,128]{3,2,1,0:T(8,128)(2,1)} %param.6) | copy-start | bytes 884740
  11.2 0.8 copy-start.3
  12.0 1.2 %copy-start.1 = (f32[1,8,32,128]{3,2,1,0:T(8,128)S(1)}, f32[1,8,32,128]{3,2,1,0:T(8,128)}, u32[]{:S(2)}) copy-start(f32[1,8,32,128]{3,2,1,0:T(8,128)} %param.9) | copy-start | bytes 393220
  12.0 1.2 %copy-start.2 = (f32[1,1,8,32,128]{4,3,2,1,0:T(8,128)S(1)}, f32[1,1,8,32,128]{4,3,2,1,0:T(8,128)}, u32[]{:S(2)}) copy-start(f32[1,1,8,32,128]{4,3,2,1,0:T(8,128)} %param.8) | copy-start | bytes 393220
  26.0 8.3 %collective-permute-start.2 = (f32[160,128]{1,0:T(8,128)S(1)}, f32[160,128]{1,0:T(8,128)S(1)}, u32[]{:S(2)}, u32[]{:S(2)}) collective-permute-start(f32[160,128]{1,0:T(8,128)S(1)} %get-tuple-element.21.after_ref), channel_id=1, source_target_pairs={{128,0},{192,64},{0,128},{64,192},{129,1},{193,65},{1,129},{65,193... | collective-permute-start | bytes 245768 | tf_op jit(solution)/shard_map/ppermute | solution.py:268
  28.4 5.8 %collective-permute-start.1 = (f32[160,128]{1,0:T(8,128)S(1)}, f32[160,128]{1,0:T(8,128)S(1)}, u32[]{:S(2)}, u32[]{:S(2)}) collective-permute-start(f32[160,128]{1,0:T(8,128)S(1)} %get-tuple-element.21.after_ref), channel_id=1, source_target_pairs={{64,0},{128,64},{192,128},{0,192},{65,1},{129,65},{193,129},{1,193... | collective-permute-start | bytes 245768 | tf_op jit(solution)/shard_map/ppermute | solution.py:268
  29.5 4.7 %collective-permute-start.3 = (f32[32,128]{1,0:T(8,128)S(1)}, f32[32,128]{1,0:T(8,128)S(1)}, u32[]{:S(2)}, u32[]{:S(2)}) collective-permute-start(f32[32,128]{1,0:T(8,128)S(1)} %slice.3), channel_id=1, source_target_pairs={{192,0},{0,64},{64,128},{128,192},{193,1},{1,65},{65,129},{129,193... | collective-permute-start | bytes 49160 | tf_op jit(solution)/shard_map/ppermute | solution.py:268
  46.4 5.8 %collective-permute-start.4 = (f32[576,128]{1,0:T(8,128)S(1)}, f32[576,128]{1,0:T(8,128)S(1)}, u32[]{:S(2)}, u32[]{:S(2)}) collective-permute-start(f32[576,128]{1,0:T(8,128)S(1)} %get-tuple-element.28), channel_id=1, source_target_pairs={{0,1},{1,0},{2,3},{3,2},{4,5},{5,4},{6,7},{7,6},{8,9},{9,8},{10,11... | collective-permute-start | bytes 884744 | tf_op jit(solution)/shard_map/ppermute | solution.py:332
  86.8 5.0 %collective-permute-start.5 = (f32[576,128]{1,0:T(8,128)S(1)}, f32[576,128]{1,0:T(8,128)S(1)}, u32[]{:S(2)}, u32[]{:S(2)}) collective-permute-start(f32[576,128]{1,0:T(8,128)S(1)} %bitcast.20), channel_id=1, source_target_pairs={{0,1},{1,0},{2,3},{3,2},{4,5},{5,4},{6,7},{7,6},{8,9},{9,8},{10,11... | collective-permute-start | bytes 884744 | tf_op jit(solution)/shard_map/ppermute | solution.py:340

commit v6 on v5

--- a/solution.py
+++ b/solution.py
@@ -18,7 +18,9 @@
 PLANE = SIZE_X * SIZE_Y
 PART = 36
 HALF = PLANE * PART
-SLOT = COLS + 8
+SLICES = SIZE_Y * SIZE_Z
+SHARE = PIX // SLICES
+SLOT = SHARE + 1
 LIMIT = 12 << 20
 
 
@@ -93,8 +95,8 @@
 
 
 def forward_kernel(
-    step, core_ref, place_ref, final_ref, start_ref, kernel_ref, bias_ref, slope_ref, lowered_ref, flipped_ref,
-    center_ref, mean_ref, weights,
+    step, core_ref, final_ref, start_ref, kernel_ref, bias_ref, slope_ref, turned_ref, flipped_ref,
+    center_ref, mean_ref, weights, lowered,
 ):
     col = columns()
     bias = bias_ref[...]
@@ -104,7 +106,7 @@
             weights[row * CH : (row + 1) * CH, tap * CH : (tap + 1) * CH] = kernel_ref[begin : begin + CH, :]
     current = start_ref[...].astype(jnp.float32)
     for section in range(STEPS_DEV):
-        buffer = lowered_ref.at[section]
+        buffer = lowered.at[section]
         clear_edges(buffer)
         spread(buffer, current.astype(jnp.bfloat16))
         tanh_out = jnp.tanh(convolve(buffer, weights, col) + bias)
@@ -114,6 +116,9 @@
             mean = jnp.sum(slope, axis=0, keepdims=True) * (STEPS_DEV * step / PIX)
             mean_ref[...] = jnp.broadcast_to(mean, (8, CH))
         current = current + step * tanh_out
+    for section in range(STEPS_DEV):
+        block = lowered[section].astype(jnp.float32)
+        turned_ref[:, section * PIX : (section + 1) * PIX] = block.T.astype(jnp.bfloat16)
     for row in range(3):
         for tap in range(3):
             begin = (8 - 3 * row - tap) * CH
@@ -130,7 +135,7 @@
 
 
 def relax_kernel(
-    step, final_ref, upper_ref, terminal_ref, own_ref, slope_ref, flipped_ref, mean_ref, packed_ref, chosen_ref, buffer
+    step, final_ref, upper_ref, terminal_ref, own_ref, slope_ref, flipped_ref, mean_ref, packed_ref, residue_ref, chosen_ref, buffer
 ):
     col = columns()
     clear_edges(buffer)
@@ -140,31 +145,15 @@
         low = (slope_ref[section] * value).astype(jnp.bfloat16)
         value = adjoint_step(buffer, flipped_ref, low, value, step, col)
     residue = value - own_ref[...]
-    for part in range(ROWS):
-        packed_ref[part, 0:COLS, :] = residue[part * COLS : (part + 1) * COLS]
-        packed_ref[part, COLS:SLOT, :] = mean_ref[...]
+    residue_ref[...] = residue
+    mean = mean_ref[0:1, :]
+    for part in range(SLICES):
+        packed_ref[part * SLOT : part * SLOT + SHARE, :] = residue[part * SHARE : (part + 1) * SHARE]
+        packed_ref[part * SLOT + SHARE : (part + 1) * SLOT, :] = mean
 
 
 def moved_by(value, mean, center):
     return exact_left(value * mean, center)
-
-
-def group_kernel(packed_ref, center_ref, local_ref, maps_ref, total_ref):
-    center = center_ref[...]
-    row = lax.broadcasted_iota(jnp.int32, (CH, CH), 0)
-    lane = lax.broadcasted_iota(jnp.int32, (CH, CH), 1)
-    identity = jnp.where(row == lane, 1.0, 0.0)
-    error = jnp.zeros((COLS, CH), jnp.float32)
-    change = jnp.zeros((CH, CH), jnp.float32)
-    for place in range(SIZE_Z - 1, -1, -1):
-        local_ref[place] = error
-        stack_parts(maps_ref, change, slice(place * CH, (place + 1) * CH))
-        mean = packed_ref[place, COLS : COLS + 1, :]
-        moved = moved_by(jnp.concatenate([error, change + identity], axis=0), mean, center)
-        error = packed_ref[place, 0:COLS, :] + error + moved[0:COLS]
-        change = change + moved[COLS:]
-    total_ref[0:COLS, :] = error
-    total_ref[COLS:, :] = change
 
 
 def stack_parts(parts_ref, value, lanes):
@@ -179,31 +168,59 @@
     return jnp.dot(jnp.concatenate([high, low, high], axis=1), parts, preferred_element_type=jnp.float32)
 
 
-def carry_kernel(place_ref, first_ref, second_ref, third_ref, local_ref, maps_ref, after_ref, upper_ref, parts):
-    place_y = place_ref[0]
-    carry = jnp.where(place_y < SIZE_Y - 3, third_ref[...], 0.0)
-    for distance, group_ref in ((2, second_ref), (1, first_ref)):
-        stack_parts(parts.at[distance - 1], group_ref[COLS:, :], slice(0, CH))
-        carry = carry + times(carry, parts[distance - 1])
-        carry = carry + jnp.where(place_y < SIZE_Y - distance, group_ref[0:COLS, :], 0.0)
-    moved = times(carry, maps_ref[...])
-    for place in range(SIZE_Z):
-        upper_ref[place] = local_ref[place] + carry + moved[:, place * CH : (place + 1) * CH]
-
-
-def turn_kernel(lowered_ref, after_ref, turned_ref):
-    for section in range(STEPS_DEV):
-        block = lowered_ref[section].astype(jnp.float32)
-        turned_ref[:, section * PIX : (section + 1) * PIX] = block.T.astype(jnp.bfloat16)
-
-
-def points_kernel(own_ref, packed_ref, error_ref, mean_ref, center_ref, points_ref, mark_ref):
+def scan_kernel(packed_ref, center_ref, upper_ref, parts):
+    center = center_ref[...]
+    row = lax.broadcasted_iota(jnp.int32, (CH, CH), 0)
+    lane = lax.broadcasted_iota(jnp.int32, (CH, CH), 1)
+    identity = jnp.where(row == lane, 1.0, 0.0)
+    middle = range(1, SIZE_Y - 1)
+
+    def residues(place):
+        begins = [(group * SIZE_Z + place) * SLOT for group in range(SIZE_Y)]
+        return jnp.concatenate([packed_ref[begin : begin + SHARE, :] for begin in begins], axis=0)
+
+    def mean(group, place):
+        begin = (group * SIZE_Z + place) * SLOT + SHARE
+        return packed_ref[begin : begin + 1, :]
+
+    def scaled(errors, place):
+        return [
+            errors[group * SHARE : (group + 1) * SHARE] * mean(group, place) for group in range(SIZE_Y)
+        ]
+
+    split_at = SIZE_Y * SHARE
+    errors = jnp.zeros((split_at, CH), jnp.float32)
+    changes = jnp.zeros((len(middle) * CH, CH), jnp.float32)
+    for place in range(SIZE_Z - 1, -1, -1):
+        rows = scaled(errors, place)
+        for k, group in enumerate(middle):
+            rows.append((changes[k * CH : (k + 1) * CH] + identity) * mean(group, place))
+        moved = exact_left(jnp.concatenate(rows, axis=0), center)
+        errors = residues(place) + errors + moved[0:split_at]
+        changes = changes + moved[split_at:]
+    carry = jnp.zeros((SHARE, CH), jnp.float32)
+    carries = [carry]
+    for group in range(SIZE_Y - 1, 0, -1):
+        if group in middle:
+            stack_parts(parts.at[group - 1], changes[(group - 1) * CH : group * CH], slice(0, CH))
+            carry = carry + times(carry, parts[group - 1])
+        carry = carry + errors[group * SHARE : (group + 1) * SHARE]
+        carries.insert(0, carry)
+    errors = jnp.concatenate(carries, axis=0)
+    for place in range(SIZE_Z - 1, -1, -1):
+        for group in range(SIZE_Y):
+            begin = (group * SIZE_Z + place) * SHARE
+            upper_ref[begin : begin + SHARE, :] = errors[group * SHARE : (group + 1) * SHARE]
+        if place > 0:
+            moved = exact_left(jnp.concatenate(scaled(errors, place), axis=0), center)
+            errors = residues(place) + errors + moved
+
+
+def points_kernel(own_ref, residue_ref, error_ref, mean_ref, center_ref, points_ref, mark_ref):
     mark_ref[...] = mean_ref[...]
     error = error_ref[...]
     moved = moved_by(error, mean_ref[0:1, :], center_ref[...])
-    for part in range(ROWS):
-        span = slice(part * COLS, (part + 1) * COLS)
-        points_ref[span, :] = own_ref[span, :] + (packed_ref[part, 0:COLS, :] + error[span] + moved[span])
+    points_ref[...] = own_ref[...] + (residue_ref[...] + error + moved)
 
 
 def second_kernel(
@@ -274,15 +291,13 @@
 
 
 def local(checkpoints, conv_weight, conv_bias, point_guess, terminal):
-    slices = SIZE_Y * SIZE_Z
-    step = 2.0 / (STEPS_DEV * slices)
+    step = 2.0 / (STEPS_DEV * SLICES)
     own = point_guess.reshape(PIX, CH)
     terminal = terminal.reshape(PIX, CH)
     kernel = conv_weight.reshape(TAPS, CH)
-    place_y = lax.axis_index("y").astype(jnp.int32).reshape(1)
-    final = (lax.axis_index(("y", "z")) == slices - 1).astype(jnp.int32).reshape(1)
+    final = (lax.axis_index(("y", "z")) == SLICES - 1).astype(jnp.int32).reshape(1)
     core = lax.axis_index("core").astype(jnp.int32).reshape(1)
-    upper = ring_down(own, ("y", "z"), slices, 1)
+    upper = ring_down(own, ("y", "z"), SLICES, 1)
 
     def bound(function):
         def kernel_of(*refs):
@@ -290,31 +305,28 @@
 
         return kernel_of
 
-    slopes, lowered, flipped, center, mean = call(
+    slopes, turned, flipped, center, mean = call(
         bound(forward_kernel),
-        [f32(STEPS_DEV, PIX, CH), bf16(STEPS_DEV, PIX, WIDE), bf16(WIDE, WIDE), bf16(2 * CH, CH), f32(8, CH)],
+        [f32(STEPS_DEV, PIX, CH), bf16(WIDE, STEPS_DEV * PIX), bf16(WIDE, WIDE), bf16(2 * CH, CH), f32(8, CH)],
         1.5,
-        "sssvvv",
-        [pltpu.VMEM((WIDE, WIDE), jnp.bfloat16)],
-    )(core, place_y, final, checkpoints.reshape(PIX, CH), kernel, conv_bias.reshape(1, CH))
+        "ssvvv",
+        [pltpu.VMEM((WIDE, WIDE), jnp.bfloat16), pltpu.VMEM((STEPS_DEV, PIX, WIDE), jnp.bfloat16)],
+    )(core, final, checkpoints.reshape(PIX, CH), kernel, conv_bias.reshape(1, CH))
 
     wide = pltpu.VMEM((PIX, WIDE), jnp.bfloat16)
-    packed, chosen = call(
-        bound(relax_kernel), [f32(ROWS, SLOT, CH), f32(PIX, CH)], 1.4, "svvvvvv", [wide]
+    packed, residue, chosen = call(
+        bound(relax_kernel),
+        [f32(SLICES * SLOT, CH), f32(PIX, CH), f32(PIX, CH)],
+        1.2,
+        "svvvvvv",
+        [wide],
     )(final, upper, terminal, own, slopes, flipped, mean)
 
-    gathered = lax.all_to_all(packed, "z", 0, 0)
-    in_group, maps, total = call(
-        group_kernel, [f32(SIZE_Z, COLS, CH), bf16(3 * CH, SIZE_Z * CH), f32(COLS + CH, CH)], 1.0
+    gathered = swapped(packed, ("y", "z"), SLICES)
+    errors = call(
+        scan_kernel, f32(PIX, CH), 2.5, scratch=[pltpu.VMEM((SIZE_Y - 2, 3 * CH, CH), jnp.bfloat16)]
     )(gathered, center)
-    first = ring_down(total, "y", SIZE_Y, 1)
-    third = ring_down(total[0:COLS], "y", SIZE_Y, 3)
-    second = ring_down(total, "y", SIZE_Y, 2)
-    turned = call(turn_kernel, bf16(WIDE, STEPS_DEV * PIX), 0.4)(lowered, total)
-    upper_error = call(
-        carry_kernel, f32(SIZE_Z, COLS, CH), 1.0, "svvvvva", [pltpu.VMEM((2, 3 * CH, CH), jnp.bfloat16)]
-    )(place_y, first, second, third, in_group, maps, turned)
-    upper_error = lax.all_to_all(upper_error, "z", 0, 0).reshape(PIX, CH)
+    upper_error = swapped(errors, ("y", "z"), SLICES)
 
     kept, sent = call(
         bound(second_kernel),
@@ -330,7 +342,7 @@
     )(core, chosen, upper_error, slopes, turned, flipped)
 
     received = lax.ppermute(sent, "core", [(0, 1), (1, 0)])
-    points, mark = call(points_kernel, [f32(PIX, CH), f32(8, CH)], 0.8)(own, packed, upper_error, mean, center)
+    points, mark = call(points_kernel, [f32(PIX, CH), f32(8, CH)], 0.8)(own, residue, upper_error, mean, center)
     half = call(add_kernel, f32(HALF, CH), 0.1, "vva")(kept, received, mark)
     parts = swapped(half, ("y", "x"), PLANE)
     copies = call(sum_kernel, f32(SIZE_Z * PART, CH), 0.1)(parts)

time: 93 us -> 91.6 us (0.985)
  blocking collectives: 55.4 us -> 62 us
  starting transfers between devices: 21.4 us -> 17 us
  waiting for transfers between devices: 5.54 us -> 1.59 us
    all_to_all x3 -> x5, blocking collectives: 34.5 us -> 62 us  [swapped(): return lax.all_to_all(parts, axes, 0, 0).reshape(rows.shape)]
    all_to_all x2 -> x0, blocking collectives: 20.9 us -> none  [the longest x1 10.5 us: local(): gathered = lax.all_to_all(packed, 'z', 0, 0)]
    ppermute x4 -> x1, starting transfers between devices: 13 us -> 8.93 us  [ring_down(): lax.ppermute(value, axis, [((i + distance) % count, i) for i in range(cou...]
    ppermute x4 -> x1, waiting for transfers between devices: 3.95 us -> 0.01 us  [ring_down(): lax.ppermute(value, axis, [((i + distance) % count, i) for i in range(cou...]
    pallas_call x10 -> x8, Pallas kernels: 6.31 us -> 6.76 us  [run(): pl.pallas_call(kernel, out_shape=outs, in_specs=[places[kind] for kind in...]
  transfers between devices with their start and end apart: 6 -> 3, of which waited for: 3 -> 2; matrix products, arithmetic and copies ran while one was open for 0% -> 0% of each run, Pallas kernels for 2% -> 2%
where the time goes in v6:
time: 91.6 us; the launch traced here: 91.3 us
  blocking collectives  62 us (68%)
  starting transfers between devices  17 us (19%)
  Pallas kernels  7.59 us (8%)
  local copies, waits for them, and re-layouts  2.46 us (3%)
  waiting for transfers between devices  1.59 us (2%)
    all_to_all x5, blocking collectives, swapped(): return lax.all_to_all(parts, axes, 0, 0).reshape(rows.shape)  62 us
    ppermute x1, starting transfers between devices, ring_down(): lax.ppermute(value, axis, [((i + distance) % count, i) for i in range(cou...  8.93 us
    pallas_call x8, Pallas kernels, run(): pl.pallas_call(kernel, out_shape=outs, in_specs=[places[kind] for kind in...  6.76 us
    ppermute x1, starting transfers between devices, local(): received = lax.ppermute(sent, 'core', [(0, 1), (1, 0)])  4.24 us
    ppermute x1, starting transfers between devices, local(): other = lax.ppermute(half, 'core', [(0, 1), (1, 0)])  3.79 us
    unnamed x10, local copies, waits for them, and re-layouts  2.46 us
  transfers between devices with their start and end apart: 3, of which 2 were waited for; matrix products, arithmetic and copies ran while one was open for 0% of the time, Pallas kernels for 2%

profile of v6, /device:TPU:1, one launch (start us, length us, event | category | flops | bytes accessed | tf_op | source)
XLA Modules:
  0.0 91.3 jit_solution(4834055150891730108)
XLA Ops:
  0.6 8.9 %collective-permute-start = (f32[256,128]{1,0:T(8,128)}, f32[256,128]{1,0:T(8,128)S(1)}, u32[]{:S(2)}, u32[]{:S(2)}) collective-permute-start(f32[256,128]{1,0:T(8,128)} %bitcast.33), channel_id=1, source_target_pairs={{8,0},{16,8},{24,16},{32,24},{40,32},{48,40},{56,48},{64,56},{72,6... | collective-permute-start | bytes 393224 | tf_op jit(solution)/shard_map/ppermute | solution.py:285
  9.6 0.0 copy-start.4
  9.6 0.7 copy-done.4
  10.2 0.0 copy-start
  10.2 1.0 %copy-done = bf16[3,3,128,128]{3,2,1,0:T(8,128)(2,1)S(1)} copy-done((bf16[3,3,128,128]{3,2,1,0:T(8,128)(2,1)S(1)}, bf16[3,3,128,128]{3,2,1,0:T(8,128)(2,1)}, u32[]{:S(2)}) %copy-start) | copy-done | bytes 294936
  11.2 0.0 copy-start.3
  11.2 0.8 copy-done.3
  12.0 0.0 copy-start.1
  12.0 0.0 copy-start.2
  12.0 1.3 %shard_map.68 = (f32[4,256,128]{2,1,0:T(8,128)S(1)}, bf16[384,1024]{1,0:T(8,128)(2,1)S(1)}, bf16[384,384]{1,0:T(8,128)(2,1)S(1)}, bf16[256,128]{1,0:T(8,128)(2,1)S(1)}, f32[8,128]{1,0:T(8,128)S(1)}) custom-call(s32[1]{0:T(128)} %bitcast.3.refs_0_.core_ref, s32[1]{0:T(128)} %bitcast.1.refs_1_.refs_0_, bf16[256,128]{1,0:T(8,128)(2,1)S(1)} %bitcast.36, ...), custom_call_target="tpu_custom_call" | custom-call | flops 1500000000 | bytes 5400000 | tf_op jit(solution)/shard_map/pallas_call | solution.py:33
  13.3 0.0 collective-permute-done.refs_1_
  13.3 0.0 copy-done.1
  13.3 0.0 copy-done.2
  13.3 1.2 %shard_map.69 = (f32[288,128]{1,0:T(8,128)S(1)}, f32[256,128]{1,0:T(8,128)S(1)}, f32[256,128]{1,0:T(8,128)S(1)}) custom-call(s32[1]{0:T(128)} %bitcast.1.refs_1_.refs_0_, f32[256,128]{1,0:T(8,128)S(1)} %collective-permute-done.refs_1_, f32[256,128]{1,0:T(8,128)S(1)} %bitcast.32, f32[256,128]{1,0:T(8,128)S(1)} %bitcast.34, ...), custom_call_target="tpu_custom_call" | custom-call | flops 1200000000 | bytes 4320000 | tf_op jit(solution)/shard_map/pallas_call | solution.py:33
  14.5 14.9 %all_to_all.25 = f32[32,1,1152]{2,1,0:T(1,128)S(1)} all-to-all(f32[32,1,1152]{2,1,0:T(1,128)S(1)} %bitcast.26), channel_id=1, replica_groups=mesh['y'=4,'z'=8,'x'=4,'core'=2] {'y','z'}, dimensions={0} | all-to-all | bytes 294912 | tf_op jit(solution)/shard_map/all_to_all | solution.py:290
  29.4 2.2 %shard_map.70 = f32[256,128]{1,0:T(8,128)S(1)} custom-call(f32[288,128]{1,0:T(8,128)S(1)} %bitcast.27, bf16[256,128]{1,0:T(8,128)(2,1)S(1)} %get-tuple-element.19.center_ref), custom_call_target="tpu_custom_call" | custom-call | flops 2500000000 | bytes 9000000 | tf_op jit(solution)/shard_map/pallas_call | solution.py:33
  31.6 12.8 %all_to_all.26 = f32[32,1,1024]{2,1,0:T(1,128)S(1)} all-to-all(f32[32,1,1024]{2,1,0:T(1,128)S(1)} %bitcast.30), channel_id=1, replica_groups=mesh['y'=4,'z'=8,'x'=4,'core'=2] {'y','z'}, dimensions={0} | all-to-all | bytes 262144 | tf_op jit(solution)/shard_map/all_to_all | solution.py:290
  44.3 1.2 %shard_map.72 = (f32[576,128]{1,0:T(8,128)S(1)}, f32[576,128]{1,0:T(8,128)S(1)}) custom-call(s32[1]{0:T(128)} %bitcast.3.refs_0_.core_ref, f32[256,128]{1,0:T(8,128)S(1)} %get-tuple-element.21.refs_1_, f32[256,128]{1,0:T(8,128)S(1)} %bitcast.28, f32[4,256,128]{2,1,0:T(8,128)S(1)} %get-tuple-element.14.refs_4_.refs_3_, ...), custom_call_target="tpu_custom_call" | custom-call | flops 1700000000 | bytes 6120000 | tf_op jit(solution)/shard_map/pallas_call | solution.py:33
  45.6 4.2 %collective-permute-start.1 = (f32[576,128]{1,0:T(8,128)S(1)}, f32[576,128]{1,0:T(8,128)S(1)}, u32[]{:S(2)}, u32[]{:S(2)}) collective-permute-start(f32[576,128]{1,0:T(8,128)S(1)} %get-tuple-element.24), channel_id=1, source_target_pairs={{0,1},{1,0},{2,3},{3,2},{4,5},{5,4},{6,7},{7,6},{8,9},{9,8},{10,11... | collective-permute-start | bytes 884744 | tf_op jit(solution)/shard_map/ppermute | solution.py:344
  49.8 0.8 shard_map.71
  50.6 0.4 collective-permute-done.1.right_ref
  51.1 13.2 %all_to_all.27 = f32[16,1,4608]{2,1,0:T(1,128)S(1)} all-to-all(f32[16,1,4608]{2,1,0:T(1,128)S(1)} %bitcast.19), channel_id=1, replica_groups=mesh['y'=4,'z'=8,'x'=4,'core'=2] {'y','x'}, dimensions={0} | all-to-all | bytes 589824 | tf_op jit(solution)/shard_map/all_to_all | solution.py:290
  64.3 10.6 %all_to_all.28 = f32[8,1,4608]{2,1,0:T(1,128)S(1)} all-to-all(f32[8,1,4608]{2,1,0:T(1,128)S(1)} %bitcast.24), channel_id=1, replica_groups=mesh['y'=4,'z'=8,'x'=4,'core'=2] {'z'}, dimensions={0} | all-to-all | bytes 294912 | tf_op jit(solution)/shard_map/all_to_all | solution.py:290
  74.9 10.5 %all_to_all.29 = f32[16,1,4608]{2,1,0:T(1,128)S(1)} all-to-all(f32[16,1,4608]{2,1,0:T(1,128)S(1)} %bitcast.21), channel_id=1, replica_groups=mesh['y'=4,'z'=8,'x'=4,'core'=2] {'y','x'}, dimensions={0} | all-to-all | bytes 589824 | tf_op jit(solution)/shard_map/all_to_all | solution.py:290
  85.4 3.8 %collective-permute-start.2 = (f32[576,128]{1,0:T(8,128)S(1)}, f32[576,128]{1,0:T(8,128)S(1)}, u32[]{:S(2)}, u32[]{:S(2)}) collective-permute-start(f32[576,128]{1,0:T(8,128)S(1)} %bitcast.22), channel_id=1, source_target_pairs={{0,1},{1,0},{2,3},{3,2},{4,5},{5,4},{6,7},{7,6},{8,9},{9,8},{10,11... | collective-permute-start | bytes 884744 | tf_op jit(solution)/shard_map/ppermute | solution.py:352
  89.2 1.2 %collective-permute-done.2.other_ref = f32[576,128]{1,0:T(8,128)S(1)} collective-permute-done((f32[576,128]{1,0:T(8,128)S(1)}, f32[576,128]{1,0:T(8,128)S(1)}, u32[]{:S(2)}, u32[]{:S(2)}) %collective-permute-start.2) | collective-permute-done | bytes 294944 | tf_op jit(solution)/shard_map/ppermute | solution.py:352
  90.4 0.8 shard_map.76
  (3 shorter events, 0.1 us)
Async XLA Ops:
  0.6 12.7 %collective-permute-start = (f32[256,128]{1,0:T(8,128)}, f32[256,128]{1,0:T(8,128)S(1)}, u32[]{:S(2)}, u32[]{:S(2)}) collective-permute-start(f32[256,128]{1,0:T(8,128)} %bitcast.33), channel_id=1, source_target_pairs={{8,0},{16,8},{24,16},{32,24},{40,32},{48,40},{56,48},{64,56},{72,6... | collective-permute-start | bytes 393224 | tf_op jit(solution)/shard_map/ppermute | solution.py:285
  9.6 0.7 copy-start.4
  10.2 1.0 %copy-start = (bf16[3,3,128,128]{3,2,1,0:T(8,128)(2,1)S(1)}, bf16[3,3,128,128]{3,2,1,0:T(8,128)(2,1)}, u32[]{:S(2)}) copy-start(bf16[3,3,128,128]{3,2,1,0:T(8,128)(2,1)} %param.6) | copy-start | bytes 884740
  11.2 0.8 copy-start.3
  12.0 1.3 %copy-start.1 = (f32[1,8,32,128]{3,2,1,0:T(8,128)S(1)}, f32[1,8,32,128]{3,2,1,0:T(8,128)}, u32[]{:S(2)}) copy-start(f32[1,8,32,128]{3,2,1,0:T(8,128)} %param.9) | copy-start | bytes 393220
  12.0 1.3 %copy-start.2 = (f32[1,1,8,32,128]{4,3,2,1,0:T(8,128)S(1)}, f32[1,1,8,32,128]{4,3,2,1,0:T(8,128)}, u32[]{:S(2)}) copy-start(f32[1,1,8,32,128]{4,3,2,1,0:T(8,128)} %param.8) | copy-start | bytes 393220
  45.6 5.4 %collective-permute-start.1 = (f32[576,128]{1,0:T(8,128)S(1)}, f32[576,128]{1,0:T(8,128)S(1)}, u32[]{:S(2)}, u32[]{:S(2)}) collective-permute-start(f32[576,128]{1,0:T(8,128)S(1)} %get-tuple-element.24), channel_id=1, source_target_pairs={{0,1},{1,0},{2,3},{3,2},{4,5},{5,4},{6,7},{7,6},{8,9},{9,8},{10,11... | collective-permute-start | bytes 884744 | tf_op jit(solution)/shard_map/ppermute | solution.py:344
  85.4 5.0 %collective-permute-start.2 = (f32[576,128]{1,0:T(8,128)S(1)}, f32[576,128]{1,0:T(8,128)S(1)}, u32[]{:S(2)}, u32[]{:S(2)}) collective-permute-start(f32[576,128]{1,0:T(8,128)S(1)} %bitcast.22), channel_id=1, source_target_pairs={{0,1},{1,0},{2,3},{3,2},{4,5},{5,4},{6,7},{7,6},{8,9},{9,8},{10,11... | collective-permute-start | bytes 884744 | tf_op jit(solution)/shard_map/ppermute | solution.py:352

commit v7 on v6

--- a/solution.py
+++ b/solution.py
@@ -94,8 +94,12 @@
     )
 
 
+def first_kernel(core_ref, final_ref, mark_ref):
+    mark_ref[...] = jnp.zeros_like(mark_ref)
+
+
 def forward_kernel(
-    step, core_ref, final_ref, start_ref, kernel_ref, bias_ref, slope_ref, turned_ref, flipped_ref,
+    step, mark_ref, start_ref, kernel_ref, bias_ref, slope_ref, turned_ref, flipped_ref,
     center_ref, mean_ref, weights, lowered,
 ):
     col = columns()
@@ -269,16 +273,31 @@
         out_ref[copy * PART : (copy + 1) * PART, :] = total
 
 
-def join_kernel(core_ref, own_ref, other_ref, out_ref, sems):
-    core = core_ref[0]
-    copies = [
-        pltpu.make_async_copy(part, out_ref.at[pl.ds(pl.multiple_of(place * HALF, 8), HALF), :], sems.at[k])
-        for k, (part, place) in enumerate(((own_ref, core), (other_ref, 1 - core)))
-    ]
-    for copy in copies:
-        copy.start()
-    for copy in copies:
-        copy.wait()
+def place_kernel(other, core_ref, half_ref, *refs):
+    out_ref, sem = refs[-2:]
+    place = 1 - core_ref[0] if other else core_ref[0]
+    copy = pltpu.make_async_copy(half_ref, out_ref.at[pl.ds(pl.multiple_of(place * HALF, 8), HALF), :], sem)
+    copy.start()
+    copy.wait()
+
+
+def placed(other, core, half, so_far=()):
+    anywhere = pl.BlockSpec(memory_space=pl.ANY)
+
+    def kernel_of(*refs):
+        place_kernel(other, *refs)
+
+    return pl.pallas_call(
+        kernel_of,
+        out_shape=f32(TAPS, CH),
+        in_specs=[pl.BlockSpec(memory_space=pltpu.SMEM), pl.BlockSpec(memory_space=pltpu.VMEM)]
+        + [anywhere] * len(so_far),
+        out_specs=anywhere,
+        scratch_shapes=[pltpu.SemaphoreType.DMA],
+        input_output_aliases={2: 0} if so_far else {},
+        cost_estimate=pl.CostEstimate(flops=0, bytes_accessed=8 * HALF * CH, transcendentals=0),
+        compiler_params=pltpu.CompilerParams(vmem_limit_bytes=LIMIT),
+    )(core, half, *so_far)
 
 
 def ring_down(value, axis, count, distance):
@@ -305,13 +324,14 @@
 
         return kernel_of
 
+    mark = call(first_kernel, f32(8, CH), 3.0, "ss")(core, final)
     slopes, turned, flipped, center, mean = call(
         bound(forward_kernel),
         [f32(STEPS_DEV, PIX, CH), bf16(WIDE, STEPS_DEV * PIX), bf16(WIDE, WIDE), bf16(2 * CH, CH), f32(8, CH)],
         1.5,
-        "ssvvv",
+        "vvvv",
         [pltpu.VMEM((WIDE, WIDE), jnp.bfloat16), pltpu.VMEM((STEPS_DEV, PIX, WIDE), jnp.bfloat16)],
-    )(core, final, checkpoints.reshape(PIX, CH), kernel, conv_bias.reshape(1, CH))
+    )(mark, checkpoints.reshape(PIX, CH), kernel, conv_bias.reshape(1, CH))
 
     wide = pltpu.VMEM((PIX, WIDE), jnp.bfloat16)
     packed, residue, chosen = call(
@@ -342,22 +362,15 @@
     )(core, chosen, upper_error, slopes, turned, flipped)
 
     received = lax.ppermute(sent, "core", [(0, 1), (1, 0)])
-    points, mark = call(points_kernel, [f32(PIX, CH), f32(8, CH)], 0.8)(own, residue, upper_error, mean, center)
-    half = call(add_kernel, f32(HALF, CH), 0.1, "vva")(kept, received, mark)
+    points, points_mark = call(points_kernel, [f32(PIX, CH), f32(8, CH)], 0.8)(own, residue, upper_error, mean, center)
+    half = call(add_kernel, f32(HALF, CH), 0.1, "vva")(kept, received, points_mark)
     parts = swapped(half, ("y", "x"), PLANE)
     copies = call(sum_kernel, f32(SIZE_Z * PART, CH), 0.1)(parts)
     parts = swapped(copies, "z", SIZE_Z)
     copies = call(sum_kernel, f32(HALF, CH), 0.1)(parts)
     half = swapped(copies, ("y", "x"), PLANE)
     other = lax.ppermute(half, "core", [(0, 1), (1, 0)])
-    grad_w = pl.pallas_call(
-        join_kernel,
-        out_shape=f32(TAPS, CH),
-        in_specs=[pl.BlockSpec(memory_space=pltpu.SMEM)] + [pl.BlockSpec(memory_space=pltpu.VMEM)] * 2,
-        out_specs=pl.BlockSpec(memory_space=pl.ANY),
-        scratch_shapes=[pltpu.SemaphoreType.DMA((2,))],
-        compiler_params=pltpu.CompilerParams(vmem_limit_bytes=LIMIT),
-    )(core, half, other)
+    grad_w = placed(True, core, other, [placed(False, core, half)])
     return points.reshape(1, 1, ROWS, COLS, CH), grad_w.reshape(3, 3, CH, CH)
 
 

time: 91.6 us -> 91.5 us (level)
  local copies, waits for them, and re-layouts: 2.46 us -> 0.97 us
  blocking collectives: 62 us -> 63.3 us
    unnamed x10, local copies, waits for them, and re-layouts: 2.46 us -> 0.97 us
    all_to_all x5, blocking collectives: 62 us -> 63.3 us  [swapped(): return lax.all_to_all(parts, axes, 0, 0).reshape(rows.shape)]
    pallas_call x8 -> x9, Pallas kernels: 6.76 us -> 6.76 us  [run(): pl.pallas_call(kernel, out_shape=outs, in_specs=[places[kind] for kind in...]
  transfers between devices with their start and end apart: 3 -> 3, of which waited for: 2 -> 3; matrix products, arithmetic and copies ran while one was open for 0% -> 0% of each run, Pallas kernels for 2% -> 3%
where the time goes in v7:
time: 91.5 us; the launch traced here: 91.2 us
  blocking collectives  63.3 us (69%)
  starting transfers between devices  17 us (19%)
  Pallas kernels  8.21 us (9%)
  waiting for transfers between devices  1.08 us (1%)
  local copies, waits for them, and re-layouts  0.97 us (1%)
    all_to_all x5, blocking collectives, swapped(): return lax.all_to_all(parts, axes, 0, 0).reshape(rows.shape)  63.3 us
    ppermute x1, starting transfers between devices, ring_down(): lax.ppermute(value, axis, [((i + distance) % count, i) for i in range(cou...  8.93 us
    pallas_call x9, Pallas kernels, run(): pl.pallas_call(kernel, out_shape=outs, in_specs=[places[kind] for kind in...  6.76 us
    ppermute x1, starting transfers between devices, local(): received = lax.ppermute(sent, 'core', [(0, 1), (1, 0)])  4.24 us
    ppermute x1, starting transfers between devices, local(): other = lax.ppermute(half, 'core', [(0, 1), (1, 0)])  3.79 us
  transfers between devices with their start and end apart: 3, of which 3 were waited for; matrix products, arithmetic and copies ran while one was open for 0% of the time, Pallas kernels for 3%

profile of v7, /device:TPU:1, one launch (start us, length us, event | category | flops | bytes accessed | tf_op | source)
XLA Modules:
  0.0 91.2 jit_solution(6659448797642269680)
XLA Ops:
  0.6 8.9 %collective-permute-start = (f32[256,128]{1,0:T(8,128)}, f32[256,128]{1,0:T(8,128)S(1)}, u32[]{:S(2)}, u32[]{:S(2)}) collective-permute-start(f32[256,128]{1,0:T(8,128)} %bitcast.33), channel_id=1, source_target_pairs={{8,0},{16,8},{24,16},{32,24},{40,32},{48,40},{56,48},{64,56},{72,6... | collective-permute-start | bytes 393224 | tf_op jit(solution)/shard_map/ppermute | solution.py:304
  9.6 0.0 copy-start
  9.6 0.0 copy-start.3
  9.6 0.0 copy-start.4
  9.6 1.0 %copy-done = bf16[3,3,128,128]{3,2,1,0:T(8,128)(2,1)S(1)} copy-done((bf16[3,3,128,128]{3,2,1,0:T(8,128)(2,1)S(1)}, bf16[3,3,128,128]{3,2,1,0:T(8,128)(2,1)}, u32[]{:S(2)}) %copy-start) | copy-done | bytes 294936
  10.5 0.0 copy-done.3
  10.5 0.0 copy-done.4
  10.5 0.0 copy-start.1
  10.5 0.0 copy-start.2
  10.5 1.3 %shard_map.69 = (f32[4,256,128]{2,1,0:T(8,128)S(1)}, bf16[384,1024]{1,0:T(8,128)(2,1)S(1)}, bf16[384,384]{1,0:T(8,128)(2,1)S(1)}, bf16[256,128]{1,0:T(8,128)(2,1)S(1)}, f32[8,128]{1,0:T(8,128)S(1)}) custom-call(f32[8,128]{1,0:T(8,128)S(1)} %shard_map.68.refs_0_, bf16[256,128]{1,0:T(8,128)(2,1)S(1)} %bitcast.36, bf16[1152,128]{1,0:T(8,128)(2,1)S(1)} %bitcast.31, ...), custom_call_target="tpu_custom_call" | custom-call | flops 1500000000 | bytes 5400000 | tf_op jit(solution)/shard_map/pallas_call | solution.py:33
  11.8 0.2 collective-permute-done.refs_1_
  12.0 0.0 copy-done.1
  12.0 0.0 copy-done.2
  12.0 1.2 %shard_map.70 = (f32[288,128]{1,0:T(8,128)S(1)}, f32[256,128]{1,0:T(8,128)S(1)}, f32[256,128]{1,0:T(8,128)S(1)}) custom-call(s32[1]{0:T(128)} %bitcast.1.final_ref.refs_0_, f32[256,128]{1,0:T(8,128)S(1)} %collective-permute-done.refs_1_, f32[256,128]{1,0:T(8,128)S(1)} %bitcast.32, f32[256,128]{1,0:T(8,128)S(1)} %bitcast.34, ...), custom_call_target="tpu_custom_call" | custom-call | flops 1200000000 | bytes 4320000 | tf_op jit(solution)/shard_map/pallas_call | solution.py:33
  13.2 16.2 %all_to_all.25 = f32[32,1,1152]{2,1,0:T(1,128)S(1)} all-to-all(f32[32,1,1152]{2,1,0:T(1,128)S(1)} %bitcast.26), channel_id=1, replica_groups=mesh['y'=4,'z'=8,'x'=4,'core'=2] {'y','z'}, dimensions={0} | all-to-all | bytes 294912 | tf_op jit(solution)/shard_map/all_to_all | solution.py:309
  29.4 2.2 %shard_map.71 = f32[256,128]{1,0:T(8,128)S(1)} custom-call(f32[288,128]{1,0:T(8,128)S(1)} %bitcast.27, bf16[256,128]{1,0:T(8,128)(2,1)S(1)} %get-tuple-element.19.center_ref), custom_call_target="tpu_custom_call" | custom-call | flops 2500000000 | bytes 9000000 | tf_op jit(solution)/shard_map/pallas_call | solution.py:33
  31.6 12.8 %all_to_all.26 = f32[32,1,1024]{2,1,0:T(1,128)S(1)} all-to-all(f32[32,1,1024]{2,1,0:T(1,128)S(1)} %bitcast.30), channel_id=1, replica_groups=mesh['y'=4,'z'=8,'x'=4,'core'=2] {'y','z'}, dimensions={0} | all-to-all | bytes 262144 | tf_op jit(solution)/shard_map/all_to_all | solution.py:309
  44.4 1.2 %shard_map.73 = (f32[576,128]{1,0:T(8,128)S(1)}, f32[576,128]{1,0:T(8,128)S(1)}) custom-call(s32[1]{0:T(128)} %bitcast.3.core_ref.refs_0_, f32[256,128]{1,0:T(8,128)S(1)} %get-tuple-element.21.refs_1_, f32[256,128]{1,0:T(8,128)S(1)} %bitcast.28, f32[4,256,128]{2,1,0:T(8,128)S(1)} %get-tuple-element.14.refs_4_.refs_3_, ...), custom_call_target="tpu_custom_call" | custom-call | flops 1700000000 | bytes 6120000 | tf_op jit(solution)/shard_map/pallas_call | solution.py:33
  45.6 4.2 %collective-permute-start.1 = (f32[576,128]{1,0:T(8,128)S(1)}, f32[576,128]{1,0:T(8,128)S(1)}, u32[]{:S(2)}, u32[]{:S(2)}) collective-permute-start(f32[576,128]{1,0:T(8,128)S(1)} %get-tuple-element.24), channel_id=1, source_target_pairs={{0,1},{1,0},{2,3},{3,2},{4,5},{5,4},{6,7},{7,6},{8,9},{9,8},{10,11... | collective-permute-start | bytes 884744 | tf_op jit(solution)/shard_map/ppermute | solution.py:364
  49.8 0.8 shard_map.72
  50.6 0.4 collective-permute-done.1.right_ref
  51.1 13.2 %all_to_all.27 = f32[16,1,4608]{2,1,0:T(1,128)S(1)} all-to-all(f32[16,1,4608]{2,1,0:T(1,128)S(1)} %bitcast.21), channel_id=1, replica_groups=mesh['y'=4,'z'=8,'x'=4,'core'=2] {'y','x'}, dimensions={0} | all-to-all | bytes 589824 | tf_op jit(solution)/shard_map/all_to_all | solution.py:309
  64.3 10.6 %all_to_all.28 = f32[8,1,4608]{2,1,0:T(1,128)S(1)} all-to-all(f32[8,1,4608]{2,1,0:T(1,128)S(1)} %bitcast.24), channel_id=1, replica_groups=mesh['y'=4,'z'=8,'x'=4,'core'=2] {'z'}, dimensions={0} | all-to-all | bytes 294912 | tf_op jit(solution)/shard_map/all_to_all | solution.py:309
  74.9 10.5 %all_to_all.29 = f32[16,1,4608]{2,1,0:T(1,128)S(1)} all-to-all(f32[16,1,4608]{2,1,0:T(1,128)S(1)} %bitcast.23), channel_id=1, replica_groups=mesh['y'=4,'z'=8,'x'=4,'core'=2] {'y','x'}, dimensions={0} | all-to-all | bytes 589824 | tf_op jit(solution)/shard_map/all_to_all | solution.py:309
  85.4 3.8 %collective-permute-start.2 = (f32[576,128]{1,0:T(8,128)S(1)}, f32[576,128]{1,0:T(8,128)S(1)}, u32[]{:S(2)}, u32[]{:S(2)}) collective-permute-start(f32[576,128]{1,0:T(8,128)S(1)} %bitcast.19), channel_id=1, source_target_pairs={{0,1},{1,0},{2,3},{3,2},{4,5},{5,4},{6,7},{7,6},{8,9},{9,8},{10,11... | collective-permute-start | bytes 884744 | tf_op jit(solution)/shard_map/ppermute | solution.py:372
  89.2 0.7 shard_map.77.refs_2_
  90.0 0.5 collective-permute-done.2.refs_1_
  90.4 0.7 shard_map.78
  (4 shorter events, 0.1 us)
Async XLA Ops:
  0.6 11.4 %collective-permute-start = (f32[256,128]{1,0:T(8,128)}, f32[256,128]{1,0:T(8,128)S(1)}, u32[]{:S(2)}, u32[]{:S(2)}) collective-permute-start(f32[256,128]{1,0:T(8,128)} %bitcast.33), channel_id=1, source_target_pairs={{8,0},{16,8},{24,16},{32,24},{40,32},{48,40},{56,48},{64,56},{72,6... | collective-permute-start | bytes 393224 | tf_op jit(solution)/shard_map/ppermute | solution.py:304
  9.6 1.0 %copy-start = (bf16[3,3,128,128]{3,2,1,0:T(8,128)(2,1)S(1)}, bf16[3,3,128,128]{3,2,1,0:T(8,128)(2,1)}, u32[]{:S(2)}) copy-start(bf16[3,3,128,128]{3,2,1,0:T(8,128)(2,1)} %param.6) | copy-start | bytes 884740
  9.6 1.0 %copy-start.3 = (bf16[1,1,8,32,128]{4,3,2,1,0:T(8,128)(2,1)S(1)}, bf16[1,1,8,32,128]{4,3,2,1,0:T(8,128)(2,1)}, u32[]{:S(2)}) copy-start(bf16[1,1,8,32,128]{4,3,2,1,0:T(8,128)(2,1)} %param.5) | copy-start | bytes 196612
  9.6 1.0 %copy-start.4 = (f32[128]{0:T(128)S(1)}, f32[128]{0:T(128)}, u32[]{:S(2)}) copy-start(f32[128]{0:T(128)} %param.7) | copy-start | bytes 1540
  10.5 1.5 %copy-start.1 = (f32[1,8,32,128]{3,2,1,0:T(8,128)S(1)}, f32[1,8,32,128]{3,2,1,0:T(8,128)}, u32[]{:S(2)}) copy-start(f32[1,8,32,128]{3,2,1,0:T(8,128)} %param.9) | copy-start | bytes 393220
  10.5 1.5 %copy-start.2 = (f32[1,1,8,32,128]{4,3,2,1,0:T(8,128)S(1)}, f32[1,1,8,32,128]{4,3,2,1,0:T(8,128)}, u32[]{:S(2)}) copy-start(f32[1,1,8,32,128]{4,3,2,1,0:T(8,128)} %param.8) | copy-start | bytes 393220
  45.6 5.4 %collective-permute-start.1 = (f32[576,128]{1,0:T(8,128)S(1)}, f32[576,128]{1,0:T(8,128)S(1)}, u32[]{:S(2)}, u32[]{:S(2)}) collective-permute-start(f32[576,128]{1,0:T(8,128)S(1)} %get-tuple-element.24), channel_id=1, source_target_pairs={{0,1},{1,0},{2,3},{3,2},{4,5},{5,4},{6,7},{7,6},{8,9},{9,8},{10,11... | collective-permute-start | bytes 884744 | tf_op jit(solution)/shard_map/ppermute | solution.py:364
  85.4 5.0 %collective-permute-start.2 = (f32[576,128]{1,0:T(8,128)S(1)}, f32[576,128]{1,0:T(8,128)S(1)}, u32[]{:S(2)}, u32[]{:S(2)}) collective-permute-start(f32[576,128]{1,0:T(8,128)S(1)} %bitcast.19), channel_id=1, source_target_pairs={{0,1},{1,0},{2,3},{3,2},{4,5},{5,4},{6,7},{7,6},{8,9},{9,8},{10,11... | collective-permute-start | bytes 884744 | tf_op jit(solution)/shard_map/ppermute | solution.py:372

commit v8 on v7

--- a/solution.py
+++ b/solution.py
@@ -11,6 +11,8 @@
 CH = 128
 PIX = ROWS * COLS
 WIDE = 3 * CH
+PIECE = 64
+LENGTH = 4
 TAPS = 9 * CH
 SIZE_Y = 4
 SIZE_Z = 8
@@ -53,8 +55,8 @@
     return jax.ShapeDtypeStruct(shape, jnp.bfloat16)
 
 
-def columns():
-    return lax.broadcasted_iota(jnp.int32, (PIX, CH), 0) % COLS
+def columns(count):
+    return lax.broadcasted_iota(jnp.int32, (count, CH), 0) % COLS
 
 
 def clear_edges(buffer):
@@ -74,13 +76,25 @@
 
 
 def from_right(value, col):
-    return jnp.where(col < COLS - 1, pltpu.roll(value, PIX - 1, 0), 0.0)
+    return jnp.where(col < COLS - 1, pltpu.roll(value, value.shape[0] - 1, 0), 0.0)
 
 
 def convolve(buffer, kernel, col):
-    taps = jnp.dot(buffer[...], kernel[...], preferred_element_type=jnp.float32)
+    taps = jnp.dot(buffer, kernel[...], preferred_element_type=jnp.float32)
     sides = from_left(taps[:, 0:CH], col) + from_right(taps[:, 2 * CH : WIDE], col)
     return taps[:, CH : 2 * CH] + sides
+
+
+def spread_piece(buffer, low, begin):
+    end = begin + PIECE
+    below, above = min(PIX, end + COLS), max(0, begin - COLS)
+    buffer[begin + COLS : below, 0:CH] = low[0 : below - begin - COLS]
+    buffer[begin:end, CH : 2 * CH] = low
+    buffer[above : end - COLS, 2 * CH : WIDE] = low[above + COLS - begin : PIECE]
+
+
+def pieces(ref, *lead):
+    return [ref[(*lead, slice(begin, begin + PIECE))] for begin in range(0, PIX, PIECE)]
 
 
 def split(value):
@@ -102,7 +116,7 @@
     step, mark_ref, start_ref, kernel_ref, bias_ref, slope_ref, turned_ref, flipped_ref,
     center_ref, mean_ref, weights, lowered,
 ):
-    col = columns()
+    col = columns(PIX)
     bias = bias_ref[...]
     for row in range(3):
         for tap in range(3):
@@ -113,7 +127,7 @@
         buffer = lowered.at[section]
         clear_edges(buffer)
         spread(buffer, current.astype(jnp.bfloat16))
-        tanh_out = jnp.tanh(convolve(buffer, weights, col) + bias)
+        tanh_out = jnp.tanh(convolve(buffer[...], weights, col) + bias)
         slope = 1.0 - tanh_out * tanh_out
         slope_ref[section] = slope
         if section == 0:
@@ -133,27 +147,40 @@
                 center_ref[CH : 2 * CH, :] = turned
 
 
-def adjoint_step(buffer, flipped, low, value, step, col):
-    spread(buffer, low)
-    return value + step * convolve(buffer, flipped, col)
+def adjoint_step(buffer, flipped, lows, values, step, col):
+    for k, low in enumerate(lows):
+        spread_piece(buffer, low, k * PIECE)
+    return [
+        value + step * convolve(buffer[k * PIECE : (k + 1) * PIECE, :], flipped, col)
+        for k, value in enumerate(values)
+    ]
+
+
+def lowered_grads(slope_ref, section, values):
+    return [(slope * value).astype(jnp.bfloat16) for slope, value in zip(pieces(slope_ref, section), values)]
 
 
 def relax_kernel(
-    step, final_ref, upper_ref, terminal_ref, own_ref, slope_ref, flipped_ref, mean_ref, packed_ref, residue_ref, chosen_ref, buffer
+    step, final_ref, upper_ref, terminal_ref, own_ref, slope_ref, flipped_ref, mean_ref,
+    packed_ref, residue_ref, chosen_ref, buffer,
 ):
-    col = columns()
+    col = columns(PIECE)
     clear_edges(buffer)
-    value = jnp.where(final_ref[0] == 1, terminal_ref[...], upper_ref[...])
-    chosen_ref[...] = value
+    final = final_ref[0] == 1
+    values = [jnp.where(final, last, upper) for last, upper in zip(pieces(terminal_ref), pieces(upper_ref))]
+    for k, value in enumerate(values):
+        chosen_ref[k * PIECE : (k + 1) * PIECE, :] = value
     for section in range(STEPS_DEV - 1, -1, -1):
-        low = (slope_ref[section] * value).astype(jnp.bfloat16)
-        value = adjoint_step(buffer, flipped_ref, low, value, step, col)
-    residue = value - own_ref[...]
-    residue_ref[...] = residue
+        lows = lowered_grads(slope_ref, section, values)
+        values = adjoint_step(buffer, flipped_ref, lows, values, step, col)
     mean = mean_ref[0:1, :]
-    for part in range(SLICES):
-        packed_ref[part * SLOT : part * SLOT + SHARE, :] = residue[part * SHARE : (part + 1) * SHARE]
-        packed_ref[part * SLOT + SHARE : (part + 1) * SLOT, :] = mean
+    for k, (value, own) in enumerate(zip(values, pieces(own_ref))):
+        residue = value - own
+        residue_ref[k * PIECE : (k + 1) * PIECE, :] = residue
+        for share in range(PIECE // SHARE):
+            begin = (k * (PIECE // SHARE) + share) * SLOT
+            packed_ref[begin : begin + SHARE, :] = residue[share * SHARE : (share + 1) * SHARE]
+            packed_ref[begin + SHARE : begin + SLOT, :] = mean
 
 
 def moved_by(value, mean, center):
@@ -177,43 +204,64 @@
     row = lax.broadcasted_iota(jnp.int32, (CH, CH), 0)
     lane = lax.broadcasted_iota(jnp.int32, (CH, CH), 1)
     identity = jnp.where(row == lane, 1.0, 0.0)
-    middle = range(1, SIZE_Y - 1)
+    groups = SLICES // LENGTH
+    pairs = groups // 2
+    middle = range(1, groups - 1)
 
     def residues(place):
-        begins = [(group * SIZE_Z + place) * SLOT for group in range(SIZE_Y)]
+        begins = [(group * LENGTH + place) * SLOT for group in range(groups)]
         return jnp.concatenate([packed_ref[begin : begin + SHARE, :] for begin in begins], axis=0)
 
     def mean(group, place):
-        begin = (group * SIZE_Z + place) * SLOT + SHARE
+        begin = (group * LENGTH + place) * SLOT + SHARE
         return packed_ref[begin : begin + 1, :]
 
     def scaled(errors, place):
-        return [
-            errors[group * SHARE : (group + 1) * SHARE] * mean(group, place) for group in range(SIZE_Y)
-        ]
-
-    split_at = SIZE_Y * SHARE
-    errors = jnp.zeros((split_at, CH), jnp.float32)
-    changes = jnp.zeros((len(middle) * CH, CH), jnp.float32)
-    for place in range(SIZE_Z - 1, -1, -1):
+        return [errors[group * SHARE : (group + 1) * SHARE] * mean(group, place) for group in range(groups)]
+
+    def change(group):
+        return changes[(group - 1) * CH : group * CH]
+
+    def prepared(place, value):
+        stack_parts(parts.at[place], value, slice(0, CH))
+        return parts[place]
+
+    split_at = groups * SHARE
+    errors = residues(LENGTH - 1)
+    starts = [identity * mean(group, LENGTH - 1) for group in middle]
+    changes = exact_left(jnp.concatenate(starts, axis=0), center)
+    for place in range(LENGTH - 2, -1, -1):
         rows = scaled(errors, place)
-        for k, group in enumerate(middle):
-            rows.append((changes[k * CH : (k + 1) * CH] + identity) * mean(group, place))
+        for group in middle:
+            rows.append((change(group) + identity) * mean(group, place))
         moved = exact_left(jnp.concatenate(rows, axis=0), center)
         errors = residues(place) + errors + moved[0:split_at]
         changes = changes + moved[split_at:]
+
+    totals = [errors[group * SHARE : (group + 1) * SHARE] for group in range(groups)]
+    maps = {group: prepared(group, change(group)) for group in middle}
+    pair_totals, pair_maps = {}, {}
+    for pair in range(1, pairs):
+        low, high = 2 * pair, 2 * pair + 1
+        pair_totals[pair] = totals[low] + totals[high] + times(totals[high], maps[low])
+        if pair < pairs - 1:
+            both = change(low) + change(high) + times(change(high), maps[low])
+            pair_maps[pair] = prepared(groups - 1 + pair, both)
+    carries = [None] * groups
     carry = jnp.zeros((SHARE, CH), jnp.float32)
-    carries = [carry]
-    for group in range(SIZE_Y - 1, 0, -1):
-        if group in middle:
-            stack_parts(parts.at[group - 1], changes[(group - 1) * CH : group * CH], slice(0, CH))
-            carry = carry + times(carry, parts[group - 1])
-        carry = carry + errors[group * SHARE : (group + 1) * SHARE]
-        carries.insert(0, carry)
+    for pair in range(pairs - 1, -1, -1):
+        low, high = 2 * pair, 2 * pair + 1
+        carries[high] = carry
+        carries[low] = totals[high] if pair == pairs - 1 else totals[high] + carry + times(carry, maps[high])
+        if pair > 0:
+            if pair < pairs - 1:
+                carry = carry + times(carry, pair_maps[pair])
+            carry = carry + pair_totals[pair]
+
     errors = jnp.concatenate(carries, axis=0)
-    for place in range(SIZE_Z - 1, -1, -1):
-        for group in range(SIZE_Y):
-            begin = (group * SIZE_Z + place) * SHARE
+    for place in range(LENGTH - 1, -1, -1):
+        for group in range(groups):
+            begin = (group * LENGTH + place) * SHARE
             upper_ref[begin : begin + SHARE, :] = errors[group * SHARE : (group + 1) * SHARE]
         if place > 0:
             moved = exact_left(jnp.concatenate(scaled(errors, place), axis=0), center)
@@ -231,17 +279,18 @@
     step, core_ref, chosen_ref, error_ref, slope_ref, turned_ref, flipped_ref, kept_ref, sent_ref,
     buffer, grads, total, ordered,
 ):
-    col = columns()
+    col = columns(PIECE)
     clear_edges(buffer)
-    value = chosen_ref[...] + error_ref[...]
+    values = [chosen + error for chosen, error in zip(pieces(chosen_ref), pieces(error_ref))]
     for section in range(STEPS_DEV - 1, -1, -1):
-        low = (slope_ref[section] * value).astype(jnp.bfloat16)
+        lows = lowered_grads(slope_ref, section, values)
         if section > 0:
-            value = adjoint_step(buffer, flipped_ref, low, value, step, col)
-        grad = low.astype(jnp.float32)
-        grads[section, :, 0:CH] = from_right(grad, col).astype(jnp.bfloat16)
-        grads[section, :, CH : 2 * CH] = low
-        grads[section, :, 2 * CH : WIDE] = from_left(grad, col).astype(jnp.bfloat16)
+            values = adjoint_step(buffer, flipped_ref, lows, values, step, col)
+        for k, low in enumerate(lows):
+            grad, span = low.astype(jnp.float32), slice(k * PIECE, (k + 1) * PIECE)
+            grads[section, span, 0:CH] = from_right(grad, col).astype(jnp.bfloat16)
+            grads[section, span, CH : 2 * CH] = low
+            grads[section, span, 2 * CH : WIDE] = from_left(grad, col).astype(jnp.bfloat16)
         term = jnp.dot(
             turned_ref[:, section * PIX : (section + 1) * PIX], grads[section], preferred_element_type=jnp.float32
         )
@@ -344,7 +393,7 @@
 
     gathered = swapped(packed, ("y", "z"), SLICES)
     errors = call(
-        scan_kernel, f32(PIX, CH), 2.5, scratch=[pltpu.VMEM((SIZE_Y - 2, 3 * CH, CH), jnp.bfloat16)]
+        scan_kernel, f32(PIX, CH), 2.5, scratch=[pltpu.VMEM((SLICES // LENGTH * 3 // 2, 3 * CH, CH), jnp.bfloat16)]
     )(gathered, center)
     upper_error = swapped(errors, ("y", "z"), SLICES)
 

time: 91.5 us -> 90.8 us (level)
  no operation moved by 1% of the time
where the time goes in v8:
time: 90.8 us; the launch traced here: 90.5 us
  blocking collectives  63.3 us (70%)
  starting transfers between devices  17 us (19%)
  Pallas kernels  7.51 us (8%)
  waiting for transfers between devices  1.08 us (1%)
  local copies, waits for them, and re-layouts  0.97 us (1%)
    all_to_all x5, blocking collectives, swapped(): return lax.all_to_all(parts, axes, 0, 0).reshape(rows.shape)  63.3 us
    ppermute x1, starting transfers between devices, ring_down(): lax.ppermute(value, axis, [((i + distance) % count, i) for i in range(cou...  8.93 us
    pallas_call x9, Pallas kernels, run(): pl.pallas_call(kernel, out_shape=outs, in_specs=[places[kind] for kind in...  6.06 us
    ppermute x1, starting transfers between devices, local(): received = lax.ppermute(sent, 'core', [(0, 1), (1, 0)])  4.25 us
    ppermute x1, starting transfers between devices, local(): other = lax.ppermute(half, 'core', [(0, 1), (1, 0)])  3.79 us
  transfers between devices with their start and end apart: 3, of which 3 were waited for; matrix products, arithmetic and copies ran while one was open for 0% of the time, Pallas kernels for 3%

profile of v8, /device:TPU:1, one launch (start us, length us, event | category | flops | bytes accessed | tf_op | source)
XLA Modules:
  0.0 90.5 jit_solution(12592323001713114778)
XLA Ops:
  0.6 8.9 %collective-permute-start = (f32[256,128]{1,0:T(8,128)}, f32[256,128]{1,0:T(8,128)S(1)}, u32[]{:S(2)}, u32[]{:S(2)}) collective-permute-start(f32[256,128]{1,0:T(8,128)} %bitcast.33), channel_id=1, source_target_pairs={{8,0},{16,8},{24,16},{32,24},{40,32},{48,40},{56,48},{64,56},{72,6... | collective-permute-start | bytes 393224 | tf_op jit(solution)/shard_map/ppermute | solution.py:353
  9.6 0.0 copy-start
  9.6 0.0 copy-start.3
  9.6 0.0 copy-start.4
  9.6 1.0 %copy-done = bf16[3,3,128,128]{3,2,1,0:T(8,128)(2,1)S(1)} copy-done((bf16[3,3,128,128]{3,2,1,0:T(8,128)(2,1)S(1)}, bf16[3,3,128,128]{3,2,1,0:T(8,128)(2,1)}, u32[]{:S(2)}) %copy-start) | copy-done | bytes 294936
  10.5 0.0 copy-done.3
  10.5 0.0 copy-done.4
  10.5 0.0 copy-start.1
  10.5 0.0 copy-start.2
  10.5 1.3 %shard_map.69 = (f32[4,256,128]{2,1,0:T(8,128)S(1)}, bf16[384,1024]{1,0:T(8,128)(2,1)S(1)}, bf16[384,384]{1,0:T(8,128)(2,1)S(1)}, bf16[256,128]{1,0:T(8,128)(2,1)S(1)}, f32[8,128]{1,0:T(8,128)S(1)}) custom-call(f32[8,128]{1,0:T(8,128)S(1)} %shard_map.68.refs_0_, bf16[256,128]{1,0:T(8,128)(2,1)S(1)} %bitcast.36, bf16[1152,128]{1,0:T(8,128)(2,1)S(1)} %bitcast.31, ...), custom_call_target="tpu_custom_call" | custom-call | flops 1500000000 | bytes 5400000 | tf_op jit(solution)/shard_map/pallas_call | solution.py:35
  11.8 0.2 collective-permute-done.refs_1_
  12.0 0.0 copy-done.1
  12.0 0.0 copy-done.2
  12.0 0.9 %shard_map.70 = (f32[288,128]{1,0:T(8,128)S(1)}, f32[256,128]{1,0:T(8,128)S(1)}, f32[256,128]{1,0:T(8,128)S(1)}) custom-call(s32[1]{0:T(128)} %bitcast.1.final_ref.refs_0_, f32[256,128]{1,0:T(8,128)S(1)} %collective-permute-done.refs_1_, f32[256,128]{1,0:T(8,128)S(1)} %bitcast.32, f32[256,128]{1,0:T(8,128)S(1)} %bitcast.34, ...), custom_call_target="tpu_custom_call" | custom-call | flops 1200000000 | bytes 4320000 | tf_op jit(solution)/shard_map/pallas_call | solution.py:35
  13.0 16.2 %all_to_all.25 = f32[32,1,1152]{2,1,0:T(1,128)S(1)} all-to-all(f32[32,1,1152]{2,1,0:T(1,128)S(1)} %bitcast.26), channel_id=1, replica_groups=mesh['y'=4,'z'=8,'x'=4,'core'=2] {'y','z'}, dimensions={0} | all-to-all | bytes 294912 | tf_op jit(solution)/shard_map/all_to_all | solution.py:358
  29.2 1.7 %shard_map.71 = f32[256,128]{1,0:T(8,128)S(1)} custom-call(f32[288,128]{1,0:T(8,128)S(1)} %bitcast.27, bf16[256,128]{1,0:T(8,128)(2,1)S(1)} %get-tuple-element.19.center_ref), custom_call_target="tpu_custom_call" | custom-call | flops 2500000000 | bytes 9000000 | tf_op jit(solution)/shard_map/pallas_call | solution.py:35
  30.9 12.8 %all_to_all.26 = f32[32,1,1024]{2,1,0:T(1,128)S(1)} all-to-all(f32[32,1,1024]{2,1,0:T(1,128)S(1)} %bitcast.30), channel_id=1, replica_groups=mesh['y'=4,'z'=8,'x'=4,'core'=2] {'y','z'}, dimensions={0} | all-to-all | bytes 262144 | tf_op jit(solution)/shard_map/all_to_all | solution.py:358
  43.6 1.3 %shard_map.73 = (f32[576,128]{1,0:T(8,128)S(1)}, f32[576,128]{1,0:T(8,128)S(1)}) custom-call(s32[1]{0:T(128)} %bitcast.3.core_ref.refs_0_, f32[256,128]{1,0:T(8,128)S(1)} %get-tuple-element.21.refs_1_, f32[256,128]{1,0:T(8,128)S(1)} %bitcast.28, f32[4,256,128]{2,1,0:T(8,128)S(1)} %get-tuple-element.14.refs_4_.refs_3_, ...), custom_call_target="tpu_custom_call" | custom-call | flops 1700000000 | bytes 6120000 | tf_op jit(solution)/shard_map/pallas_call | solution.py:35
  44.9 4.2 %collective-permute-start.1 = (f32[576,128]{1,0:T(8,128)S(1)}, f32[576,128]{1,0:T(8,128)S(1)}, u32[]{:S(2)}, u32[]{:S(2)}) collective-permute-start(f32[576,128]{1,0:T(8,128)S(1)} %get-tuple-element.24), channel_id=1, source_target_pairs={{0,1},{1,0},{2,3},{3,2},{4,5},{5,4},{6,7},{7,6},{8,9},{9,8},{10,11... | collective-permute-start | bytes 884744 | tf_op jit(solution)/shard_map/ppermute | solution.py:413
  49.1 0.8 shard_map.72
  50.0 0.4 collective-permute-done.1.right_ref
  50.4 13.2 %all_to_all.27 = f32[16,1,4608]{2,1,0:T(1,128)S(1)} all-to-all(f32[16,1,4608]{2,1,0:T(1,128)S(1)} %bitcast.21), channel_id=1, replica_groups=mesh['y'=4,'z'=8,'x'=4,'core'=2] {'y','x'}, dimensions={0} | all-to-all | bytes 589824 | tf_op jit(solution)/shard_map/all_to_all | solution.py:358
  63.6 10.6 %all_to_all.28 = f32[8,1,4608]{2,1,0:T(1,128)S(1)} all-to-all(f32[8,1,4608]{2,1,0:T(1,128)S(1)} %bitcast.24), channel_id=1, replica_groups=mesh['y'=4,'z'=8,'x'=4,'core'=2] {'z'}, dimensions={0} | all-to-all | bytes 294912 | tf_op jit(solution)/shard_map/all_to_all | solution.py:358
  74.2 10.5 %all_to_all.29 = f32[16,1,4608]{2,1,0:T(1,128)S(1)} all-to-all(f32[16,1,4608]{2,1,0:T(1,128)S(1)} %bitcast.23), channel_id=1, replica_groups=mesh['y'=4,'z'=8,'x'=4,'core'=2] {'y','x'}, dimensions={0} | all-to-all | bytes 589824 | tf_op jit(solution)/shard_map/all_to_all | solution.py:358
  84.8 3.8 %collective-permute-start.2 = (f32[576,128]{1,0:T(8,128)S(1)}, f32[576,128]{1,0:T(8,128)S(1)}, u32[]{:S(2)}, u32[]{:S(2)}) collective-permute-start(f32[576,128]{1,0:T(8,128)S(1)} %bitcast.19), channel_id=1, source_target_pairs={{0,1},{1,0},{2,3},{3,2},{4,5},{5,4},{6,7},{7,6},{8,9},{9,8},{10,11... | collective-permute-start | bytes 884744 | tf_op jit(solution)/shard_map/ppermute | solution.py:421
  88.5 0.7 shard_map.77.refs_2_
  89.3 0.5 collective-permute-done.2.refs_1_
  89.8 0.7 shard_map.78
  (4 shorter events, 0.1 us)
Async XLA Ops:
  0.6 11.4 %collective-permute-start = (f32[256,128]{1,0:T(8,128)}, f32[256,128]{1,0:T(8,128)S(1)}, u32[]{:S(2)}, u32[]{:S(2)}) collective-permute-start(f32[256,128]{1,0:T(8,128)} %bitcast.33), channel_id=1, source_target_pairs={{8,0},{16,8},{24,16},{32,24},{40,32},{48,40},{56,48},{64,56},{72,6... | collective-permute-start | bytes 393224 | tf_op jit(solution)/shard_map/ppermute | solution.py:353
  9.6 1.0 %copy-start = (bf16[3,3,128,128]{3,2,1,0:T(8,128)(2,1)S(1)}, bf16[3,3,128,128]{3,2,1,0:T(8,128)(2,1)}, u32[]{:S(2)}) copy-start(bf16[3,3,128,128]{3,2,1,0:T(8,128)(2,1)} %param.6) | copy-start | bytes 884740
  9.6 1.0 %copy-start.3 = (bf16[1,1,8,32,128]{4,3,2,1,0:T(8,128)(2,1)S(1)}, bf16[1,1,8,32,128]{4,3,2,1,0:T(8,128)(2,1)}, u32[]{:S(2)}) copy-start(bf16[1,1,8,32,128]{4,3,2,1,0:T(8,128)(2,1)} %param.5) | copy-start | bytes 196612
  9.6 1.0 %copy-start.4 = (f32[128]{0:T(128)S(1)}, f32[128]{0:T(128)}, u32[]{:S(2)}) copy-start(f32[128]{0:T(128)} %param.7) | copy-start | bytes 1540
  10.5 1.5 %copy-start.1 = (f32[1,8,32,128]{3,2,1,0:T(8,128)S(1)}, f32[1,8,32,128]{3,2,1,0:T(8,128)}, u32[]{:S(2)}) copy-start(f32[1,8,32,128]{3,2,1,0:T(8,128)} %param.9) | copy-start | bytes 393220
  10.5 1.5 %copy-start.2 = (f32[1,1,8,32,128]{4,3,2,1,0:T(8,128)S(1)}, f32[1,1,8,32,128]{4,3,2,1,0:T(8,128)}, u32[]{:S(2)}) copy-start(f32[1,1,8,32,128]{4,3,2,1,0:T(8,128)} %param.8) | copy-start | bytes 393220
  44.9 5.5 %collective-permute-start.1 = (f32[576,128]{1,0:T(8,128)S(1)}, f32[576,128]{1,0:T(8,128)S(1)}, u32[]{:S(2)}, u32[]{:S(2)}) collective-permute-start(f32[576,128]{1,0:T(8,128)S(1)} %get-tuple-element.24), channel_id=1, source_target_pairs={{0,1},{1,0},{2,3},{3,2},{4,5},{5,4},{6,7},{7,6},{8,9},{9,8},{10,11... | collective-permute-start | bytes 884744 | tf_op jit(solution)/shard_map/ppermute | solution.py:413
  84.8 5.0 %collective-permute-start.2 = (f32[576,128]{1,0:T(8,128)S(1)}, f32[576,128]{1,0:T(8,128)S(1)}, u32[]{:S(2)}, u32[]{:S(2)}) collective-permute-start(f32[576,128]{1,0:T(8,128)S(1)} %bitcast.19), channel_id=1, source_target_pairs={{0,1},{1,0},{2,3},{3,2},{4,5},{5,4},{6,7},{7,6},{8,9},{9,8},{10,11... | collective-permute-start | bytes 884744 | tf_op jit(solution)/shard_map/ppermute | solution.py:421

commit v9 on v8

--- a/solution.py
+++ b/solution.py
@@ -275,9 +275,21 @@
     points_ref[...] = own_ref[...] + (residue_ref[...] + error + moved)
 
 
+def half_rows(turned_ref, half, lanes):
+    begins = [pl.multiple_of(row * CH + half * (CH // 2), CH // 2) for row in range(3)]
+    return jnp.concatenate([turned_ref[pl.ds(begin, CH // 2), lanes] for begin in begins], axis=0)
+
+
+def store_half(out_ref, taps):
+    height = CH // 2
+    for row in range(3):
+        for tap in range(3):
+            begin = (3 * row + tap) * height
+            out_ref[begin : begin + height, :] = taps[row * height : (row + 1) * height, tap * CH : (tap + 1) * CH]
+
+
 def second_kernel(
-    step, core_ref, chosen_ref, error_ref, slope_ref, turned_ref, flipped_ref, kept_ref, sent_ref,
-    buffer, grads, total, ordered,
+    step, core_ref, chosen_ref, error_ref, slope_ref, turned_ref, flipped_ref, sent_ref, grads_ref, buffer, total
 ):
     col = columns(PIECE)
     clear_edges(buffer)
@@ -287,27 +299,26 @@
         if section > 0:
             values = adjoint_step(buffer, flipped_ref, lows, values, step, col)
         for k, low in enumerate(lows):
-            grad, span = low.astype(jnp.float32), slice(k * PIECE, (k + 1) * PIECE)
-            grads[section, span, 0:CH] = from_right(grad, col).astype(jnp.bfloat16)
-            grads[section, span, CH : 2 * CH] = low
-            grads[section, span, 2 * CH : WIDE] = from_left(grad, col).astype(jnp.bfloat16)
+            begin = section * PIX + k * PIECE
+            grad, span = low.astype(jnp.float32), slice(begin, begin + PIECE)
+            grads_ref[span, 0:CH] = from_right(grad, col).astype(jnp.bfloat16)
+            grads_ref[span, CH : 2 * CH] = low
+            grads_ref[span, 2 * CH : WIDE] = from_left(grad, col).astype(jnp.bfloat16)
+        part = slice(section * PIX, (section + 1) * PIX)
         term = jnp.dot(
-            turned_ref[:, section * PIX : (section + 1) * PIX], grads[section], preferred_element_type=jnp.float32
+            half_rows(turned_ref, 1 - core_ref[0], part), grads_ref[part, :], preferred_element_type=jnp.float32
         )
         if section == STEPS_DEV - 1:
             total[...] = term
         elif section > 0:
             total[...] += term
         else:
-            for row in range(3):
-                for tap in range(3):
-                    rows, lanes = slice(row * CH, (row + 1) * CH), slice(tap * CH, (tap + 1) * CH)
-                    begin = (3 * row + tap) * CH
-                    ordered[begin : begin + CH, :] = step * (total[rows, lanes] + term[rows, lanes])
-    first_core = core_ref[0] == 0
-    lower, upper = ordered[0:HALF, :], ordered[HALF:TAPS, :]
-    kept_ref[...] = jnp.where(first_core, lower, upper)
-    sent_ref[...] = jnp.where(first_core, upper, lower)
+            store_half(sent_ref, step * (total[...] + term))
+
+
+def kept_kernel(step, core_ref, turned_ref, grads_ref, kept_ref):
+    rows = half_rows(turned_ref, core_ref[0], slice(0, STEPS_DEV * PIX))
+    store_half(kept_ref, step * jnp.dot(rows, grads_ref[...], preferred_element_type=jnp.float32))
 
 
 def add_kernel(left_ref, right_ref, after_ref, out_ref):
@@ -323,11 +334,16 @@
 
 
 def place_kernel(other, core_ref, half_ref, *refs):
-    out_ref, sem = refs[-2:]
+    out_ref, sems = refs[-2:]
     place = 1 - core_ref[0] if other else core_ref[0]
-    copy = pltpu.make_async_copy(half_ref, out_ref.at[pl.ds(pl.multiple_of(place * HALF, 8), HALF), :], sem)
-    copy.start()
-    copy.wait()
+    copies = []
+    for row in range(3):
+        taps = slice(3 * row, 3 * row + 3)
+        copies.append(pltpu.make_async_copy(half_ref.at[taps], out_ref.at[taps, place], sems.at[row]))
+    for copy in copies:
+        copy.start()
+    for copy in copies:
+        copy.wait()
 
 
 def placed(other, core, half, so_far=()):
@@ -338,15 +354,15 @@
 
     return pl.pallas_call(
         kernel_of,
-        out_shape=f32(TAPS, CH),
+        out_shape=f32(9, 2, CH // 2, CH),
         in_specs=[pl.BlockSpec(memory_space=pltpu.SMEM), pl.BlockSpec(memory_space=pltpu.VMEM)]
         + [anywhere] * len(so_far),
         out_specs=anywhere,
-        scratch_shapes=[pltpu.SemaphoreType.DMA],
+        scratch_shapes=[pltpu.SemaphoreType.DMA((3,))],
         input_output_aliases={2: 0} if so_far else {},
         cost_estimate=pl.CostEstimate(flops=0, bytes_accessed=8 * HALF * CH, transcendentals=0),
         compiler_params=pltpu.CompilerParams(vmem_limit_bytes=LIMIT),
-    )(core, half, *so_far)
+    )(core, half.reshape(9, CH // 2, CH), *so_far)
 
 
 def ring_down(value, axis, count, distance):
@@ -397,20 +413,16 @@
     )(gathered, center)
     upper_error = swapped(errors, ("y", "z"), SLICES)
 
-    kept, sent = call(
+    sent, grads = call(
         bound(second_kernel),
-        [f32(HALF, CH)] * 2,
-        1.7,
+        [f32(HALF, CH), bf16(STEPS_DEV * PIX, WIDE)],
+        1.1,
         "svvvvv",
-        [
-            wide,
-            pltpu.VMEM((STEPS_DEV, PIX, WIDE), jnp.bfloat16),
-            pltpu.VMEM((WIDE, WIDE), jnp.float32),
-            pltpu.VMEM((TAPS, CH), jnp.float32),
-        ],
+        [wide, pltpu.VMEM((WIDE // 2, WIDE), jnp.float32)],
     )(core, chosen, upper_error, slopes, turned, flipped)
 
     received = lax.ppermute(sent, "core", [(0, 1), (1, 0)])
+    kept = call(bound(kept_kernel), f32(HALF, CH), 0.4, "svv")(core, turned, grads)
     points, points_mark = call(points_kernel, [f32(PIX, CH), f32(8, CH)], 0.8)(own, residue, upper_error, mean, center)
     half = call(add_kernel, f32(HALF, CH), 0.1, "vva")(kept, received, points_mark)
     parts = swapped(half, ("y", "x"), PLANE)

time: 90.8 us -> 90.5 us (level)
    pallas_call x9 -> x10, Pallas kernels: 6.06 us -> 6.21 us  [run(): pl.pallas_call(kernel, out_shape=outs, in_specs=[places[kind] for kind in...]
  transfers between devices with their start and end apart: 3 -> 3, of which waited for: 3 -> 2; matrix products, arithmetic and copies ran while one was open for 0% -> 0% of each run, Pallas kernels for 3% -> 4%
where the time goes in v9:
time: 90.5 us; the launch traced here: 90.3 us
  blocking collectives  63.3 us (70%)
  starting transfers between devices  17 us (19%)
  Pallas kernels  7.67 us (8%)
  local copies, waits for them, and re-layouts  0.97 us (1%)
    all_to_all x5, blocking collectives, swapped(): return lax.all_to_all(parts, axes, 0, 0).reshape(rows.shape)  63.3 us
    ppermute x1, starting transfers between devices, ring_down(): lax.ppermute(value, axis, [((i + distance) % count, i) for i in range(cou...  8.93 us
    pallas_call x10, Pallas kernels, run(): pl.pallas_call(kernel, out_shape=outs, in_specs=[places[kind] for kind in...  6.21 us
    ppermute x1, starting transfers between devices, local(): received = lax.ppermute(sent, 'core', [(0, 1), (1, 0)])  4.24 us
    ppermute x1, starting transfers between devices, local(): other = lax.ppermute(half, 'core', [(0, 1), (1, 0)])  3.79 us
  transfers between devices with their start and end apart: 3, of which 2 were waited for; matrix products, arithmetic and copies ran while one was open for 0% of the time, Pallas kernels for 4%

profile of v9, /device:TPU:1, one launch (start us, length us, event | category | flops | bytes accessed | tf_op | source)
XLA Modules:
  0.0 90.3 jit_solution(2949522103484098991)
XLA Ops:
  0.6 8.9 %collective-permute-start = (f32[256,128]{1,0:T(8,128)}, f32[256,128]{1,0:T(8,128)S(1)}, u32[]{:S(2)}, u32[]{:S(2)}) collective-permute-start(f32[256,128]{1,0:T(8,128)} %bitcast.36), channel_id=1, source_target_pairs={{8,0},{16,8},{24,16},{32,24},{40,32},{48,40},{56,48},{64,56},{72,6... | collective-permute-start | bytes 393224 | tf_op jit(solution)/shard_map/ppermute | solution.py:369
  9.6 0.0 copy-start
  9.6 0.0 copy-start.3
  9.6 0.0 copy-start.4
  9.6 1.0 %copy-done = bf16[3,3,128,128]{3,2,1,0:T(8,128)(2,1)S(1)} copy-done((bf16[3,3,128,128]{3,2,1,0:T(8,128)(2,1)S(1)}, bf16[3,3,128,128]{3,2,1,0:T(8,128)(2,1)}, u32[]{:S(2)}) %copy-start) | copy-done | bytes 294936
  10.5 0.0 copy-done.3
  10.5 0.0 copy-done.4
  10.5 0.0 copy-start.1
  10.5 0.0 copy-start.2
  10.5 1.3 %shard_map.69 = (f32[4,256,128]{2,1,0:T(8,128)S(1)}, bf16[384,1024]{1,0:T(8,128)(2,1)S(1)}, bf16[384,384]{1,0:T(8,128)(2,1)S(1)}, bf16[256,128]{1,0:T(8,128)(2,1)S(1)}, f32[8,128]{1,0:T(8,128)S(1)}) custom-call(f32[8,128]{1,0:T(8,128)S(1)} %shard_map.68.refs_0_, bf16[256,128]{1,0:T(8,128)(2,1)S(1)} %bitcast.39, bf16[1152,128]{1,0:T(8,128)(2,1)S(1)} %bitcast.34, ...), custom_call_target="tpu_custom_call" | custom-call | flops 1500000000 | bytes 5400000 | tf_op jit(solution)/shard_map/pallas_call | solution.py:35
  11.8 0.2 collective-permute-done.refs_1_
  12.0 0.0 copy-done.1
  12.0 0.0 copy-done.2
  12.0 0.9 %shard_map.70 = (f32[288,128]{1,0:T(8,128)S(1)}, f32[256,128]{1,0:T(8,128)S(1)}, f32[256,128]{1,0:T(8,128)S(1)}) custom-call(s32[1]{0:T(128)} %bitcast.1.final_ref.refs_0_, f32[256,128]{1,0:T(8,128)S(1)} %collective-permute-done.refs_1_, f32[256,128]{1,0:T(8,128)S(1)} %bitcast.35, f32[256,128]{1,0:T(8,128)S(1)} %bitcast.37, ...), custom_call_target="tpu_custom_call" | custom-call | flops 1200000000 | bytes 4320000 | tf_op jit(solution)/shard_map/pallas_call | solution.py:35
  13.0 16.2 %all_to_all.25 = f32[32,1,1152]{2,1,0:T(1,128)S(1)} all-to-all(f32[32,1,1152]{2,1,0:T(1,128)S(1)} %bitcast.29), channel_id=1, replica_groups=mesh['y'=4,'z'=8,'x'=4,'core'=2] {'y','z'}, dimensions={0} | all-to-all | bytes 294912 | tf_op jit(solution)/shard_map/all_to_all | solution.py:374
  29.2 1.7 %shard_map.71 = f32[256,128]{1,0:T(8,128)S(1)} custom-call(f32[288,128]{1,0:T(8,128)S(1)} %bitcast.30, bf16[256,128]{1,0:T(8,128)(2,1)S(1)} %get-tuple-element.19.center_ref), custom_call_target="tpu_custom_call" | custom-call | flops 2500000000 | bytes 9000000 | tf_op jit(solution)/shard_map/pallas_call | solution.py:35
  30.8 12.8 %all_to_all.26 = f32[32,1,1024]{2,1,0:T(1,128)S(1)} all-to-all(f32[32,1,1024]{2,1,0:T(1,128)S(1)} %bitcast.33), channel_id=1, replica_groups=mesh['y'=4,'z'=8,'x'=4,'core'=2] {'y','z'}, dimensions={0} | all-to-all | bytes 262144 | tf_op jit(solution)/shard_map/all_to_all | solution.py:374
  43.6 1.0 %shard_map.73 = (f32[576,128]{1,0:T(8,128)S(1)}, bf16[1024,384]{1,0:T(8,128)(2,1)S(1)}) custom-call(s32[1]{0:T(128)} %bitcast.3.core_ref.refs_0_, f32[256,128]{1,0:T(8,128)S(1)} %get-tuple-element.22.refs_1_, f32[256,128]{1,0:T(8,128)S(1)} %bitcast.31, f32[4,256,128]{2,1,0:T(8,128)S(1)} %get-tuple-element.14.refs_4_.refs_3_, ...), custom_call_target="tpu_custom_call" | custom-call | flops 1100000000 | bytes 3960000 | tf_op jit(solution)/shard_map/pallas_call | solution.py:35
  44.7 4.2 %collective-permute-start.1 = (f32[576,128]{1,0:T(8,128)S(1)}, f32[576,128]{1,0:T(8,128)S(1)}, u32[]{:S(2)}, u32[]{:S(2)}) collective-permute-start(f32[576,128]{1,0:T(8,128)S(1)} %get-tuple-element.24), channel_id=1, source_target_pairs={{0,1},{1,0},{2,3},{3,2},{4,5},{5,4},{6,7},{7,6},{8,9},{9,8},{10,11... | collective-permute-start | bytes 884744 | tf_op jit(solution)/shard_map/ppermute | solution.py:424
  48.9 0.4 shard_map.74.left_ref
  49.3 0.8 shard_map.72
  50.1 0.0 collective-permute-done.1.right_ref
  50.1 13.2 %all_to_all.27 = f32[16,1,4608]{2,1,0:T(1,128)S(1)} all-to-all(f32[16,1,4608]{2,1,0:T(1,128)S(1)} %bitcast.23), channel_id=1, replica_groups=mesh['y'=4,'z'=8,'x'=4,'core'=2] {'y','x'}, dimensions={0} | all-to-all | bytes 589824 | tf_op jit(solution)/shard_map/all_to_all | solution.py:374
  63.4 10.6 %all_to_all.28 = f32[8,1,4608]{2,1,0:T(1,128)S(1)} all-to-all(f32[8,1,4608]{2,1,0:T(1,128)S(1)} %bitcast.26), channel_id=1, replica_groups=mesh['y'=4,'z'=8,'x'=4,'core'=2] {'z'}, dimensions={0} | all-to-all | bytes 294912 | tf_op jit(solution)/shard_map/all_to_all | solution.py:374
  74.0 10.5 %all_to_all.29 = f32[16,1,4608]{2,1,0:T(1,128)S(1)} all-to-all(f32[16,1,4608]{2,1,0:T(1,128)S(1)} %bitcast.25), channel_id=1, replica_groups=mesh['y'=4,'z'=8,'x'=4,'core'=2] {'y','x'}, dimensions={0} | all-to-all | bytes 589824 | tf_op jit(solution)/shard_map/all_to_all | solution.py:374
  84.5 3.8 %collective-permute-start.2 = (f32[576,128]{1,0:T(8,128)S(1)}, f32[576,128]{1,0:T(8,128)S(1)}, u32[]{:S(2)}, u32[]{:S(2)}) collective-permute-start(f32[576,128]{1,0:T(8,128)S(1)} %bitcast.21), channel_id=1, source_target_pairs={{0,1},{1,0},{2,3},{3,2},{4,5},{5,4},{6,7},{7,6},{8,9},{9,8},{10,11... | collective-permute-start | bytes 884744 | tf_op jit(solution)/shard_map/ppermute | solution.py:433
  88.3 0.7 shard_map.78.refs_2_
  89.1 0.5 collective-permute-done.2
  89.5 0.7 shard_map.79
  (4 shorter events, 0.1 us)
Async XLA Ops:
  0.6 11.4 %collective-permute-start = (f32[256,128]{1,0:T(8,128)}, f32[256,128]{1,0:T(8,128)S(1)}, u32[]{:S(2)}, u32[]{:S(2)}) collective-permute-start(f32[256,128]{1,0:T(8,128)} %bitcast.36), channel_id=1, source_target_pairs={{8,0},{16,8},{24,16},{32,24},{40,32},{48,40},{56,48},{64,56},{72,6... | collective-permute-start | bytes 393224 | tf_op jit(solution)/shard_map/ppermute | solution.py:369
  9.6 1.0 %copy-start = (bf16[3,3,128,128]{3,2,1,0:T(8,128)(2,1)S(1)}, bf16[3,3,128,128]{3,2,1,0:T(8,128)(2,1)}, u32[]{:S(2)}) copy-start(bf16[3,3,128,128]{3,2,1,0:T(8,128)(2,1)} %param.6) | copy-start | bytes 884740
  9.6 1.0 %copy-start.3 = (bf16[1,1,8,32,128]{4,3,2,1,0:T(8,128)(2,1)S(1)}, bf16[1,1,8,32,128]{4,3,2,1,0:T(8,128)(2,1)}, u32[]{:S(2)}) copy-start(bf16[1,1,8,32,128]{4,3,2,1,0:T(8,128)(2,1)} %param.5) | copy-start | bytes 196612
  9.6 1.0 %copy-start.4 = (f32[128]{0:T(128)S(1)}, f32[128]{0:T(128)}, u32[]{:S(2)}) copy-start(f32[128]{0:T(128)} %param.7) | copy-start | bytes 1540
  10.5 1.5 %copy-start.1 = (f32[1,8,32,128]{3,2,1,0:T(8,128)S(1)}, f32[1,8,32,128]{3,2,1,0:T(8,128)}, u32[]{:S(2)}) copy-start(f32[1,8,32,128]{3,2,1,0:T(8,128)} %param.9) | copy-start | bytes 393220
  10.5 1.5 %copy-start.2 = (f32[1,1,8,32,128]{4,3,2,1,0:T(8,128)S(1)}, f32[1,1,8,32,128]{4,3,2,1,0:T(8,128)}, u32[]{:S(2)}) copy-start(f32[1,1,8,32,128]{4,3,2,1,0:T(8,128)} %param.8) | copy-start | bytes 393220
  44.7 5.5 %collective-permute-start.1 = (f32[576,128]{1,0:T(8,128)S(1)}, f32[576,128]{1,0:T(8,128)S(1)}, u32[]{:S(2)}, u32[]{:S(2)}) collective-permute-start(f32[576,128]{1,0:T(8,128)S(1)} %get-tuple-element.24), channel_id=1, source_target_pairs={{0,1},{1,0},{2,3},{3,2},{4,5},{5,4},{6,7},{7,6},{8,9},{9,8},{10,11... | collective-permute-start | bytes 884744 | tf_op jit(solution)/shard_map/ppermute | solution.py:424
  84.5 5.0 %collective-permute-start.2 = (f32[576,128]{1,0:T(8,128)S(1)}, f32[576,128]{1,0:T(8,128)S(1)}, u32[]{:S(2)}, u32[]{:S(2)}) collective-permute-start(f32[576,128]{1,0:T(8,128)S(1)} %bitcast.21), channel_id=1, source_target_pairs={{0,1},{1,0},{2,3},{3,2},{4,5},{5,4},{6,7},{7,6},{8,9},{9,8},{10,11... | collective-permute-start | bytes 884744 | tf_op jit(solution)/shard_map/ppermute | solution.py:433

commit v10 on v9

--- a/solution.py
+++ b/solution.py
@@ -108,7 +108,7 @@
     )
 
 
-def first_kernel(core_ref, final_ref, mark_ref):
+def first_kernel(mark_ref):
     mark_ref[...] = jnp.zeros_like(mark_ref)
 
 
@@ -161,12 +161,12 @@
 
 
 def relax_kernel(
-    step, final_ref, upper_ref, terminal_ref, own_ref, slope_ref, flipped_ref, mean_ref,
+    step, upper_ref, terminal_ref, own_ref, slope_ref, flipped_ref, mean_ref,
     packed_ref, residue_ref, chosen_ref, buffer,
 ):
     col = columns(PIECE)
     clear_edges(buffer)
-    final = final_ref[0] == 1
+    final = lax.axis_index(("y", "z")) == SLICES - 1
     values = [jnp.where(final, last, upper) for last, upper in zip(pieces(terminal_ref), pieces(upper_ref))]
     for k, value in enumerate(values):
         chosen_ref[k * PIECE : (k + 1) * PIECE, :] = value
@@ -289,7 +289,7 @@
 
 
 def second_kernel(
-    step, core_ref, chosen_ref, error_ref, slope_ref, turned_ref, flipped_ref, sent_ref, grads_ref, buffer, total
+    step, chosen_ref, error_ref, slope_ref, turned_ref, flipped_ref, sent_ref, grads_ref, buffer, total
 ):
     col = columns(PIECE)
     clear_edges(buffer)
@@ -306,7 +306,7 @@
             grads_ref[span, 2 * CH : WIDE] = from_left(grad, col).astype(jnp.bfloat16)
         part = slice(section * PIX, (section + 1) * PIX)
         term = jnp.dot(
-            half_rows(turned_ref, 1 - core_ref[0], part), grads_ref[part, :], preferred_element_type=jnp.float32
+            half_rows(turned_ref, 1 - lax.axis_index("core"), part), grads_ref[part, :], preferred_element_type=jnp.float32
         )
         if section == STEPS_DEV - 1:
             total[...] = term
@@ -316,8 +316,8 @@
             store_half(sent_ref, step * (total[...] + term))
 
 
-def kept_kernel(step, core_ref, turned_ref, grads_ref, kept_ref):
-    rows = half_rows(turned_ref, core_ref[0], slice(0, STEPS_DEV * PIX))
+def kept_kernel(step, turned_ref, grads_ref, kept_ref):
+    rows = half_rows(turned_ref, lax.axis_index("core"), slice(0, STEPS_DEV * PIX))
     store_half(kept_ref, step * jnp.dot(rows, grads_ref[...], preferred_element_type=jnp.float32))
 
 
@@ -333,9 +333,10 @@
         out_ref[copy * PART : (copy + 1) * PART, :] = total
 
 
-def place_kernel(other, core_ref, half_ref, *refs):
+def place_kernel(other, half_ref, *refs):
     out_ref, sems = refs[-2:]
-    place = 1 - core_ref[0] if other else core_ref[0]
+    core = lax.axis_index("core")
+    place = 1 - core if other else core
     copies = []
     for row in range(3):
         taps = slice(3 * row, 3 * row + 3)
@@ -346,7 +347,7 @@
         copy.wait()
 
 
-def placed(other, core, half, so_far=()):
+def placed(other, half, so_far=()):
     anywhere = pl.BlockSpec(memory_space=pl.ANY)
 
     def kernel_of(*refs):
@@ -355,14 +356,13 @@
     return pl.pallas_call(
         kernel_of,
         out_shape=f32(9, 2, CH // 2, CH),
-        in_specs=[pl.BlockSpec(memory_space=pltpu.SMEM), pl.BlockSpec(memory_space=pltpu.VMEM)]
-        + [anywhere] * len(so_far),
+        in_specs=[pl.BlockSpec(memory_space=pltpu.VMEM)] + [anywhere] * len(so_far),
         out_specs=anywhere,
         scratch_shapes=[pltpu.SemaphoreType.DMA((3,))],
-        input_output_aliases={2: 0} if so_far else {},
+        input_output_aliases={1: 0} if so_far else {},
         cost_estimate=pl.CostEstimate(flops=0, bytes_accessed=8 * HALF * CH, transcendentals=0),
         compiler_params=pltpu.CompilerParams(vmem_limit_bytes=LIMIT),
-    )(core, half.reshape(9, CH // 2, CH), *so_far)
+    )(half.reshape(9, CH // 2, CH), *so_far)
 
 
 def ring_down(value, axis, count, distance):
@@ -379,8 +379,6 @@
     own = point_guess.reshape(PIX, CH)
     terminal = terminal.reshape(PIX, CH)
     kernel = conv_weight.reshape(TAPS, CH)
-    final = (lax.axis_index(("y", "z")) == SLICES - 1).astype(jnp.int32).reshape(1)
-    core = lax.axis_index("core").astype(jnp.int32).reshape(1)
     upper = ring_down(own, ("y", "z"), SLICES, 1)
 
     def bound(function):
@@ -389,7 +387,7 @@
 
         return kernel_of
 
-    mark = call(first_kernel, f32(8, CH), 3.0, "ss")(core, final)
+    mark = call(first_kernel, f32(8, CH), 3.0)()
     slopes, turned, flipped, center, mean = call(
         bound(forward_kernel),
         [f32(STEPS_DEV, PIX, CH), bf16(WIDE, STEPS_DEV * PIX), bf16(WIDE, WIDE), bf16(2 * CH, CH), f32(8, CH)],
@@ -403,9 +401,8 @@
         bound(relax_kernel),
         [f32(SLICES * SLOT, CH), f32(PIX, CH), f32(PIX, CH)],
         1.2,
-        "svvvvvv",
-        [wide],
-    )(final, upper, terminal, own, slopes, flipped, mean)
+        scratch=[wide],
+    )(upper, terminal, own, slopes, flipped, mean)
 
     gathered = swapped(packed, ("y", "z"), SLICES)
     errors = call(
@@ -417,12 +414,11 @@
         bound(second_kernel),
         [f32(HALF, CH), bf16(STEPS_DEV * PIX, WIDE)],
         1.1,
-        "svvvvv",
-        [wide, pltpu.VMEM((WIDE // 2, WIDE), jnp.float32)],
-    )(core, chosen, upper_error, slopes, turned, flipped)
+        scratch=[wide, pltpu.VMEM((WIDE // 2, WIDE), jnp.float32)],
+    )(chosen, upper_error, slopes, turned, flipped)
 
     received = lax.ppermute(sent, "core", [(0, 1), (1, 0)])
-    kept = call(bound(kept_kernel), f32(HALF, CH), 0.4, "svv")(core, turned, grads)
+    kept = call(bound(kept_kernel), f32(HALF, CH), 0.4)(turned, grads)
     points, points_mark = call(points_kernel, [f32(PIX, CH), f32(8, CH)], 0.8)(own, residue, upper_error, mean, center)
     half = call(add_kernel, f32(HALF, CH), 0.1, "vva")(kept, received, points_mark)
     parts = swapped(half, ("y", "x"), PLANE)
@@ -431,7 +427,7 @@
     copies = call(sum_kernel, f32(HALF, CH), 0.1)(parts)
     half = swapped(copies, ("y", "x"), PLANE)
     other = lax.ppermute(half, "core", [(0, 1), (1, 0)])
-    grad_w = placed(True, core, other, [placed(False, core, half)])
+    grad_w = placed(True, other, [placed(False, half)])
     return points.reshape(1, 1, ROWS, COLS, CH), grad_w.reshape(3, 3, CH, CH)
 
 

time: 90.5 us -> 90.5 us (level)
  no operation moved by 1% of the time
where the time goes in v10:
time: 90.5 us; the launch traced here: 90.3 us
  blocking collectives  63.3 us (70%)
  starting transfers between devices  17 us (19%)
  Pallas kernels  7.63 us (8%)
  waiting for transfers between devices  1.02 us (1%)
    all_to_all x5, blocking collectives, swapped(): return lax.all_to_all(parts, axes, 0, 0).reshape(rows.shape)  63.3 us
    ppermute x1, starting transfers between devices, ring_down(): lax.ppermute(value, axis, [((i + distance) % count, i) for i in range(cou...  8.93 us
    pallas_call x10, Pallas kernels, run(): pl.pallas_call(kernel, out_shape=outs, in_specs=[places[kind] for kind in...  6.17 us
    ppermute x1, starting transfers between devices, local(): received = lax.ppermute(sent, 'core', [(0, 1), (1, 0)])  4.24 us
    ppermute x1, starting transfers between devices, local(): other = lax.ppermute(half, 'core', [(0, 1), (1, 0)])  3.79 us
  transfers between devices with their start and end apart: 3, of which 2 were waited for; matrix products, arithmetic and copies ran while one was open for 0% of the time, Pallas kernels for 4%

profile of v10, /device:TPU:1, one launch (start us, length us, event | category | flops | bytes accessed | tf_op | source)
XLA Modules:
  0.0 90.3 jit_solution(17732327665724266533)
XLA Ops:
  0.6 0.0 copy-start
  0.6 0.0 copy-start.3
  0.6 8.9 %collective-permute-start = (f32[256,128]{1,0:T(8,128)}, f32[256,128]{1,0:T(8,128)S(1)}, u32[]{:S(2)}, u32[]{:S(2)}) collective-permute-start(f32[256,128]{1,0:T(8,128)} %bitcast.34), channel_id=1, source_target_pairs={{8,0},{16,8},{24,16},{32,24},{40,32},{48,40},{56,48},{64,56},{72,6... | collective-permute-start | bytes 393224 | tf_op jit(solution)/shard_map/ppermute | solution.py:369
  9.6 0.0 copy-start.4
  9.6 0.0 copy-done
  9.6 0.0 copy-done.3
  9.6 0.6 copy-done.4
  10.2 0.0 copy-start.1
  10.2 0.0 copy-start.2
  10.2 1.3 %shard_map.69 = (f32[4,256,128]{2,1,0:T(8,128)S(1)}, bf16[384,1024]{1,0:T(8,128)(2,1)S(1)}, bf16[384,384]{1,0:T(8,128)(2,1)S(1)}, bf16[256,128]{1,0:T(8,128)(2,1)S(1)}, f32[8,128]{1,0:T(8,128)S(1)}) custom-call(f32[8,128]{1,0:T(8,128)S(1)} %shard_map.68.refs_0_, bf16[256,128]{1,0:T(8,128)(2,1)S(1)} %bitcast.37, bf16[1152,128]{1,0:T(8,128)(2,1)S(1)} %bitcast.32, ...), custom_call_target="tpu_custom_call" | custom-call | flops 1500000000 | bytes 5400000 | tf_op jit(solution)/shard_map/pallas_call | solution.py:35
  11.5 0.5 collective-permute-done.refs_0_
  12.1 0.0 copy-done.1
  12.1 0.0 copy-done.2
  12.1 0.9 %shard_map.70 = (f32[288,128]{1,0:T(8,128)S(1)}, f32[256,128]{1,0:T(8,128)S(1)}, f32[256,128]{1,0:T(8,128)S(1)}) custom-call(f32[256,128]{1,0:T(8,128)S(1)} %collective-permute-done.refs_0_, f32[256,128]{1,0:T(8,128)S(1)} %bitcast.33, f32[256,128]{1,0:T(8,128)S(1)} %bitcast.35, f32[4,256,128]{2,1,0:T(8,128)S(1)} %get-tuple-element.14.refs_3_.refs_2_, ...), custom_call_target="tpu_custom_call" | custom-call | flops 1200000000 | bytes 4320000 | tf_op jit(solution)/shard_map/pallas_call | solution.py:35
  13.0 16.2 %all_to_all.25 = f32[32,1,1152]{2,1,0:T(1,128)S(1)} all-to-all(f32[32,1,1152]{2,1,0:T(1,128)S(1)} %bitcast.27), channel_id=1, replica_groups=mesh['y'=4,'z'=8,'x'=4,'core'=2] {'y','z'}, dimensions={0} | all-to-all | bytes 294912 | tf_op jit(solution)/shard_map/all_to_all | solution.py:374
  29.2 1.7 %shard_map.71 = f32[256,128]{1,0:T(8,128)S(1)} custom-call(f32[288,128]{1,0:T(8,128)S(1)} %bitcast.28, bf16[256,128]{1,0:T(8,128)(2,1)S(1)} %get-tuple-element.19.center_ref), custom_call_target="tpu_custom_call" | custom-call | flops 2500000000 | bytes 9000000 | tf_op jit(solution)/shard_map/pallas_call | solution.py:35
  30.9 12.8 %all_to_all.26 = f32[32,1,1024]{2,1,0:T(1,128)S(1)} all-to-all(f32[32,1,1024]{2,1,0:T(1,128)S(1)} %bitcast.31), channel_id=1, replica_groups=mesh['y'=4,'z'=8,'x'=4,'core'=2] {'y','z'}, dimensions={0} | all-to-all | bytes 262144 | tf_op jit(solution)/shard_map/all_to_all | solution.py:374
  43.6 1.0 %shard_map.73 = (f32[576,128]{1,0:T(8,128)S(1)}, bf16[1024,384]{1,0:T(8,128)(2,1)S(1)}) custom-call(f32[256,128]{1,0:T(8,128)S(1)} %get-tuple-element.22.refs_0_, f32[256,128]{1,0:T(8,128)S(1)} %bitcast.29, f32[4,256,128]{2,1,0:T(8,128)S(1)} %get-tuple-element.14.refs_3_.refs_2_, bf16[384,1024]{1,0:T(8,128)(2,1)S(1)} %get-tuple-element.21.refs_3_.refs_0_, ...), custom_call_target="tpu_custom_call" | custom-call | flops 1100000000 | bytes 3960000 | tf_op jit(solution)/shard_map/pallas_call | solution.py:35
  44.7 4.2 %collective-permute-start.1 = (f32[576,128]{1,0:T(8,128)S(1)}, f32[576,128]{1,0:T(8,128)S(1)}, u32[]{:S(2)}, u32[]{:S(2)}) collective-permute-start(f32[576,128]{1,0:T(8,128)S(1)} %get-tuple-element.24), channel_id=1, source_target_pairs={{0,1},{1,0},{2,3},{3,2},{4,5},{5,4},{6,7},{7,6},{8,9},{9,8},{10,11... | collective-permute-start | bytes 884744 | tf_op jit(solution)/shard_map/ppermute | solution.py:420
  48.9 0.4 shard_map.74.left_ref
  49.3 0.8 shard_map.72
  50.1 0.0 collective-permute-done.1.right_ref
  50.1 13.2 %all_to_all.27 = f32[16,1,4608]{2,1,0:T(1,128)S(1)} all-to-all(f32[16,1,4608]{2,1,0:T(1,128)S(1)} %bitcast.21), channel_id=1, replica_groups=mesh['y'=4,'z'=8,'x'=4,'core'=2] {'y','x'}, dimensions={0} | all-to-all | bytes 589824 | tf_op jit(solution)/shard_map/all_to_all | solution.py:374
  63.4 10.6 %all_to_all.28 = f32[8,1,4608]{2,1,0:T(1,128)S(1)} all-to-all(f32[8,1,4608]{2,1,0:T(1,128)S(1)} %bitcast.24), channel_id=1, replica_groups=mesh['y'=4,'z'=8,'x'=4,'core'=2] {'z'}, dimensions={0} | all-to-all | bytes 294912 | tf_op jit(solution)/shard_map/all_to_all | solution.py:374
  74.0 10.5 %all_to_all.29 = f32[16,1,4608]{2,1,0:T(1,128)S(1)} all-to-all(f32[16,1,4608]{2,1,0:T(1,128)S(1)} %bitcast.23), channel_id=1, replica_groups=mesh['y'=4,'z'=8,'x'=4,'core'=2] {'y','x'}, dimensions={0} | all-to-all | bytes 589824 | tf_op jit(solution)/shard_map/all_to_all | solution.py:374
  84.5 3.8 %collective-permute-start.2 = (f32[576,128]{1,0:T(8,128)S(1)}, f32[576,128]{1,0:T(8,128)S(1)}, u32[]{:S(2)}, u32[]{:S(2)}) collective-permute-start(f32[576,128]{1,0:T(8,128)S(1)} %bitcast.19), channel_id=1, source_target_pairs={{0,1},{1,0},{2,3},{3,2},{4,5},{5,4},{6,7},{7,6},{8,9},{9,8},{10,11... | collective-permute-start | bytes 884744 | tf_op jit(solution)/shard_map/ppermute | solution.py:429
  88.3 0.7 shard_map.78.refs_1_
  89.1 0.5 collective-permute-done.2
  89.5 0.7 shard_map.79
  (4 shorter events, 0.1 us)
Async XLA Ops:
  0.6 9.0 %copy-start = (bf16[3,3,128,128]{3,2,1,0:T(8,128)(2,1)S(1)}, bf16[3,3,128,128]{3,2,1,0:T(8,128)(2,1)}, u32[]{:S(2)}) copy-start(bf16[3,3,128,128]{3,2,1,0:T(8,128)(2,1)} %param.6) | copy-start | bytes 884740
  0.6 9.0 %copy-start.3 = (bf16[1,1,8,32,128]{4,3,2,1,0:T(8,128)(2,1)S(1)}, bf16[1,1,8,32,128]{4,3,2,1,0:T(8,128)(2,1)}, u32[]{:S(2)}) copy-start(bf16[1,1,8,32,128]{4,3,2,1,0:T(8,128)(2,1)} %param.5) | copy-start | bytes 196612
  0.6 11.4 %collective-permute-start = (f32[256,128]{1,0:T(8,128)}, f32[256,128]{1,0:T(8,128)S(1)}, u32[]{:S(2)}, u32[]{:S(2)}) collective-permute-start(f32[256,128]{1,0:T(8,128)} %bitcast.34), channel_id=1, source_target_pairs={{8,0},{16,8},{24,16},{32,24},{40,32},{48,40},{56,48},{64,56},{72,6... | collective-permute-start | bytes 393224 | tf_op jit(solution)/shard_map/ppermute | solution.py:369
  9.6 0.7 copy-start.4
  10.2 1.8 %copy-start.1 = (f32[1,8,32,128]{3,2,1,0:T(8,128)S(1)}, f32[1,8,32,128]{3,2,1,0:T(8,128)}, u32[]{:S(2)}) copy-start(f32[1,8,32,128]{3,2,1,0:T(8,128)} %param.9) | copy-start | bytes 393220
  10.2 1.8 %copy-start.2 = (f32[1,1,8,32,128]{4,3,2,1,0:T(8,128)S(1)}, f32[1,1,8,32,128]{4,3,2,1,0:T(8,128)}, u32[]{:S(2)}) copy-start(f32[1,1,8,32,128]{4,3,2,1,0:T(8,128)} %param.8) | copy-start | bytes 393220
  44.7 5.5 %collective-permute-start.1 = (f32[576,128]{1,0:T(8,128)S(1)}, f32[576,128]{1,0:T(8,128)S(1)}, u32[]{:S(2)}, u32[]{:S(2)}) collective-permute-start(f32[576,128]{1,0:T(8,128)S(1)} %get-tuple-element.24), channel_id=1, source_target_pairs={{0,1},{1,0},{2,3},{3,2},{4,5},{5,4},{6,7},{7,6},{8,9},{9,8},{10,11... | collective-permute-start | bytes 884744 | tf_op jit(solution)/shard_map/ppermute | solution.py:420
  84.5 5.0 %collective-permute-start.2 = (f32[576,128]{1,0:T(8,128)S(1)}, f32[576,128]{1,0:T(8,128)S(1)}, u32[]{:S(2)}, u32[]{:S(2)}) collective-permute-start(f32[576,128]{1,0:T(8,128)S(1)} %bitcast.19), channel_id=1, source_target_pairs={{0,1},{1,0},{2,3},{3,2},{4,5},{5,4},{6,7},{7,6},{8,9},{9,8},{10,11... | collective-permute-start | bytes 884744 | tf_op jit(solution)/shard_map/ppermute | solution.py:429

commit v11 on v9

--- a/solution.py
+++ b/solution.py
@@ -135,8 +135,12 @@
             mean_ref[...] = jnp.broadcast_to(mean, (8, CH))
         current = current + step * tanh_out
     for section in range(STEPS_DEV):
-        block = lowered[section].astype(jnp.float32)
-        turned_ref[:, section * PIX : (section + 1) * PIX] = block.T.astype(jnp.bfloat16)
+        lanes = slice(section * PIX, (section + 1) * PIX)
+        for row in range(3):
+            block = lowered[section, :, row * CH : (row + 1) * CH].astype(jnp.float32)
+            for tap, moved in enumerate((from_left(block, col), block, from_right(block, col))):
+                begin = (3 * row + tap) * CH
+                turned_ref[begin : begin + CH, lanes] = moved.T.astype(jnp.bfloat16)
     for row in range(3):
         for tap in range(3):
             begin = (8 - 3 * row - tap) * CH
@@ -276,16 +280,8 @@
 
 
 def half_rows(turned_ref, half, lanes):
-    begins = [pl.multiple_of(row * CH + half * (CH // 2), CH // 2) for row in range(3)]
+    begins = [pl.multiple_of(tap * CH + half * (CH // 2), CH // 2) for tap in range(9)]
     return jnp.concatenate([turned_ref[pl.ds(begin, CH // 2), lanes] for begin in begins], axis=0)
-
-
-def store_half(out_ref, taps):
-    height = CH // 2
-    for row in range(3):
-        for tap in range(3):
-            begin = (3 * row + tap) * height
-            out_ref[begin : begin + height, :] = taps[row * height : (row + 1) * height, tap * CH : (tap + 1) * CH]
 
 
 def second_kernel(
@@ -300,25 +296,24 @@
             values = adjoint_step(buffer, flipped_ref, lows, values, step, col)
         for k, low in enumerate(lows):
             begin = section * PIX + k * PIECE
-            grad, span = low.astype(jnp.float32), slice(begin, begin + PIECE)
-            grads_ref[span, 0:CH] = from_right(grad, col).astype(jnp.bfloat16)
-            grads_ref[span, CH : 2 * CH] = low
-            grads_ref[span, 2 * CH : WIDE] = from_left(grad, col).astype(jnp.bfloat16)
+            grads_ref[begin : begin + PIECE, :] = low
         part = slice(section * PIX, (section + 1) * PIX)
         term = jnp.dot(
-            half_rows(turned_ref, 1 - core_ref[0], part), grads_ref[part, :], preferred_element_type=jnp.float32
+            half_rows(turned_ref, 1 - core_ref[0], part),
+            jnp.concatenate(lows, axis=0),
+            preferred_element_type=jnp.float32,
         )
         if section == STEPS_DEV - 1:
             total[...] = term
         elif section > 0:
             total[...] += term
         else:
-            store_half(sent_ref, step * (total[...] + term))
+            sent_ref[...] = step * (total[...] + term)
 
 
 def kept_kernel(step, core_ref, turned_ref, grads_ref, kept_ref):
     rows = half_rows(turned_ref, core_ref[0], slice(0, STEPS_DEV * PIX))
-    store_half(kept_ref, step * jnp.dot(rows, grads_ref[...], preferred_element_type=jnp.float32))
+    kept_ref[...] = step * jnp.dot(rows, grads_ref[...], preferred_element_type=jnp.float32)
 
 
 def add_kernel(left_ref, right_ref, after_ref, out_ref):
@@ -392,7 +387,7 @@
     mark = call(first_kernel, f32(8, CH), 3.0, "ss")(core, final)
     slopes, turned, flipped, center, mean = call(
         bound(forward_kernel),
-        [f32(STEPS_DEV, PIX, CH), bf16(WIDE, STEPS_DEV * PIX), bf16(WIDE, WIDE), bf16(2 * CH, CH), f32(8, CH)],
+        [f32(STEPS_DEV, PIX, CH), bf16(TAPS, STEPS_DEV * PIX), bf16(WIDE, WIDE), bf16(2 * CH, CH), f32(8, CH)],
         1.5,
         "vvvv",
         [pltpu.VMEM((WIDE, WIDE), jnp.bfloat16), pltpu.VMEM((STEPS_DEV, PIX, WIDE), jnp.bfloat16)],
@@ -415,10 +410,10 @@
 
     sent, grads = call(
         bound(second_kernel),
-        [f32(HALF, CH), bf16(STEPS_DEV * PIX, WIDE)],
+        [f32(HALF, CH), bf16(STEPS_DEV * PIX, CH)],
         1.1,
         "svvvvv",
-        [wide, pltpu.VMEM((WIDE // 2, WIDE), jnp.float32)],
+        [wide, pltpu.VMEM((HALF, CH), jnp.float32)],
     )(core, chosen, upper_error, slopes, turned, flipped)
 
     received = lax.ppermute(sent, "core", [(0, 1), (1, 0)])

time: 90.5 us -> 91 us (level)
  no operation moved by 1% of the time
where the time goes in v11:
time: 91 us; the launch traced here: 90.7 us
  blocking collectives  63.3 us (70%)
  starting transfers between devices  17 us (19%)
  Pallas kernels  8.15 us (9%)
  local copies, waits for them, and re-layouts  0.97 us (1%)
    all_to_all x5, blocking collectives, swapped(): return lax.all_to_all(parts, axes, 0, 0).reshape(rows.shape)  63.3 us
    ppermute x1, starting transfers between devices, ring_down(): lax.ppermute(value, axis, [((i + distance) % count, i) for i in range(cou...  8.93 us
    pallas_call x10, Pallas kernels, run(): pl.pallas_call(kernel, out_shape=outs, in_specs=[places[kind] for kind in...  6.69 us
    ppermute x1, starting transfers between devices, local(): received = lax.ppermute(sent, 'core', [(0, 1), (1, 0)])  4.24 us
    ppermute x1, starting transfers between devices, local(): other = lax.ppermute(half, 'core', [(0, 1), (1, 0)])  3.79 us
  transfers between devices with their start and end apart: 3, of which 2 were waited for; matrix products, arithmetic and copies ran while one was open for 0% of the time, Pallas kernels for 4%

profile of v11, /device:TPU:1, one launch (start us, length us, event | category | flops | bytes accessed | tf_op | source)
XLA Modules:
  0.0 90.7 jit_solution(12465802806853161955)
XLA Ops:
  0.6 8.9 %collective-permute-start = (f32[256,128]{1,0:T(8,128)}, f32[256,128]{1,0:T(8,128)S(1)}, u32[]{:S(2)}, u32[]{:S(2)}) collective-permute-start(f32[256,128]{1,0:T(8,128)} %bitcast.36), channel_id=1, source_target_pairs={{8,0},{16,8},{24,16},{32,24},{40,32},{48,40},{56,48},{64,56},{72,6... | collective-permute-start | bytes 393224 | tf_op jit(solution)/shard_map/ppermute | solution.py:364
  9.6 0.0 copy-start
  9.6 0.0 copy-start.3
  9.6 0.0 copy-start.4
  9.6 1.0 %copy-done = bf16[3,3,128,128]{3,2,1,0:T(8,128)(2,1)S(1)} copy-done((bf16[3,3,128,128]{3,2,1,0:T(8,128)(2,1)S(1)}, bf16[3,3,128,128]{3,2,1,0:T(8,128)(2,1)}, u32[]{:S(2)}) %copy-start) | copy-done | bytes 294936
  10.5 0.0 copy-done.3
  10.5 0.0 copy-done.4
  10.5 0.0 copy-start.1
  10.5 0.0 copy-start.2
  10.5 1.3 %shard_map.69 = (f32[4,256,128]{2,1,0:T(8,128)S(1)}, bf16[1152,1024]{1,0:T(8,128)(2,1)S(1)}, bf16[384,384]{1,0:T(8,128)(2,1)S(1)}, bf16[256,128]{1,0:T(8,128)(2,1)S(1)}, f32[8,128]{1,0:T(8,128)S(1)}) custom-call(f32[8,128]{1,0:T(8,128)S(1)} %shard_map.68.refs_0_, bf16[256,128]{1,0:T(8,128)(2,1)S(1)} %bitcast.39, bf16[1152,128]{1,0:T(8,128)(2,1)S(1)} %bitcast.34, ...), custom_call_target="tpu_custom_call" | custom-call | flops 1500000000 | bytes 5400000 | tf_op jit(solution)/shard_map/pallas_call | solution.py:35
  11.9 0.2 collective-permute-done.refs_1_
  12.0 0.0 copy-done.1
  12.0 0.0 copy-done.2
  12.0 0.9 %shard_map.70 = (f32[288,128]{1,0:T(8,128)S(1)}, f32[256,128]{1,0:T(8,128)S(1)}, f32[256,128]{1,0:T(8,128)S(1)}) custom-call(s32[1]{0:T(128)} %bitcast.1.final_ref.refs_0_, f32[256,128]{1,0:T(8,128)S(1)} %collective-permute-done.refs_1_, f32[256,128]{1,0:T(8,128)S(1)} %bitcast.35, f32[256,128]{1,0:T(8,128)S(1)} %bitcast.37, ...), custom_call_target="tpu_custom_call" | custom-call | flops 1200000000 | bytes 4320000 | tf_op jit(solution)/shard_map/pallas_call | solution.py:35
  13.0 16.2 %all_to_all.25 = f32[32,1,1152]{2,1,0:T(1,128)S(1)} all-to-all(f32[32,1,1152]{2,1,0:T(1,128)S(1)} %bitcast.29), channel_id=1, replica_groups=mesh['y'=4,'z'=8,'x'=4,'core'=2] {'y','z'}, dimensions={0} | all-to-all | bytes 294912 | tf_op jit(solution)/shard_map/all_to_all | solution.py:369
  29.2 1.7 %shard_map.71 = f32[256,128]{1,0:T(8,128)S(1)} custom-call(f32[288,128]{1,0:T(8,128)S(1)} %bitcast.30, bf16[256,128]{1,0:T(8,128)(2,1)S(1)} %get-tuple-element.19.center_ref), custom_call_target="tpu_custom_call" | custom-call | flops 2500000000 | bytes 9000000 | tf_op jit(solution)/shard_map/pallas_call | solution.py:35
  30.8 12.8 %all_to_all.26 = f32[32,1,1024]{2,1,0:T(1,128)S(1)} all-to-all(f32[32,1,1024]{2,1,0:T(1,128)S(1)} %bitcast.33), channel_id=1, replica_groups=mesh['y'=4,'z'=8,'x'=4,'core'=2] {'y','z'}, dimensions={0} | all-to-all | bytes 262144 | tf_op jit(solution)/shard_map/all_to_all | solution.py:369
  43.6 1.4 %shard_map.73 = (f32[576,128]{1,0:T(8,128)S(1)}, bf16[1024,128]{1,0:T(8,128)(2,1)S(1)}) custom-call(s32[1]{0:T(128)} %bitcast.3.core_ref.refs_0_, f32[256,128]{1,0:T(8,128)S(1)} %get-tuple-element.22.refs_1_, f32[256,128]{1,0:T(8,128)S(1)} %bitcast.31, f32[4,256,128]{2,1,0:T(8,128)S(1)} %get-tuple-element.14.refs_4_.refs_3_, ...), custom_call_target="tpu_custom_call" | custom-call | flops 1100000000 | bytes 3960000 | tf_op jit(solution)/shard_map/pallas_call | solution.py:35
  45.0 4.2 %collective-permute-start.1 = (f32[576,128]{1,0:T(8,128)S(1)}, f32[576,128]{1,0:T(8,128)S(1)}, u32[]{:S(2)}, u32[]{:S(2)}) collective-permute-start(f32[576,128]{1,0:T(8,128)S(1)} %get-tuple-element.24), channel_id=1, source_target_pairs={{0,1},{1,0},{2,3},{3,2},{4,5},{5,4},{6,7},{7,6},{8,9},{9,8},{10,11... | collective-permute-start | bytes 884744 | tf_op jit(solution)/shard_map/ppermute | solution.py:419
  49.2 0.5 shard_map.74.left_ref
  49.7 0.8 shard_map.72
  50.5 0.0 collective-permute-done.1.right_ref
  50.6 13.3 %all_to_all.27 = f32[16,1,4608]{2,1,0:T(1,128)S(1)} all-to-all(f32[16,1,4608]{2,1,0:T(1,128)S(1)} %bitcast.23), channel_id=1, replica_groups=mesh['y'=4,'z'=8,'x'=4,'core'=2] {'y','x'}, dimensions={0} | all-to-all | bytes 589824 | tf_op jit(solution)/shard_map/all_to_all | solution.py:369
  63.9 10.6 %all_to_all.28 = f32[8,1,4608]{2,1,0:T(1,128)S(1)} all-to-all(f32[8,1,4608]{2,1,0:T(1,128)S(1)} %bitcast.26), channel_id=1, replica_groups=mesh['y'=4,'z'=8,'x'=4,'core'=2] {'z'}, dimensions={0} | all-to-all | bytes 294912 | tf_op jit(solution)/shard_map/all_to_all | solution.py:369
  74.6 10.4 %all_to_all.29 = f32[16,1,4608]{2,1,0:T(1,128)S(1)} all-to-all(f32[16,1,4608]{2,1,0:T(1,128)S(1)} %bitcast.25), channel_id=1, replica_groups=mesh['y'=4,'z'=8,'x'=4,'core'=2] {'y','x'}, dimensions={0} | all-to-all | bytes 589824 | tf_op jit(solution)/shard_map/all_to_all | solution.py:369
  84.9 3.8 %collective-permute-start.2 = (f32[576,128]{1,0:T(8,128)S(1)}, f32[576,128]{1,0:T(8,128)S(1)}, u32[]{:S(2)}, u32[]{:S(2)}) collective-permute-start(f32[576,128]{1,0:T(8,128)S(1)} %bitcast.21), channel_id=1, source_target_pairs={{0,1},{1,0},{2,3},{3,2},{4,5},{5,4},{6,7},{7,6},{8,9},{9,8},{10,11... | collective-permute-start | bytes 884744 | tf_op jit(solution)/shard_map/ppermute | solution.py:428
  88.7 0.7 shard_map.78.refs_2_
  89.5 0.5 collective-permute-done.2
  89.9 0.7 shard_map.79
  (4 shorter events, 0.1 us)
Async XLA Ops:
  0.6 11.4 %collective-permute-start = (f32[256,128]{1,0:T(8,128)}, f32[256,128]{1,0:T(8,128)S(1)}, u32[]{:S(2)}, u32[]{:S(2)}) collective-permute-start(f32[256,128]{1,0:T(8,128)} %bitcast.36), channel_id=1, source_target_pairs={{8,0},{16,8},{24,16},{32,24},{40,32},{48,40},{56,48},{64,56},{72,6... | collective-permute-start | bytes 393224 | tf_op jit(solution)/shard_map/ppermute | solution.py:364
  9.6 1.0 %copy-start = (bf16[3,3,128,128]{3,2,1,0:T(8,128)(2,1)S(1)}, bf16[3,3,128,128]{3,2,1,0:T(8,128)(2,1)}, u32[]{:S(2)}) copy-start(bf16[3,3,128,128]{3,2,1,0:T(8,128)(2,1)} %param.6) | copy-start | bytes 884740
  9.6 1.0 %copy-start.3 = (bf16[1,1,8,32,128]{4,3,2,1,0:T(8,128)(2,1)S(1)}, bf16[1,1,8,32,128]{4,3,2,1,0:T(8,128)(2,1)}, u32[]{:S(2)}) copy-start(bf16[1,1,8,32,128]{4,3,2,1,0:T(8,128)(2,1)} %param.5) | copy-start | bytes 196612
  9.6 1.0 %copy-start.4 = (f32[128]{0:T(128)S(1)}, f32[128]{0:T(128)}, u32[]{:S(2)}) copy-start(f32[128]{0:T(128)} %param.7) | copy-start | bytes 1540
  10.5 1.5 %copy-start.1 = (f32[1,8,32,128]{3,2,1,0:T(8,128)S(1)}, f32[1,8,32,128]{3,2,1,0:T(8,128)}, u32[]{:S(2)}) copy-start(f32[1,8,32,128]{3,2,1,0:T(8,128)} %param.9) | copy-start | bytes 393220
  10.5 1.5 %copy-start.2 = (f32[1,1,8,32,128]{4,3,2,1,0:T(8,128)S(1)}, f32[1,1,8,32,128]{4,3,2,1,0:T(8,128)}, u32[]{:S(2)}) copy-start(f32[1,1,8,32,128]{4,3,2,1,0:T(8,128)} %param.8) | copy-start | bytes 393220
  45.0 5.6 %collective-permute-start.1 = (f32[576,128]{1,0:T(8,128)S(1)}, f32[576,128]{1,0:T(8,128)S(1)}, u32[]{:S(2)}, u32[]{:S(2)}) collective-permute-start(f32[576,128]{1,0:T(8,128)S(1)} %get-tuple-element.24), channel_id=1, source_target_pairs={{0,1},{1,0},{2,3},{3,2},{4,5},{5,4},{6,7},{7,6},{8,9},{9,8},{10,11... | collective-permute-start | bytes 884744 | tf_op jit(solution)/shard_map/ppermute | solution.py:419
  84.9 5.0 %collective-permute-start.2 = (f32[576,128]{1,0:T(8,128)S(1)}, f32[576,128]{1,0:T(8,128)S(1)}, u32[]{:S(2)}, u32[]{:S(2)}) collective-permute-start(f32[576,128]{1,0:T(8,128)S(1)} %bitcast.21), channel_id=1, source_target_pairs={{0,1},{1,0},{2,3},{3,2},{4,5},{5,4},{6,7},{7,6},{8,9},{9,8},{10,11... | collective-permute-start | bytes 884744 | tf_op jit(solution)/shard_map/ppermute | solution.py:428

commit v12 on v9

--- a/solution.py
+++ b/solution.py
@@ -11,7 +11,8 @@
 CH = 128
 PIX = ROWS * COLS
 WIDE = 3 * CH
-PIECE = 64
+FIRST_PIECE = 64
+SECOND_PIECE = 128
 LENGTH = 4
 TAPS = 9 * CH
 SIZE_Y = 4
@@ -86,15 +87,15 @@
 
 
 def spread_piece(buffer, low, begin):
-    end = begin + PIECE
+    end = begin + low.shape[0]
     below, above = min(PIX, end + COLS), max(0, begin - COLS)
     buffer[begin + COLS : below, 0:CH] = low[0 : below - begin - COLS]
     buffer[begin:end, CH : 2 * CH] = low
-    buffer[above : end - COLS, 2 * CH : WIDE] = low[above + COLS - begin : PIECE]
-
-
-def pieces(ref, *lead):
-    return [ref[(*lead, slice(begin, begin + PIECE))] for begin in range(0, PIX, PIECE)]
+    buffer[above : end - COLS, 2 * CH : WIDE] = low[above + COLS - begin : end - begin]
+
+
+def pieces(ref, size, *lead):
+    return [ref[(*lead, slice(begin, begin + size))] for begin in range(0, PIX, size)]
 
 
 def split(value):
@@ -148,37 +149,38 @@
 
 
 def adjoint_step(buffer, flipped, lows, values, step, col):
+    size = PIX // len(lows)
     for k, low in enumerate(lows):
-        spread_piece(buffer, low, k * PIECE)
+        spread_piece(buffer, low, k * size)
     return [
-        value + step * convolve(buffer[k * PIECE : (k + 1) * PIECE, :], flipped, col)
+        value + step * convolve(buffer[k * size : (k + 1) * size, :], flipped, col)
         for k, value in enumerate(values)
     ]
 
 
 def lowered_grads(slope_ref, section, values):
-    return [(slope * value).astype(jnp.bfloat16) for slope, value in zip(pieces(slope_ref, section), values)]
+    return [(slope * value).astype(jnp.bfloat16) for slope, value in zip(pieces(slope_ref, PIX // len(values), section), values)]
 
 
 def relax_kernel(
     step, final_ref, upper_ref, terminal_ref, own_ref, slope_ref, flipped_ref, mean_ref,
     packed_ref, residue_ref, chosen_ref, buffer,
 ):
-    col = columns(PIECE)
+    col = columns(FIRST_PIECE)
     clear_edges(buffer)
     final = final_ref[0] == 1
-    values = [jnp.where(final, last, upper) for last, upper in zip(pieces(terminal_ref), pieces(upper_ref))]
+    values = [jnp.where(final, last, upper) for last, upper in zip(pieces(terminal_ref, FIRST_PIECE), pieces(upper_ref, FIRST_PIECE))]
     for k, value in enumerate(values):
-        chosen_ref[k * PIECE : (k + 1) * PIECE, :] = value
+        chosen_ref[k * FIRST_PIECE : (k + 1) * FIRST_PIECE, :] = value
     for section in range(STEPS_DEV - 1, -1, -1):
         lows = lowered_grads(slope_ref, section, values)
         values = adjoint_step(buffer, flipped_ref, lows, values, step, col)
     mean = mean_ref[0:1, :]
-    for k, (value, own) in enumerate(zip(values, pieces(own_ref))):
+    for k, (value, own) in enumerate(zip(values, pieces(own_ref, FIRST_PIECE))):
         residue = value - own
-        residue_ref[k * PIECE : (k + 1) * PIECE, :] = residue
-        for share in range(PIECE // SHARE):
-            begin = (k * (PIECE // SHARE) + share) * SLOT
+        residue_ref[k * FIRST_PIECE : (k + 1) * FIRST_PIECE, :] = residue
+        for share in range(FIRST_PIECE // SHARE):
+            begin = (k * (FIRST_PIECE // SHARE) + share) * SLOT
             packed_ref[begin : begin + SHARE, :] = residue[share * SHARE : (share + 1) * SHARE]
             packed_ref[begin + SHARE : begin + SLOT, :] = mean
 
@@ -291,16 +293,16 @@
 def second_kernel(
     step, core_ref, chosen_ref, error_ref, slope_ref, turned_ref, flipped_ref, sent_ref, grads_ref, buffer, total
 ):
-    col = columns(PIECE)
+    col = columns(SECOND_PIECE)
     clear_edges(buffer)
-    values = [chosen + error for chosen, error in zip(pieces(chosen_ref), pieces(error_ref))]
+    values = [chosen + error for chosen, error in zip(pieces(chosen_ref, SECOND_PIECE), pieces(error_ref, SECOND_PIECE))]
     for section in range(STEPS_DEV - 1, -1, -1):
         lows = lowered_grads(slope_ref, section, values)
         if section > 0:
             values = adjoint_step(buffer, flipped_ref, lows, values, step, col)
         for k, low in enumerate(lows):
-            begin = section * PIX + k * PIECE
-            grad, span = low.astype(jnp.float32), slice(begin, begin + PIECE)
+            begin = section * PIX + k * SECOND_PIECE
+            grad, span = low.astype(jnp.float32), slice(begin, begin + SECOND_PIECE)
             grads_ref[span, 0:CH] = from_right(grad, col).astype(jnp.bfloat16)
             grads_ref[span, CH : 2 * CH] = low
             grads_ref[span, 2 * CH : WIDE] = from_left(grad, col).astype(jnp.bfloat16)
@@ -425,11 +427,11 @@
     kept = call(bound(kept_kernel), f32(HALF, CH), 0.4, "svv")(core, turned, grads)
     points, points_mark = call(points_kernel, [f32(PIX, CH), f32(8, CH)], 0.8)(own, residue, upper_error, mean, center)
     half = call(add_kernel, f32(HALF, CH), 0.1, "vva")(kept, received, points_mark)
-    parts = swapped(half, ("y", "x"), PLANE)
+    parts = swapped(half, ("x", "y"), PLANE)
     copies = call(sum_kernel, f32(SIZE_Z * PART, CH), 0.1)(parts)
     parts = swapped(copies, "z", SIZE_Z)
     copies = call(sum_kernel, f32(HALF, CH), 0.1)(parts)
-    half = swapped(copies, ("y", "x"), PLANE)
+    half = swapped(copies, ("x", "y"), PLANE)
     other = lax.ppermute(half, "core", [(0, 1), (1, 0)])
     grad_w = placed(True, core, other, [placed(False, core, half)])
     return points.reshape(1, 1, ROWS, COLS, CH), grad_w.reshape(3, 3, CH, CH)

time: 90.5 us -> 90.7 us (level)
  no operation moved by 1% of the time
where the time goes in v12:
time: 90.7 us; the launch traced here: 90.4 us
  blocking collectives  63.3 us (70%)
  starting transfers between devices  17.1 us (19%)
  Pallas kernels  7.64 us (8%)
  local copies, waits for them, and re-layouts  0.97 us (1%)
    all_to_all x5, blocking collectives, swapped(): return lax.all_to_all(parts, axes, 0, 0).reshape(rows.shape)  63.3 us
    ppermute x1, starting transfers between devices, ring_down(): lax.ppermute(value, axis, [((i + distance) % count, i) for i in range(cou...  8.93 us
    pallas_call x10, Pallas kernels, run(): pl.pallas_call(kernel, out_shape=outs, in_specs=[places[kind] for kind in...  6.18 us
    ppermute x1, starting transfers between devices, local(): received = lax.ppermute(sent, 'core', [(0, 1), (1, 0)])  4.24 us
    ppermute x1, starting transfers between devices, local(): other = lax.ppermute(half, 'core', [(0, 1), (1, 0)])  3.9 us
  transfers between devices with their start and end apart: 3, of which 2 were waited for; matrix products, arithmetic and copies ran while one was open for 0% of the time, Pallas kernels for 4%

profile of v12, /device:TPU:1, one launch (start us, length us, event | category | flops | bytes accessed | tf_op | source)
XLA Modules:
  0.0 90.4 jit_solution(5819357677302363413)
XLA Ops:
  0.6 8.9 %collective-permute-start = (f32[256,128]{1,0:T(8,128)}, f32[256,128]{1,0:T(8,128)S(1)}, u32[]{:S(2)}, u32[]{:S(2)}) collective-permute-start(f32[256,128]{1,0:T(8,128)} %bitcast.36), channel_id=1, source_target_pairs={{8,0},{16,8},{24,16},{32,24},{40,32},{48,40},{56,48},{64,56},{72,6... | collective-permute-start | bytes 393224 | tf_op jit(solution)/shard_map/ppermute | solution.py:371
  9.6 0.0 copy-start
  9.6 0.0 copy-start.3
  9.6 0.0 copy-start.4
  9.6 1.0 %copy-done = bf16[3,3,128,128]{3,2,1,0:T(8,128)(2,1)S(1)} copy-done((bf16[3,3,128,128]{3,2,1,0:T(8,128)(2,1)S(1)}, bf16[3,3,128,128]{3,2,1,0:T(8,128)(2,1)}, u32[]{:S(2)}) %copy-start) | copy-done | bytes 294936
  10.5 0.0 copy-done.3
  10.5 0.0 copy-done.4
  10.5 0.0 copy-start.1
  10.5 0.0 copy-start.2
  10.5 1.3 %shard_map.69 = (f32[4,256,128]{2,1,0:T(8,128)S(1)}, bf16[384,1024]{1,0:T(8,128)(2,1)S(1)}, bf16[384,384]{1,0:T(8,128)(2,1)S(1)}, bf16[256,128]{1,0:T(8,128)(2,1)S(1)}, f32[8,128]{1,0:T(8,128)S(1)}) custom-call(f32[8,128]{1,0:T(8,128)S(1)} %shard_map.68.refs_0_, bf16[256,128]{1,0:T(8,128)(2,1)S(1)} %bitcast.39, bf16[1152,128]{1,0:T(8,128)(2,1)S(1)} %bitcast.34, ...), custom_call_target="tpu_custom_call" | custom-call | flops 1500000000 | bytes 5400000 | tf_op jit(solution)/shard_map/pallas_call | solution.py:36
  11.8 0.2 collective-permute-done.refs_1_
  12.0 0.0 copy-done.1
  12.0 0.0 copy-done.2
  12.0 0.9 %shard_map.70 = (f32[288,128]{1,0:T(8,128)S(1)}, f32[256,128]{1,0:T(8,128)S(1)}, f32[256,128]{1,0:T(8,128)S(1)}) custom-call(s32[1]{0:T(128)} %bitcast.1.final_ref.refs_0_, f32[256,128]{1,0:T(8,128)S(1)} %collective-permute-done.refs_1_, f32[256,128]{1,0:T(8,128)S(1)} %bitcast.35, f32[256,128]{1,0:T(8,128)S(1)} %bitcast.37, ...), custom_call_target="tpu_custom_call" | custom-call | flops 1200000000 | bytes 4320000 | tf_op jit(solution)/shard_map/pallas_call | solution.py:36
  13.0 16.2 %all_to_all.25 = f32[32,1,1152]{2,1,0:T(1,128)S(1)} all-to-all(f32[32,1,1152]{2,1,0:T(1,128)S(1)} %bitcast.29), channel_id=1, replica_groups=mesh['y'=4,'z'=8,'x'=4,'core'=2] {'y','z'}, dimensions={0} | all-to-all | bytes 294912 | tf_op jit(solution)/shard_map/all_to_all | solution.py:376
  29.2 1.7 %shard_map.71 = f32[256,128]{1,0:T(8,128)S(1)} custom-call(f32[288,128]{1,0:T(8,128)S(1)} %bitcast.30, bf16[256,128]{1,0:T(8,128)(2,1)S(1)} %get-tuple-element.19.center_ref), custom_call_target="tpu_custom_call" | custom-call | flops 2500000000 | bytes 9000000 | tf_op jit(solution)/shard_map/pallas_call | solution.py:36
  30.8 12.8 %all_to_all.26 = f32[32,1,1024]{2,1,0:T(1,128)S(1)} all-to-all(f32[32,1,1024]{2,1,0:T(1,128)S(1)} %bitcast.33), channel_id=1, replica_groups=mesh['y'=4,'z'=8,'x'=4,'core'=2] {'y','z'}, dimensions={0} | all-to-all | bytes 262144 | tf_op jit(solution)/shard_map/all_to_all | solution.py:376
  43.6 1.0 %shard_map.73 = (f32[576,128]{1,0:T(8,128)S(1)}, bf16[1024,384]{1,0:T(8,128)(2,1)S(1)}) custom-call(s32[1]{0:T(128)} %bitcast.3.core_ref.refs_0_, f32[256,128]{1,0:T(8,128)S(1)} %get-tuple-element.22.refs_1_, f32[256,128]{1,0:T(8,128)S(1)} %bitcast.31, f32[4,256,128]{2,1,0:T(8,128)S(1)} %get-tuple-element.14.refs_4_.refs_3_, ...), custom_call_target="tpu_custom_call" | custom-call | flops 1100000000 | bytes 3960000 | tf_op jit(solution)/shard_map/pallas_call | solution.py:36
  44.6 4.2 %collective-permute-start.1 = (f32[576,128]{1,0:T(8,128)S(1)}, f32[576,128]{1,0:T(8,128)S(1)}, u32[]{:S(2)}, u32[]{:S(2)}) collective-permute-start(f32[576,128]{1,0:T(8,128)S(1)} %get-tuple-element.24), channel_id=1, source_target_pairs={{0,1},{1,0},{2,3},{3,2},{4,5},{5,4},{6,7},{7,6},{8,9},{9,8},{10,11... | collective-permute-start | bytes 884744 | tf_op jit(solution)/shard_map/ppermute | solution.py:426
  48.9 0.4 shard_map.74.left_ref
  49.2 0.8 shard_map.72
  50.1 0.0 collective-permute-done.1.right_ref
  50.1 12.5 %all_to_all.27 = f32[16,1,4608]{2,1,0:T(1,128)S(1)} all-to-all(f32[16,1,4608]{2,1,0:T(1,128)S(1)} %bitcast.23), channel_id=1, replica_groups=mesh['y'=4,'z'=8,'x'=4,'core'=2] {'x','y'}, dimensions={0} | all-to-all | bytes 589824 | tf_op jit(solution)/shard_map/all_to_all | solution.py:376
  62.7 10.6 %all_to_all.28 = f32[8,1,4608]{2,1,0:T(1,128)S(1)} all-to-all(f32[8,1,4608]{2,1,0:T(1,128)S(1)} %bitcast.26), channel_id=1, replica_groups=mesh['y'=4,'z'=8,'x'=4,'core'=2] {'z'}, dimensions={0} | all-to-all | bytes 294912 | tf_op jit(solution)/shard_map/all_to_all | solution.py:376
  73.3 11.3 %all_to_all.29 = f32[16,1,4608]{2,1,0:T(1,128)S(1)} all-to-all(f32[16,1,4608]{2,1,0:T(1,128)S(1)} %bitcast.25), channel_id=1, replica_groups=mesh['y'=4,'z'=8,'x'=4,'core'=2] {'x','y'}, dimensions={0} | all-to-all | bytes 589824 | tf_op jit(solution)/shard_map/all_to_all | solution.py:376
  84.6 3.9 %collective-permute-start.2 = (f32[576,128]{1,0:T(8,128)S(1)}, f32[576,128]{1,0:T(8,128)S(1)}, u32[]{:S(2)}, u32[]{:S(2)}) collective-permute-start(f32[576,128]{1,0:T(8,128)S(1)} %bitcast.21), channel_id=1, source_target_pairs={{0,1},{1,0},{2,3},{3,2},{4,5},{5,4},{6,7},{7,6},{8,9},{9,8},{10,11... | collective-permute-start | bytes 884744 | tf_op jit(solution)/shard_map/ppermute | solution.py:435
  88.5 0.7 shard_map.78.refs_2_
  89.2 0.5 collective-permute-done.2
  89.7 0.7 shard_map.79
  (4 shorter events, 0.1 us)
Async XLA Ops:
  0.6 11.4 %collective-permute-start = (f32[256,128]{1,0:T(8,128)}, f32[256,128]{1,0:T(8,128)S(1)}, u32[]{:S(2)}, u32[]{:S(2)}) collective-permute-start(f32[256,128]{1,0:T(8,128)} %bitcast.36), channel_id=1, source_target_pairs={{8,0},{16,8},{24,16},{32,24},{40,32},{48,40},{56,48},{64,56},{72,6... | collective-permute-start | bytes 393224 | tf_op jit(solution)/shard_map/ppermute | solution.py:371
  9.6 1.0 %copy-start = (bf16[3,3,128,128]{3,2,1,0:T(8,128)(2,1)S(1)}, bf16[3,3,128,128]{3,2,1,0:T(8,128)(2,1)}, u32[]{:S(2)}) copy-start(bf16[3,3,128,128]{3,2,1,0:T(8,128)(2,1)} %param.6) | copy-start | bytes 884740
  9.6 1.0 %copy-start.3 = (bf16[1,1,8,32,128]{4,3,2,1,0:T(8,128)(2,1)S(1)}, bf16[1,1,8,32,128]{4,3,2,1,0:T(8,128)(2,1)}, u32[]{:S(2)}) copy-start(bf16[1,1,8,32,128]{4,3,2,1,0:T(8,128)(2,1)} %param.5) | copy-start | bytes 196612
  9.6 1.0 %copy-start.4 = (f32[128]{0:T(128)S(1)}, f32[128]{0:T(128)}, u32[]{:S(2)}) copy-start(f32[128]{0:T(128)} %param.7) | copy-start | bytes 1540
  10.5 1.5 %copy-start.1 = (f32[1,8,32,128]{3,2,1,0:T(8,128)S(1)}, f32[1,8,32,128]{3,2,1,0:T(8,128)}, u32[]{:S(2)}) copy-start(f32[1,8,32,128]{3,2,1,0:T(8,128)} %param.9) | copy-start | bytes 393220
  10.5 1.5 %copy-start.2 = (f32[1,1,8,32,128]{4,3,2,1,0:T(8,128)S(1)}, f32[1,1,8,32,128]{4,3,2,1,0:T(8,128)}, u32[]{:S(2)}) copy-start(f32[1,1,8,32,128]{4,3,2,1,0:T(8,128)} %param.8) | copy-start | bytes 393220
  44.6 5.5 %collective-permute-start.1 = (f32[576,128]{1,0:T(8,128)S(1)}, f32[576,128]{1,0:T(8,128)S(1)}, u32[]{:S(2)}, u32[]{:S(2)}) collective-permute-start(f32[576,128]{1,0:T(8,128)S(1)} %get-tuple-element.24), channel_id=1, source_target_pairs={{0,1},{1,0},{2,3},{3,2},{4,5},{5,4},{6,7},{7,6},{8,9},{9,8},{10,11... | collective-permute-start | bytes 884744 | tf_op jit(solution)/shard_map/ppermute | solution.py:426
  84.6 5.1 %collective-permute-start.2 = (f32[576,128]{1,0:T(8,128)S(1)}, f32[576,128]{1,0:T(8,128)S(1)}, u32[]{:S(2)}, u32[]{:S(2)}) collective-permute-start(f32[576,128]{1,0:T(8,128)S(1)} %bitcast.21), channel_id=1, source_target_pairs={{0,1},{1,0},{2,3},{3,2},{4,5},{5,4},{6,7},{7,6},{8,9},{9,8},{10,11... | collective-permute-start | bytes 884744 | tf_op jit(solution)/shard_map/ppermute | solution.py:435

commit v13 on v10

--- a/solution.py
+++ b/solution.py
@@ -11,7 +11,8 @@
 CH = 128
 PIX = ROWS * COLS
 WIDE = 3 * CH
-PIECE = 64
+FIRST_PIECE = 64
+SECOND_PIECE = 128
 LENGTH = 4
 TAPS = 9 * CH
 SIZE_Y = 4
@@ -86,15 +87,15 @@
 
 
 def spread_piece(buffer, low, begin):
-    end = begin + PIECE
+    end = begin + low.shape[0]
     below, above = min(PIX, end + COLS), max(0, begin - COLS)
     buffer[begin + COLS : below, 0:CH] = low[0 : below - begin - COLS]
     buffer[begin:end, CH : 2 * CH] = low
-    buffer[above : end - COLS, 2 * CH : WIDE] = low[above + COLS - begin : PIECE]
-
-
-def pieces(ref, *lead):
-    return [ref[(*lead, slice(begin, begin + PIECE))] for begin in range(0, PIX, PIECE)]
+    buffer[above : end - COLS, 2 * CH : WIDE] = low[above + COLS - begin : end - begin]
+
+
+def pieces(ref, size, *lead):
+    return [ref[(*lead, slice(begin, begin + size))] for begin in range(0, PIX, size)]
 
 
 def split(value):
@@ -148,37 +149,38 @@
 
 
 def adjoint_step(buffer, flipped, lows, values, step, col):
+    size = PIX // len(lows)
     for k, low in enumerate(lows):
-        spread_piece(buffer, low, k * PIECE)
+        spread_piece(buffer, low, k * size)
     return [
-        value + step * convolve(buffer[k * PIECE : (k + 1) * PIECE, :], flipped, col)
+        value + step * convolve(buffer[k * size : (k + 1) * size, :], flipped, col)
         for k, value in enumerate(values)
     ]
 
 
 def lowered_grads(slope_ref, section, values):
-    return [(slope * value).astype(jnp.bfloat16) for slope, value in zip(pieces(slope_ref, section), values)]
+    return [(slope * value).astype(jnp.bfloat16) for slope, value in zip(pieces(slope_ref, PIX // len(values), section), values)]
 
 
 def relax_kernel(
     step, upper_ref, terminal_ref, own_ref, slope_ref, flipped_ref, mean_ref,
     packed_ref, residue_ref, chosen_ref, buffer,
 ):
-    col = columns(PIECE)
+    col = columns(FIRST_PIECE)
     clear_edges(buffer)
     final = lax.axis_index(("y", "z")) == SLICES - 1
-    values = [jnp.where(final, last, upper) for last, upper in zip(pieces(terminal_ref), pieces(upper_ref))]
+    values = [jnp.where(final, last, upper) for last, upper in zip(pieces(terminal_ref, FIRST_PIECE), pieces(upper_ref, FIRST_PIECE))]
     for k, value in enumerate(values):
-        chosen_ref[k * PIECE : (k + 1) * PIECE, :] = value
+        chosen_ref[k * FIRST_PIECE : (k + 1) * FIRST_PIECE, :] = value
     for section in range(STEPS_DEV - 1, -1, -1):
         lows = lowered_grads(slope_ref, section, values)
         values = adjoint_step(buffer, flipped_ref, lows, values, step, col)
     mean = mean_ref[0:1, :]
-    for k, (value, own) in enumerate(zip(values, pieces(own_ref))):
+    for k, (value, own) in enumerate(zip(values, pieces(own_ref, FIRST_PIECE))):
         residue = value - own
-        residue_ref[k * PIECE : (k + 1) * PIECE, :] = residue
-        for share in range(PIECE // SHARE):
-            begin = (k * (PIECE // SHARE) + share) * SLOT
+        residue_ref[k * FIRST_PIECE : (k + 1) * FIRST_PIECE, :] = residue
+        for share in range(FIRST_PIECE // SHARE):
+            begin = (k * (FIRST_PIECE // SHARE) + share) * SLOT
             packed_ref[begin : begin + SHARE, :] = residue[share * SHARE : (share + 1) * SHARE]
             packed_ref[begin + SHARE : begin + SLOT, :] = mean
 
@@ -291,16 +293,16 @@
 def second_kernel(
     step, chosen_ref, error_ref, slope_ref, turned_ref, flipped_ref, sent_ref, grads_ref, buffer, total
 ):
-    col = columns(PIECE)
+    col = columns(SECOND_PIECE)
     clear_edges(buffer)
-    values = [chosen + error for chosen, error in zip(pieces(chosen_ref), pieces(error_ref))]
+    values = [chosen + error for chosen, error in zip(pieces(chosen_ref, SECOND_PIECE), pieces(error_ref, SECOND_PIECE))]
     for section in range(STEPS_DEV - 1, -1, -1):
         lows = lowered_grads(slope_ref, section, values)
         if section > 0:
             values = adjoint_step(buffer, flipped_ref, lows, values, step, col)
         for k, low in enumerate(lows):
-            begin = section * PIX + k * PIECE
-            grad, span = low.astype(jnp.float32), slice(begin, begin + PIECE)
+            begin = section * PIX + k * SECOND_PIECE
+            grad, span = low.astype(jnp.float32), slice(begin, begin + SECOND_PIECE)
             grads_ref[span, 0:CH] = from_right(grad, col).astype(jnp.bfloat16)
             grads_ref[span, CH : 2 * CH] = low
             grads_ref[span, 2 * CH : WIDE] = from_left(grad, col).astype(jnp.bfloat16)
@@ -421,11 +423,11 @@
     kept = call(bound(kept_kernel), f32(HALF, CH), 0.4)(turned, grads)
     points, points_mark = call(points_kernel, [f32(PIX, CH), f32(8, CH)], 0.8)(own, residue, upper_error, mean, center)
     half = call(add_kernel, f32(HALF, CH), 0.1, "vva")(kept, received, points_mark)
-    parts = swapped(half, ("y", "x"), PLANE)
+    parts = swapped(half, ("x", "y"), PLANE)
     copies = call(sum_kernel, f32(SIZE_Z * PART, CH), 0.1)(parts)
     parts = swapped(copies, "z", SIZE_Z)
     copies = call(sum_kernel, f32(HALF, CH), 0.1)(parts)
-    half = swapped(copies, ("y", "x"), PLANE)
+    half = swapped(copies, ("x", "y"), PLANE)
     other = lax.ppermute(half, "core", [(0, 1), (1, 0)])
     grad_w = placed(True, other, [placed(False, half)])
     return points.reshape(1, 1, ROWS, COLS, CH), grad_w.reshape(3, 3, CH, CH)

time: 90.5 us -> 90.7 us (level)
  no operation moved by 1% of the time
where the time goes in v13:
time: 90.7 us; the launch traced here: 90.4 us
  blocking collectives  63.3 us (70%)
  starting transfers between devices  17.1 us (19%)
  Pallas kernels  7.6 us (8%)
  waiting for transfers between devices  1.02 us (1%)
    all_to_all x5, blocking collectives, swapped(): return lax.all_to_all(parts, axes, 0, 0).reshape(rows.shape)  63.3 us
    ppermute x1, starting transfers between devices, ring_down(): lax.ppermute(value, axis, [((i + distance) % count, i) for i in range(cou...  8.93 us
    pallas_call x10, Pallas kernels, run(): pl.pallas_call(kernel, out_shape=outs, in_specs=[places[kind] for kind in...  6.14 us
    ppermute x1, starting transfers between devices, local(): received = lax.ppermute(sent, 'core', [(0, 1), (1, 0)])  4.24 us
    ppermute x1, starting transfers between devices, local(): other = lax.ppermute(half, 'core', [(0, 1), (1, 0)])  3.9 us
  transfers between devices with their start and end apart: 3, of which 2 were waited for; matrix products, arithmetic and copies ran while one was open for 0% of the time, Pallas kernels for 4%

profile of v13, /device:TPU:1, one launch (start us, length us, event | category | flops | bytes accessed | tf_op | source)
XLA Modules:
  0.0 90.4 jit_solution(8607697249146078678)
XLA Ops:
  0.6 0.0 copy-start
  0.6 0.0 copy-start.3
  0.6 8.9 %collective-permute-start = (f32[256,128]{1,0:T(8,128)}, f32[256,128]{1,0:T(8,128)S(1)}, u32[]{:S(2)}, u32[]{:S(2)}) collective-permute-start(f32[256,128]{1,0:T(8,128)} %bitcast.34), channel_id=1, source_target_pairs={{8,0},{16,8},{24,16},{32,24},{40,32},{48,40},{56,48},{64,56},{72,6... | collective-permute-start | bytes 393224 | tf_op jit(solution)/shard_map/ppermute | solution.py:371
  9.6 0.0 copy-start.4
  9.6 0.0 copy-done
  9.6 0.0 copy-done.3
  9.6 0.6 copy-done.4
  10.2 0.0 copy-start.1
  10.2 0.0 copy-start.2
  10.2 1.3 %shard_map.69 = (f32[4,256,128]{2,1,0:T(8,128)S(1)}, bf16[384,1024]{1,0:T(8,128)(2,1)S(1)}, bf16[384,384]{1,0:T(8,128)(2,1)S(1)}, bf16[256,128]{1,0:T(8,128)(2,1)S(1)}, f32[8,128]{1,0:T(8,128)S(1)}) custom-call(f32[8,128]{1,0:T(8,128)S(1)} %shard_map.68.refs_0_, bf16[256,128]{1,0:T(8,128)(2,1)S(1)} %bitcast.37, bf16[1152,128]{1,0:T(8,128)(2,1)S(1)} %bitcast.32, ...), custom_call_target="tpu_custom_call" | custom-call | flops 1500000000 | bytes 5400000 | tf_op jit(solution)/shard_map/pallas_call | solution.py:36
  11.5 0.5 collective-permute-done.refs_0_
  12.1 0.0 copy-done.1
  12.1 0.0 copy-done.2
  12.1 0.9 %shard_map.70 = (f32[288,128]{1,0:T(8,128)S(1)}, f32[256,128]{1,0:T(8,128)S(1)}, f32[256,128]{1,0:T(8,128)S(1)}) custom-call(f32[256,128]{1,0:T(8,128)S(1)} %collective-permute-done.refs_0_, f32[256,128]{1,0:T(8,128)S(1)} %bitcast.33, f32[256,128]{1,0:T(8,128)S(1)} %bitcast.35, f32[4,256,128]{2,1,0:T(8,128)S(1)} %get-tuple-element.14.refs_3_.refs_2_, ...), custom_call_target="tpu_custom_call" | custom-call | flops 1200000000 | bytes 4320000 | tf_op jit(solution)/shard_map/pallas_call | solution.py:36
  13.0 16.2 %all_to_all.25 = f32[32,1,1152]{2,1,0:T(1,128)S(1)} all-to-all(f32[32,1,1152]{2,1,0:T(1,128)S(1)} %bitcast.27), channel_id=1, replica_groups=mesh['y'=4,'z'=8,'x'=4,'core'=2] {'y','z'}, dimensions={0} | all-to-all | bytes 294912 | tf_op jit(solution)/shard_map/all_to_all | solution.py:376
  29.2 1.7 %shard_map.71 = f32[256,128]{1,0:T(8,128)S(1)} custom-call(f32[288,128]{1,0:T(8,128)S(1)} %bitcast.28, bf16[256,128]{1,0:T(8,128)(2,1)S(1)} %get-tuple-element.19.center_ref), custom_call_target="tpu_custom_call" | custom-call | flops 2500000000 | bytes 9000000 | tf_op jit(solution)/shard_map/pallas_call | solution.py:36
  30.9 12.8 %all_to_all.26 = f32[32,1,1024]{2,1,0:T(1,128)S(1)} all-to-all(f32[32,1,1024]{2,1,0:T(1,128)S(1)} %bitcast.31), channel_id=1, replica_groups=mesh['y'=4,'z'=8,'x'=4,'core'=2] {'y','z'}, dimensions={0} | all-to-all | bytes 262144 | tf_op jit(solution)/shard_map/all_to_all | solution.py:376
  43.6 1.0 %shard_map.73 = (f32[576,128]{1,0:T(8,128)S(1)}, bf16[1024,384]{1,0:T(8,128)(2,1)S(1)}) custom-call(f32[256,128]{1,0:T(8,128)S(1)} %get-tuple-element.22.refs_0_, f32[256,128]{1,0:T(8,128)S(1)} %bitcast.29, f32[4,256,128]{2,1,0:T(8,128)S(1)} %get-tuple-element.14.refs_3_.refs_2_, bf16[384,1024]{1,0:T(8,128)(2,1)S(1)} %get-tuple-element.21.refs_3_.refs_0_, ...), custom_call_target="tpu_custom_call" | custom-call | flops 1100000000 | bytes 3960000 | tf_op jit(solution)/shard_map/pallas_call | solution.py:36
  44.6 4.2 %collective-permute-start.1 = (f32[576,128]{1,0:T(8,128)S(1)}, f32[576,128]{1,0:T(8,128)S(1)}, u32[]{:S(2)}, u32[]{:S(2)}) collective-permute-start(f32[576,128]{1,0:T(8,128)S(1)} %get-tuple-element.24), channel_id=1, source_target_pairs={{0,1},{1,0},{2,3},{3,2},{4,5},{5,4},{6,7},{7,6},{8,9},{9,8},{10,11... | collective-permute-start | bytes 884744 | tf_op jit(solution)/shard_map/ppermute | solution.py:422
  48.9 0.4 shard_map.74.left_ref
  49.2 0.8 shard_map.72
  50.1 0.0 collective-permute-done.1.right_ref
  50.1 12.5 %all_to_all.27 = f32[16,1,4608]{2,1,0:T(1,128)S(1)} all-to-all(f32[16,1,4608]{2,1,0:T(1,128)S(1)} %bitcast.21), channel_id=1, replica_groups=mesh['y'=4,'z'=8,'x'=4,'core'=2] {'x','y'}, dimensions={0} | all-to-all | bytes 589824 | tf_op jit(solution)/shard_map/all_to_all | solution.py:376
  62.6 10.6 %all_to_all.28 = f32[8,1,4608]{2,1,0:T(1,128)S(1)} all-to-all(f32[8,1,4608]{2,1,0:T(1,128)S(1)} %bitcast.24), channel_id=1, replica_groups=mesh['y'=4,'z'=8,'x'=4,'core'=2] {'z'}, dimensions={0} | all-to-all | bytes 294912 | tf_op jit(solution)/shard_map/all_to_all | solution.py:376
  73.3 11.3 %all_to_all.29 = f32[16,1,4608]{2,1,0:T(1,128)S(1)} all-to-all(f32[16,1,4608]{2,1,0:T(1,128)S(1)} %bitcast.23), channel_id=1, replica_groups=mesh['y'=4,'z'=8,'x'=4,'core'=2] {'x','y'}, dimensions={0} | all-to-all | bytes 589824 | tf_op jit(solution)/shard_map/all_to_all | solution.py:376
  84.6 3.9 %collective-permute-start.2 = (f32[576,128]{1,0:T(8,128)S(1)}, f32[576,128]{1,0:T(8,128)S(1)}, u32[]{:S(2)}, u32[]{:S(2)}) collective-permute-start(f32[576,128]{1,0:T(8,128)S(1)} %bitcast.19), channel_id=1, source_target_pairs={{0,1},{1,0},{2,3},{3,2},{4,5},{5,4},{6,7},{7,6},{8,9},{9,8},{10,11... | collective-permute-start | bytes 884744 | tf_op jit(solution)/shard_map/ppermute | solution.py:431
  88.5 0.7 shard_map.78.refs_1_
  89.2 0.5 collective-permute-done.2
  89.7 0.7 shard_map.79
  (4 shorter events, 0.1 us)
Async XLA Ops:
  0.6 9.0 %copy-start = (bf16[3,3,128,128]{3,2,1,0:T(8,128)(2,1)S(1)}, bf16[3,3,128,128]{3,2,1,0:T(8,128)(2,1)}, u32[]{:S(2)}) copy-start(bf16[3,3,128,128]{3,2,1,0:T(8,128)(2,1)} %param.6) | copy-start | bytes 884740
  0.6 9.0 %copy-start.3 = (bf16[1,1,8,32,128]{4,3,2,1,0:T(8,128)(2,1)S(1)}, bf16[1,1,8,32,128]{4,3,2,1,0:T(8,128)(2,1)}, u32[]{:S(2)}) copy-start(bf16[1,1,8,32,128]{4,3,2,1,0:T(8,128)(2,1)} %param.5) | copy-start | bytes 196612
  0.6 11.4 %collective-permute-start = (f32[256,128]{1,0:T(8,128)}, f32[256,128]{1,0:T(8,128)S(1)}, u32[]{:S(2)}, u32[]{:S(2)}) collective-permute-start(f32[256,128]{1,0:T(8,128)} %bitcast.34), channel_id=1, source_target_pairs={{8,0},{16,8},{24,16},{32,24},{40,32},{48,40},{56,48},{64,56},{72,6... | collective-permute-start | bytes 393224 | tf_op jit(solution)/shard_map/ppermute | solution.py:371
  9.6 0.7 copy-start.4
  10.2 1.8 %copy-start.1 = (f32[1,8,32,128]{3,2,1,0:T(8,128)S(1)}, f32[1,8,32,128]{3,2,1,0:T(8,128)}, u32[]{:S(2)}) copy-start(f32[1,8,32,128]{3,2,1,0:T(8,128)} %param.9) | copy-start | bytes 393220
  10.2 1.8 %copy-start.2 = (f32[1,1,8,32,128]{4,3,2,1,0:T(8,128)S(1)}, f32[1,1,8,32,128]{4,3,2,1,0:T(8,128)}, u32[]{:S(2)}) copy-start(f32[1,1,8,32,128]{4,3,2,1,0:T(8,128)} %param.8) | copy-start | bytes 393220
  44.6 5.5 %collective-permute-start.1 = (f32[576,128]{1,0:T(8,128)S(1)}, f32[576,128]{1,0:T(8,128)S(1)}, u32[]{:S(2)}, u32[]{:S(2)}) collective-permute-start(f32[576,128]{1,0:T(8,128)S(1)} %get-tuple-element.24), channel_id=1, source_target_pairs={{0,1},{1,0},{2,3},{3,2},{4,5},{5,4},{6,7},{7,6},{8,9},{9,8},{10,11... | collective-permute-start | bytes 884744 | tf_op jit(solution)/shard_map/ppermute | solution.py:422
  84.6 5.1 %collective-permute-start.2 = (f32[576,128]{1,0:T(8,128)S(1)}, f32[576,128]{1,0:T(8,128)S(1)}, u32[]{:S(2)}, u32[]{:S(2)}) collective-permute-start(f32[576,128]{1,0:T(8,128)S(1)} %bitcast.19), channel_id=1, source_target_pairs={{0,1},{1,0},{2,3},{3,2},{4,5},{5,4},{6,7},{7,6},{8,9},{9,8},{10,11... | collective-permute-start | bytes 884744 | tf_op jit(solution)/shard_map/ppermute | solution.py:431
